TPU v7x, 32 devices: a whole 2x2x4 slice. The times are simulated.
32 devices in a mesh: docs: 16 (over z, y, x), blk: 2 (over core).
Axes of the slice: x: 2, y: 2, z: 4, core: 2. Of those that a mesh axis runs over, the one named last changes fastest.
Arguments:
- text_tokens: bfloat16 [16, 736, 768], P('docs', 'blk'), may hold values from -6 to 6
- visual_tokens: bfloat16 [16, 96, 768], P('docs', 'blk'), may hold values from -6 to 6
- text_mask: int32 [16, 736], P('docs'), may hold values from 0 to 1, as said below
- visual_mask: int32 [16, 96], P('docs'), may hold values from 0 to 1, as said below
- w_qkv: bfloat16 [2, 768, 2304], P(None, 'docs'), may hold values from -0.3125 to 0.3125
- w_out: bfloat16 [2, 768, 768], P(None, 'docs'), may hold values from -1.5 to 1.5
- w_gate: bfloat16 [2, 768, 12], P(None, 'docs'), may hold values from -0.21875 to 0.21875
- w_up: bfloat16 [2, 768, 3072], P(None, 'docs'), may hold values from -0.21875 to 0.21875
- w_down: bfloat16 [2, 3072, 768], P(None, 'docs'), may hold values from -0.109375 to 0.109375
- gain_attn: bfloat16 [2, 768], P(None, 'docs'), may hold values from 0.5 to 1.5
- gain_ffn: bfloat16 [2, 768], P(None, 'docs'), may hold values from 0.5 to 1.5
- text_cotangent: bfloat16 [16, 736, 768], P('docs', 'blk'), may hold values from -6 to 6
- visual_cotangent: bfloat16 [16, 96, 768], P('docs', 'blk'), may hold values from -6 to 6
Outputs:
- text_out: bfloat16 [16, 736, 768], P('docs', 'blk')
- visual_out: bfloat16 [16, 96, 768], P('docs', 'blk')
- text_grad: float32 [16, 736, 768], P('docs', 'blk')
- visual_grad: float32 [16, 96, 768], P('docs', 'blk')
- grad_qkv: float32 [2, 768, 2304], P(None, 'docs')
- grad_out: float32 [2, 768, 768], P(None, 'docs')
- grad_gate: float32 [2, 768, 12], P(None, 'docs')
- grad_up: float32 [2, 768, 3072], P(None, 'docs')
- grad_down: float32 [2, 3072, 768], P(None, 'docs')
- grad_gain_attn: float32 [2, 768], P(None, 'docs')
- grad_gain_ffn: float32 [2, 768], P(None, 'docs')
Inputs may be any that keep to these rules, and one draw needn't show every extreme that they name: `text_mask`: in each document the slots with mask 1 are a prefix holding at least one eighth of the 736 text slots (and at least one); some document has all 736 text slots valid. `visual_mask`: in each document the slots with mask 1 are a prefix of at least one visual slot; some document has all 96 visual slots valid.
All inputs are finite; a program needn't handle non-finite values.
Results may differ from a plain program's by a relative error of at most 0.017.
Values may be sent and summed in bfloat16 or wider, within the bound.
A program may use at most 256 MiB of HBM per device.

v0:
```python
import functools
import types
from typing import NamedTuple

import jax
import jax.numpy as jnp
from jax import lax
from jax.experimental import pallas as pl
from jax.experimental.pallas import tpu as pltpu
from jax.sharding import PartitionSpec as P

epsilon = 1e-05
big_negative = -1e30
MESH = pl.DeviceIdType.MESH
docs_axis, core_axis = "docs", "blk"
lane = 128
row_tile = 16
vmem_limit = 61 * 1024 * 1024
low, full = jnp.bfloat16, jnp.float32
by_x, by_y, upward, downward, crosswise = range(5)
lines_first, planes_first, line_only, plane_shared = range(4)
quads = ((False, False), (False, True), (True, False), (True, True))


def dot(left, right):
    return jnp.dot(left, right, preferred_element_type=full)


def dot_back(left, right):
    return lax.dot_general(left, right, (((1,), (1,)), ((), ())), preferred_element_type=full)


def dot_rows(left, right):
    return lax.dot_general(left, right, (((0,), (0,)), ((), ())), preferred_element_type=full)


def normalize(values):
    centred = values - jnp.mean(values, -1, keepdims=True)
    inverse = lax.rsqrt(jnp.mean(centred * centred, -1, keepdims=True) + epsilon)
    return centred * inverse, inverse


def over_rows(first, last, size, body):
    def step(at, carry):
        body(pl.ds(pl.multiple_of(first + at * size, row_tile), size))
        return carry

    lax.fori_loop(0, (last - first) // size, step, 0)


def over_columns(first, last, size, body):
    def step(at, carry):
        body(pl.ds(pl.multiple_of(first + at * size, lane), size))
        return carry

    lax.fori_loop(0, (last - first) // size, step, 0)


def gelu_both(value):
    root = 0.7978845608028654
    square = value * value
    bent = jnp.tanh(root * (value + 0.044715 * value * square))
    cdf = 0.5 * (1.0 + bent)
    slope = cdf + 0.5 * value * (1.0 - bent * bent) * (root * (1.0 + 0.134145 * square))
    return value * cdf, slope


def add_rows(target, others, first=0):
    size = max(size for size in (16, 32, 48) if others[0].shape[0] % size == 0)

    def body(step, carry):
        at = pl.multiple_of(step * size, row_tile)
        total = others[0][pl.ds(at, size), :].astype(full)
        for other in others[1:]:
            total = total + other[pl.ds(at, size), :].astype(full)
        target[pl.ds(first + at, size), :] = total.astype(target.dtype)
        return carry

    lax.fori_loop(0, others[0].shape[0] // size, body, 0)


def when(conditions, body):
    conditions = [condition for condition in conditions if condition is not None]
    if not conditions:
        body()
        return
    pl.when(functools.reduce(jnp.logical_and, conditions))(body)


def merged(*groups):
    space = types.SimpleNamespace()
    for group in groups:
        vars(space).update(group._asdict())
    return space


class Place:
    def __init__(self, line_size):
        docs = lax.axis_index(docs_axis)
        self.core = lax.axis_index(core_axis)
        self.line_size = line_size
        self.z, self.y, self.x = docs // 4, (docs // 2) % 2, docs % 2
        self.up_valid = self.z < line_size - 1
        self.down_valid = self.z > 0

    def index(self, z, flip_y=False, flip_x=False):
        y = 1 - self.y if flip_y else self.y
        x = 1 - self.x if flip_x else self.x
        return z * 4 + y * 2 + x

    def device(self, step):
        z, y, x = self.z, self.y, self.x
        docs = (
            z * 4 + y * 2 + 1 - x,
            z * 4 + (1 - y) * 2 + x,
            (z + 1) * 4 + y * 2 + x,
            (z - 1) * 4 + y * 2 + x,
            z * 4 + (1 - y) * 2 + 1 - x,
        )[step]
        return (docs, self.core)

    def greet(self):
        barrier = pltpu.get_barrier_semaphore()

        def signal(device):
            pl.semaphore_signal(barrier, inc=1, device_id=device, device_id_type=MESH)

        for step in (by_x, by_y, crosswise):
            signal(self.device(step))
        pl.when(self.up_valid)(lambda: signal(self.device(upward)))
        pl.when(self.down_valid)(lambda: signal(self.device(downward)))
        signal((self.index(self.z), 1 - self.core))

    def meet(self):
        peers = 4
        for valid in (self.up_valid, self.down_valid):
            peers = peers + jnp.where(valid, 1, 0)
        pl.semaphore_wait(pltpu.get_barrier_semaphore(), peers)


class Piece(NamedTuple):
    array: int
    part: int
    first: int
    rows: int
    flip: int
    route: int


class Gather:
    def __init__(self, place, pieces, sizes, splits, owns, outs, send_sems, recv_sems, local_sems):
        self.place, self.pieces, self.sizes, self.splits = place, pieces, sizes, splits
        self.owns, self.outs = owns, outs
        self.send_sems, self.recv_sems, self.local_sems = send_sems, recv_sems, local_sems
        self.sends = []

    def has(self, at, source_z):
        half = self.place.line_size // 2
        return source_z // half == self.place.core if self.splits[self.pieces[at].array] else None

    def block(self, at, source):
        piece = self.pieces[at]
        if self.splits[piece.array]:
            source = source - self.place.core * (self.place.line_size // 2) * 4
        if piece.route == line_only:
            source = source // 4
        first = source * self.sizes[piece.array] + piece.first
        rows = pl.ds(pl.multiple_of(first, row_tile), piece.rows)
        return self.outs[piece.array].at[piece.part, rows, :]

    def mine(self, at, step=None):
        piece = self.pieces[at]
        ref, offset = self.owns[piece.array]
        if piece.route == plane_shared:
            to = self.place.index(0, step in (by_y, crosswise), step in (by_x, crosswise))
            return ref.at[to, pl.ds(piece.first, piece.rows), :]
        first = pl.multiple_of(offset + piece.first, row_tile)
        return ref.at[piece.part, pl.ds(first, piece.rows), :]

    def copy(self, at, source, step, own=False):
        return pltpu.make_async_remote_copy(
            src_ref=self.mine(at, step) if own else self.block(at, source),
            dst_ref=self.block(at, source),
            send_sem=self.send_sems.at[at, source, step],
            recv_sem=self.recv_sems.at[at, source],
            device_id=self.place.device(step),
            device_id_type=MESH,
        )

    def local(self, at):
        here = self.place.index(self.place.z)
        return pltpu.make_async_copy(self.mine(at), self.block(at, here), self.local_sems.at[at])

    def send(self, conditions, *which):
        when(conditions, lambda: self.copy(*which).start())
        self.sends.append((conditions, which))

    def wait(self, conditions, at, source):
        when(conditions, lambda: self.copy(at, source, by_x).wait_recv())

    def units(self, distance):
        place = self.place
        if distance == 0:
            return [(place.z, None, None)]
        return [
            (place.z - distance, place.z >= distance, (upward, place.up_valid)),
            (place.z + distance, place.z < place.line_size - distance, (downward, place.down_valid)),
        ]

    def both_ways(self, conditions, at, source, own=False):
        self.send(conditions + [self.place.up_valid], at, source, upward, own)
        self.send(conditions + [self.place.down_valid], at, source, downward, own)

    def own(self, at):
        place = self.place
        here = place.index(place.z)
        held = [self.has(at, place.z)]
        when(held, lambda: self.local(at).start())
        self.both_ways(held, at, here, True)
        route = self.pieces[at].route
        if route != line_only:
            self.send(held, at, here, by_x, True)
            self.send(held, at, here, by_y, True)
        if route == plane_shared:
            self.send(held, at, here, crosswise, True)

    def beside(self, at, distance):
        piece = self.pieces[at]
        for source_z, valid, _ in self.units(distance):
            conditions = [valid, self.has(at, source_z)]
            for other in (0, 1):
                source = self.place.index(source_z, other == 1, other == 0)
                if other == piece.flip or piece.route != lines_first:
                    self.wait(conditions, at, source)
                if other == piece.flip and piece.route != plane_shared:
                    self.send(conditions, at, source, by_x if other else by_y)
                if piece.route != lines_first:
                    self.both_ways(conditions, at, source)

    def along(self, at, distance, quad=quads[0]):
        for source_z, valid, (step, onward) in self.units(distance):
            source = self.place.index(source_z, *quad)
            conditions = [valid, self.has(at, source_z)]
            self.wait(conditions, at, source)
            self.send(conditions + [onward], at, source, step)
            if self.pieces[at].route == lines_first:
                self.send(conditions, at, source, by_x)
                self.send(conditions, at, source, by_y)

    def late_round(self, at, number):
        place = self.place
        last = place.line_size - 1
        if number == 1:
            self.beside(at, 0)
        if number == 2:
            held = [self.has(at, place.z)]
            fourth = place.index(place.z, *quads[3])
            self.wait(held, at, fourth)
            self.both_ways(held, at, fourth)
        for quad, behind in zip(quads, (0, 1, 1, 2)):
            if 1 <= number - behind <= last:
                self.along(at, number - behind, quad)

    def rest(self, array):
        for at, piece in enumerate(self.pieces):
            if piece.array != array:
                continue
            if piece.route in (planes_first, plane_shared):
                self.along(at, self.place.line_size - 1, quads[3])
            elif piece.route == lines_first:
                for distance in range(self.place.line_size):
                    for source_z, valid, _ in self.units(distance):
                        conditions = [valid, self.has(at, source_z)]
                        beside = (piece.flip == 0, piece.flip == 1)
                        self.wait(conditions, at, self.place.index(source_z, *beside))
                        self.wait(conditions, at, self.place.index(source_z, *quads[3]))
            when([self.has(at, self.place.z)], lambda: self.local(at).wait())

    def run(self, plan, stages):
        for kind, at, number in plan:
            if kind == 0:
                self.own(at)
            elif kind == 1:
                self.beside(at, number)
            elif kind == 2:
                self.along(at, number)
            elif kind == 3:
                self.late_round(at, number)
            elif kind == 4:
                self.rest(at)
            else:
                stages[at]()

    def finish(self):
        for conditions, which in self.sends:
            when(conditions, lambda: self.copy(*which).wait_send())


class Scatter:
    def __init__(self, place, pieces, splits, raws, parts, buffers, send_sems, recv_sems, finish):
        self.place, self.pieces, self.splits = place, pieces, splits
        self.raws, self.parts, self.buffers = raws, parts, buffers
        self.send_sems, self.recv_sems, self.finish_rows = send_sems, recv_sems, finish
        self.sends = []

    shares = ((quads[1], 1, by_x), (quads[2], 2, by_y), (quads[3], 0, crosswise))

    def has(self, at, z_to):
        half = self.place.line_size // 2
        return z_to // half == self.place.core if self.splits[self.pieces[at].array] else None

    def slot(self, at, z_to):
        half = self.place.line_size // 2
        return z_to - self.place.core * half if self.splits[self.pieces[at].array] else z_to

    def block(self, refs, at, z_to, quad):
        piece = self.pieces[at]
        ref = refs[piece.array]
        if piece.route == line_only:
            first = z_to * (ref.shape[1] // self.place.line_size) + piece.first
        else:
            split = 2 if self.splits[piece.array] else 1
            rows = ref.shape[1] // (4 * self.place.line_size // split)
            first = self.place.index(self.slot(at, z_to), *quad) * rows + piece.first
        return ref.at[piece.part, pl.ds(pl.multiple_of(first, row_tile), piece.rows), :]

    def quads(self, at):
        return quads[:1] if self.pieces[at].route == line_only else quads

    def raw_of(self, at, z_to, quad):
        return self.block(self.raws, at, z_to, quad)

    def part_of(self, at, z_to, quad):
        return self.block(self.parts, at, z_to, quad)

    def landed(self, at, kind, z_to, quad=0):
        ref = self.buffers[at][kind]
        if self.pieces[at].route == lines_first:
            return ref.at[self.slot(at, z_to)]
        return ref.at[self.slot(at, z_to), quad] if kind >= 3 else ref.at[0]

    def copy(self, source, at, kind, z_to, step, number, quad=0):
        arrival = kind if kind < 3 else 3 + (kind - 3) * 4 + quad
        return pltpu.make_async_remote_copy(
            src_ref=source,
            dst_ref=self.landed(at, kind, z_to, quad),
            send_sem=self.send_sems.at[at, z_to, number],
            recv_sem=self.recv_sems.at[at, z_to, arrival],
            device_id=self.place.device(step),
            device_id_type=MESH,
        )

    def arrived(self, at, kind, z_to, quad=0):
        held = self.landed(at, kind, z_to, quad)
        self.copy(held, at, kind, z_to, by_x, 0, quad).wait_recv()

    def send(self, conditions, *which):
        when(conditions, lambda: self.copy(*which).start())
        self.sends.append((conditions, which))

    def destination(self, step):
        size = self.place.line_size
        chosen = 0
        for at in range(size):
            order = sorted(range(size), key=lambda other: (-abs(other - at), other))
            chosen = chosen + jnp.where(self.place.z == at, order[step], 0)
        return chosen

    def raw(self, at, step):
        place = self.place
        z_to = self.destination(step)
        conditions = [self.has(at, z_to)]
        if self.pieces[at].route == lines_first:
            self.plane_raw(conditions, self.raw_of, at, z_to)
            return
        first, last = place.z == 0, place.z == place.line_size - 1
        for number, quad in enumerate(self.quads(at)):
            source = self.raw_of(at, z_to, quad)
            up = conditions + [first, z_to > place.z]
            self.send(up, source, at, 3, z_to, upward, number, number)
            down = conditions + [last, z_to < place.z]
            self.send(down, source, at, 4, z_to, downward, 4 + number, number)

    def plane_raw(self, conditions, source, at, z_to):
        if self.pieces[at].flip == 0:
            self.send(conditions, source(at, z_to, (True, True)), at, 0, z_to, by_y, 8)
            self.send(conditions, source(at, z_to, (True, False)), at, 2, z_to, by_y, 9)
        else:
            self.send(conditions, source(at, z_to, (True, True)), at, 0, z_to, by_x, 8)
            self.send(conditions, source(at, z_to, (False, True)), at, 1, z_to, by_x, 9)

    def plane_pair(self, conditions, at, z_to):
        flip = self.pieces[at].flip
        held = self.landed(at, 0, z_to)

        def body():
            self.arrived(at, 0, z_to)
            add_rows(held, [held, self.part_of(at, z_to, (flip == 1, flip == 0))])

        when(conditions, body)
        if flip == 0:
            self.send(conditions, held, at, 1, z_to, by_x, 10)
        else:
            self.send(conditions, held, at, 2, z_to, by_y, 10)

    def pair(self, at, step):
        z_to = self.destination(step)
        self.plane_pair([self.has(at, z_to)], at, z_to)

    def line(self, at, step):
        place, piece = self.place, self.pieces[at]
        z = place.z
        z_to = self.destination(step)
        conditions = [self.has(at, z_to)]
        first, last = z == 0, z == place.line_size - 1
        inner = jnp.logical_and(z > 0, z < place.line_size - 1)
        ways = (
            (3, [z_to > z], [first], [z > 0], upward, 0),
            (4, [z_to < z], [last], [z < place.line_size - 1], downward, 4),
        )
        ends = (([first], (4,)), ([last], (3,)), ([inner], (3, 4)))
        if piece.route == lines_first:
            held = self.landed(at, 1, z_to)
            base = [held, self.landed(at, 2, z_to), self.part_of(at, z_to, quads[0])]

            def wait():
                self.arrived(at, 1, z_to)
                self.arrived(at, 2, z_to)

            when(conditions, wait)
            for kind, onward, starts, passes, step_to, number in ways:
                when(conditions + onward + starts, lambda: add_rows(held, base))

                def passing():
                    self.arrived(at, kind, z_to)
                    add_rows(held, base + [self.landed(at, kind, z_to)])

                when(conditions + onward + passes, passing)
                self.send(conditions + onward, held, at, kind, z_to, step_to, number)
            for which, kinds in ends:

                def end():
                    for kind in kinds:
                        self.arrived(at, kind, z_to)
                    self.finish_rows(piece, base + [self.landed(at, kind, z_to) for kind in kinds])

                when(conditions + [z_to == z] + which, end)
            return
        for kind, onward, _, passes, step_to, number in ways:
            for at_quad, quad in enumerate(self.quads(at)):
                held = self.landed(at, kind, z_to, at_quad)

                def passing():
                    self.arrived(at, kind, z_to, at_quad)
                    add_rows(held, [held, self.part_of(at, z_to, quad)])

                which = conditions + onward + passes
                when(which, passing)
                self.send(which, held, at, kind, z_to, step_to, number + at_quad, at_quad)
        here = conditions + [z_to == z]
        for which, kinds in ends:

            def end():
                for at_quad, quad in reversed(list(enumerate(self.quads(at)))):
                    own = self.part_of(at, z_to, quad)
                    for kind in kinds:
                        self.arrived(at, kind, z_to, at_quad)
                    total = [own] + [self.landed(at, kind, z_to, at_quad) for kind in kinds]
                    if piece.route == planes_first or at_quad:
                        add_rows(own, total)
                    else:
                        self.finish_rows(piece, total)

            when(here + which, end)
        if step == place.line_size - 1 and piece.route == planes_first:
            self.plane_raw(here, self.part_of, at, z_to)
        if step == place.line_size - 1 and piece.route == plane_shared:
            for number, (quad, kind, step_to) in enumerate(self.shares):
                self.send(here, self.part_of(at, z_to, quad), at, kind, z_to, step_to, 8 + number)

    def tail(self, at):
        z, piece = self.place.z, self.pieces[at]
        if piece.route == plane_shared:
            for quad, kind, _ in self.shares:
                self.arrived(at, kind, z)
                self.finish_rows(piece, [self.landed(at, kind, z)], quad)
            return
        conditions = [self.has(at, z)]
        self.plane_pair(conditions, at, z)

        def end():
            self.arrived(at, 1, z)
            self.arrived(at, 2, z)
            total = [self.landed(at, kind, z) for kind in (1, 2)] + [self.part_of(at, z, quads[0])]
            self.finish_rows(piece, total)

        when(conditions, end)

    def run(self, plan, stages):
        for kind, at, number in plan:
            if kind == 0:
                self.raw(at, number)
            elif kind == 1:
                self.pair(at, number)
            elif kind == 2:
                self.line(at, number)
            elif kind == 3:
                self.tail(at)
            else:
                stages[at]()

    def finish(self):
        for conditions, which in self.sends:
            when(conditions, lambda: self.copy(*which).wait_send())


class Moves:
    def __init__(self, place, local_sems, send_sems, recv_sems):
        self.place = place
        self.other = (place.index(place.z), 1 - place.core)
        self.local_sems, self.send_sems, self.recv_sems = local_sems, send_sems, recv_sems
        self.locals, self.remotes = 0, 0
        self.to_end = []

    def local(self, source, target):
        made = pltpu.make_async_copy(source, target, self.local_sems.at[self.locals])
        self.locals += 1
        made.start()
        return made

    def save(self, source, target):
        self.to_end.append(self.local(source, target).wait)

    def across(self, source, target, arrives=None):
        sems = dict(
            send_sem=self.send_sems.at[self.remotes],
            recv_sem=self.recv_sems.at[self.remotes],
            device_id=self.other,
            device_id_type=MESH,
        )
        self.remotes += 1
        made = pltpu.make_async_remote_copy(src_ref=source, dst_ref=target, **sems)
        made.start()
        self.to_end.append(made.wait_send)
        arrives = target if arrives is None else arrives
        return pltpu.make_async_remote_copy(src_ref=arrives, dst_ref=arrives, **sems)

    def peer(self, source, target, step):
        made = pltpu.make_async_remote_copy(
            src_ref=source,
            dst_ref=target,
            send_sem=self.send_sems.at[self.remotes],
            recv_sem=self.recv_sems.at[self.remotes],
            device_id=self.place.device(step),
            device_id_type=MESH,
        )
        self.remotes += 1
        made.start()
        self.to_end.append(made.wait_send)
        return made

    def finish(self):
        for wait in self.to_end:
            wait()


class Rows:
    def __init__(self, text, visual):
        self.text, self.visual = text, visual
        self.split = 2 * text
        self.count = 2 * (text + visual)
        self.spans = ((0, self.split), (self.split, self.count))
        self.own = ((0, text), (self.split, self.split + visual))
        self.other = ((text, self.split), (self.split + visual, self.count))
        self.packed = ((0, text), (text, text + visual))
        self.sizes = (chunk_of(text), chunk_of(visual))

    def over(self, body):
        for s, (first, last) in enumerate(self.spans):
            over_rows(first, last, self.sizes[s], functools.partial(body, s))

    def over_own(self, s, body):
        shift = self.own[s][0] - self.packed[s][0]

        def shifted(piece):
            body(pl.ds(pl.multiple_of(piece.start + shift, row_tile), piece.size), piece)

        over_rows(*self.packed[s], self.sizes[s], shifted)

    def swap_parts(self, moves, wide, received, which=(0, 1)):
        return [
            moves.across(wide.at[slice(*self.other[s])], received.at[slice(*self.packed[s])])
            for s in which
        ]

    def swap_own(self, moves, ref, s):
        return moves.across(ref.at[slice(*self.own[s])], ref.at[slice(*self.other[s])])


class Plane:
    steps = (by_x, by_y, crosswise)

    def __init__(self, place, moves, size):
        self.place, self.moves, self.size = place, moves, size
        self.half = 4 * size

    def part(self, ref, at, count=1):
        return ref.at[at * self.size : (at + count) * self.size]

    def spread(self, own, target):
        other = self.moves.across(own, self.part(target, 4))
        return other, [
            self.moves.peer(own, self.part(target, 1 + at), step) for at, step in enumerate(self.steps)
        ]

    def pass_on(self, target, arrivals):
        for arrival in arrivals:
            arrival.wait_recv()
        return self.moves.across(self.part(target, 1, 3), self.part(target, 5, 3))

    def halve(self, wide, received):
        return self.moves.across(self.part(wide, 4, 4), received)

    def share(self, wide, received, outgoing, landing):
        outgoing[...] = (
            wide[self.size : self.half, :] + received[self.size : self.half, :]
        ).astype(outgoing.dtype)
        return [
            self.moves.peer(self.part(outgoing, at), self.part(landing, at), step)
            for at, step in enumerate(self.steps)
        ]

    def total(self, wide, received, landing):
        value = wide[: self.size, :] + received[: self.size, :]
        for at in range(3):
            value = value + landing[at * self.size : (at + 1) * self.size, :].astype(full)
        return value


def chunk_of(count):
    return max(size for size in range(row_tile, 385, row_tile) if count % size == 0)


def query_spans(count):
    edges = list(range(0, count - 256, 512)) + [count]
    return list(zip(edges[:-1], edges[1:]))


def head_wide(values, odd):
    empty = jnp.zeros_like(values)
    return jnp.concatenate([empty, values] if odd else [values, empty], 0)


def column_of(row, count):
    return jnp.broadcast_to(row, (lane, count)).T


def scratch_of(group):
    return [pltpu.VMEM(shape, dtype) for shape, dtype in group]


def shapes_of(group):
    return [jax.ShapeDtypeStruct(shape, dtype) for shape, dtype in group]


def same_as(arrays):
    return [(array.shape, array.dtype) for array in arrays]


def sems(*counts):
    return [pltpu.SemaphoreType.DMA(count if isinstance(count, tuple) else (count,)) for count in counts]


def specs_of(count, in_vmem):
    spaces = [pltpu.VMEM] * in_vmem + [pl.ANY] * (count - in_vmem)
    return [pl.BlockSpec(memory_space=space) for space in spaces]


front_pieces = (
    (0, 0, 0, 48, 0, 0), (0, 1, 0, 48, 1, 0), (1, 0, 0, 16, 0, 0), (1, 0, 16, 32, 1, 0),
    (2, 0, 0, 48, 0, 0), (2, 1, 0, 48, 1, 0), (3, 0, 0, 16, 0, 0), (3, 0, 16, 16, 1, 0),
    (3, 0, 32, 64, 0, 1), (4, 0, 0, 48, 0, 3), (5, 0, 0, 96, 0, 2),
)
front_plan = (
    (0, 1, 0), (5, 0, 0), (0, 9, 0), (0, 5, 0), (0, 0, 0), (2, 1, 1), (2, 0, 1), (2, 1, 2), (1, 1, 0),
    (2, 5, 1), (3, 9, 1), (0, 2, 0), (1, 0, 1), (2, 0, 2), (1, 1, 1), (0, 10, 0), (2, 1, 3), (0, 7, 0),
    (1, 5, 1), (3, 9, 2), (1, 1, 3), (2, 2, 1), (0, 6, 0), (2, 7, 1), (1, 0, 2), (5, 1, 0), (1, 0, 0),
    (2, 0, 3), (1, 1, 2), (2, 7, 2), (2, 5, 2), (2, 5, 3), (0, 4, 0), (1, 0, 3), (0, 3, 0), (2, 4, 1),
    (1, 5, 3), (2, 2, 2), (2, 6, 1), (2, 4, 2), (1, 7, 1), (0, 8, 0), (4, 0, 0), (1, 2, 0), (2, 7, 3),
    (2, 10, 1), (5, 2, 0), (5, 3, 0), (1, 5, 0), (3, 9, 3), (2, 2, 3), (2, 3, 1), (2, 10, 2), (2, 4, 3),
    (5, 4, 0), (5, 5, 0), (5, 6, 0), (3, 9, 4), (2, 3, 2), (1, 2, 3), (1, 4, 2), (5, 7, 0), (3, 8, 1),
    (2, 6, 2), (5, 8, 0), (1, 4, 3), (1, 5, 2), (1, 4, 1), (1, 3, 1), (1, 4, 0), (1, 3, 0), (2, 10, 3),
    (1, 7, 0), (4, 4, 0), (1, 2, 1), (1, 2, 2), (5, 9, 0), (5, 10, 0), (1, 3, 2), (1, 6, 0), (1, 6, 1),
    (5, 11, 0), (3, 8, 2), (1, 7, 2), (1, 7, 3), (4, 2, 0), (5, 12, 0), (2, 3, 3), (1, 3, 3), (5, 13, 0),
    (2, 6, 3), (5, 14, 0), (4, 5, 0), (5, 21, 0), (3, 8, 3), (4, 1, 0), (5, 16, 0), (1, 6, 3), (1, 6, 2),
    (5, 17, 0), (5, 22, 0), (5, 15, 0), (3, 8, 4), (5, 19, 0), (4, 3, 0), (5, 18, 0), (5, 20, 0),
)
ffn_pieces = (
    (0, 0, 0, 48, 0, 0), (0, 0, 48, 48, 1, 0), (1, 0, 0, 96, 0, 2),
)
ffn_plan = (
    (0, 1, 0), (0, 0, 0), (0, 2, 0), (0, 1, 1), (4, 2, 0), (0, 2, 1), (0, 0, 1), (0, 2, 2), (1, 0, 0),
    (0, 0, 2), (2, 2, 0), (1, 1, 0), (4, 0, 0), (4, 1, 0), (1, 0, 1), (0, 1, 2), (2, 2, 1), (4, 10, 0),
    (1, 1, 1), (2, 2, 2), (4, 4, 0), (4, 3, 0), (2, 0, 0), (0, 1, 3), (4, 9, 0), (2, 1, 0), (1, 0, 2),
    (1, 1, 2), (0, 2, 3), (0, 0, 3), (4, 5, 0), (4, 13, 0), (4, 7, 0), (2, 1, 1), (4, 8, 0), (1, 1, 3),
    (2, 0, 1), (2, 1, 2), (2, 0, 2), (4, 14, 0), (4, 6, 0), (1, 0, 3), (2, 2, 3), (4, 11, 0), (4, 12, 0),
    (2, 1, 3), (2, 0, 3), (4, 15, 0),
)
attention_pieces = (
    (0, 0, 0, 16, 0, 0), (0, 0, 16, 16, 1, 0), (0, 0, 32, 16, 1, 1), (1, 0, 0, 48, 0, 0),
    (1, 1, 0, 48, 1, 0), (2, 0, 0, 48, 0, 0), (2, 1, 0, 48, 1, 0), (3, 0, 0, 48, 0, 3),
)
attention_plan = (
    (0, 1, 0), (0, 7, 0), (0, 4, 0), (0, 3, 0), (0, 0, 0), (0, 1, 1), (0, 7, 1), (0, 2, 0), (4, 0, 0),
    (0, 0, 1), (0, 1, 2), (0, 0, 2), (4, 1, 0), (2, 7, 0), (1, 1, 0), (0, 2, 1), (1, 4, 0), (0, 3, 1),
    (0, 4, 1), (1, 0, 0), (1, 0, 1), (4, 2, 0), (4, 3, 0), (1, 4, 1), (0, 3, 2), (0, 3, 3), (2, 2, 0),
    (0, 2, 2), (0, 4, 2), (4, 4, 0), (0, 0, 3), (1, 1, 1), (1, 1, 2), (4, 5, 0), (1, 3, 0), (1, 4, 2),
    (1, 3, 1), (0, 7, 2), (2, 7, 1), (1, 3, 2), (0, 1, 3), (2, 7, 2), (0, 7, 3), (4, 6, 0), (4, 7, 0),
    (1, 3, 3), (1, 0, 2), (0, 4, 3), (2, 7, 3), (4, 8, 0), (2, 4, 0), (4, 9, 0), (0, 5, 0), (0, 6, 0),
    (2, 0, 0), (2, 4, 1), (0, 2, 3), (1, 0, 3), (2, 1, 0), (2, 3, 0), (2, 0, 1), (1, 5, 0), (0, 6, 1),
    (1, 6, 0), (2, 1, 1), (0, 5, 1), (2, 2, 1), (2, 3, 1), (1, 4, 3), (2, 0, 2), (2, 2, 2), (3, 7, 0),
    (2, 1, 2), (1, 1, 3), (2, 6, 0), (2, 4, 2), (1, 5, 1), (2, 0, 3), (0, 6, 2), (2, 3, 2), (2, 2, 3),
    (1, 6, 1), (0, 5, 2), (2, 5, 0), (2, 4, 3), (2, 5, 1), (1, 6, 2), (1, 5, 2), (0, 6, 3), (2, 3, 3),
    (2, 6, 1), (3, 2, 0), (0, 5, 3), (4, 13, 0), (2, 1, 3), (4, 10, 0), (2, 5, 2), (2, 6, 2), (1, 5, 3),
    (1, 6, 3), (4, 11, 0), (4, 12, 0), (2, 5, 3), (2, 6, 3),
)


class FrontIn(NamedTuple):
    w_qkv: object
    w_gate: object
    w_up: object
    gain_attn: object
    gain_ffn: object
    text_mask: object
    visual_mask: object
    text: object
    visual: object
    text_dy: object
    visual_dy: object
    w_out: object
    w_down: object


class FrontOut(NamedTuple):
    full_qkv: object
    full_up: object
    full_out: object
    full_down: object
    full_up_v: object
    full_down_v: object
    h: object
    qkv: object
    gates_t: object
    text_t: object
    visual_t: object
    logs: object
    mix_t: object
    middle: object
    hm: object
    hm_v: object
    act: object
    act_v: object
    slope: object
    slope_v: object
    part_down: object
    part_down_v: object
    dy: object
    dy_v: object
    gains: object
    bias: object


class FrontKept(NamedTuple):
    s_h: object
    s_qkv: object
    s_gates_t: object
    s_text_t: object
    s_visual_t: object
    s_logs: object
    s_mix_t: object
    s_middle: object
    s_hm: object
    s_hm_v: object
    s_act: object
    s_act_v: object
    s_slope: object
    s_slope_v: object
    s_part_down: object
    s_part_down_v: object
    s_dy: object
    s_dy_v: object
    s_gains: object
    s_bias: object


class FrontScratch(NamedTuple):
    own_qkv: object
    own_up: object
    own_up_v: object
    s_w_qkv: object
    s_w_up: object
    s_w_up_v: object
    s_w_out: object
    x: object
    wide: object
    received: object
    gate_rows: object
    q_t: object
    v_t: object
    mix: object


def prepare_shards(v, core, heads):
    first = core == 0
    rows = v.w_qkv.shape[1]
    third = v.w_qkv.shape[2] // 3
    half = third // 2
    for s in range(2):
        for at in range(3):
            columns = [v.w_qkv[s, :, at * third + way * half : at * third + (way + 1) * half] for way in (0, 1)]
            v.own_qkv[s, :, at * half : (at + 1) * half] = jnp.where(first, *columns)
        gate = v.w_gate[:, s, :].astype(full)
        gate = jnp.where(first, gate[:heads], gate[heads:])
        gains = [ref[s : s + 1, :].astype(full) for ref in (v.gain_attn, v.gain_ffn)]
        small = jnp.concatenate([gate, *gains, jnp.zeros((lane - heads - 2, rows), full)], 0)
        small = jnp.concatenate([small, jnp.zeros((lane, lane - rows), full)], 1).T[:rows]
        v.own_qkv[s, :, 3 * half :] = small.astype(low)


def prepare_hidden(v, core, block):
    first = core == 0
    pieces = []
    for s in range(2):
        for start in range(0, v.w_up.shape[2], 2 * block):
            ways = [v.w_up[s, :, start + way * block : start + (way + 1) * block].astype(full) for way in (0, 1)]
            pieces.append(jnp.where(first, *ways))
    count = len(pieces) // 2
    v.own_up[0, :, :] = jnp.concatenate(pieces[:count], 1).astype(low)
    for quad in range(4):
        v.own_up_v[quad, :, :] = jnp.concatenate(pieces[count + quad :: 4], 1).astype(low)


def prepare_bias(v, core):
    pieces = []
    for ref in (v.text_mask, v.visual_mask):
        mask = ref[...].astype(full)
        half = mask.shape[1] // 2
        swapped = jnp.concatenate([mask[:, half:], mask[:, :half]], 1)
        pieces.append(jnp.where(core == 0, mask, swapped))
    row = jnp.concatenate(pieces, 1)
    v.s_bias[...] = column_of(jnp.where(row > 0.0, 0.0, big_negative), row.shape[1])


def attend_head(rows, head_width, v, number):
    width = v.s_qkv.shape[1] // 3
    pair = 2 * head_width
    at, odd = number // 2, number % 2
    keys = v.s_qkv[:, width + at * pair : width + (at + 1) * pair]
    bias = v.s_bias[:, 0:1]
    head = slice(number * head_width, (number + 1) * head_width)
    for first, last in query_spans(rows.count):
        scores = dot(keys, head_wide(v.q_t[head, first:last], odd)) + bias
        for t, target in enumerate((v.s_text_t, v.s_visual_t)):
            start, stop = rows.spans[t]
            part = scores[start:stop]
            top = jnp.max(part, 0, keepdims=True)
            raised = jnp.exp(part - top)
            total = jnp.sum(raised, 0, keepdims=True)
            probs = (raised * (1.0 / total)).astype(low)
            target[head, first:last] = dot(v.v_t[head, start:stop], probs)
            row = 8 * t + number
            v.s_logs[row : row + 1, first:last] = top + jnp.log(total)


def front_kernel(line_size, heads, scale, pieces, plan, *refs):
    groups = []
    for group in (FrontIn, FrontOut, FrontKept, FrontScratch):
        count = len(group._fields)
        groups.append(group(*refs[:count]))
        refs = refs[count:]
    v = merged(*groups)
    place = Place(line_size)
    core = place.core
    rows = Rows(v.text.shape[1], v.visual.shape[1])
    shard, block = v.w_qkv.shape[1], v.w_down.shape[1] // 2
    owns = (
        (v.own_qkv, 0),
        (v.own_up, 0),
        (v.w_out, 0),
        (v.w_down, core * block),
        (v.own_up_v, 0),
        (v.w_down.at[pl.ds(1, 1)], core * block),
    )
    gather = Gather(
        place,
        pieces,
        (shard, shard, shard, block, shard, block),
        (False, False, True, False, False, False),
        owns,
        (v.s_w_qkv, v.s_w_up, v.s_w_out, v.full_down, v.s_w_up_v, v.full_down_v),
        *refs[:3],
    )
    moves = Moves(place, *refs[3:])
    width = v.s_qkv.shape[1] // 3
    head_width = width // heads
    hidden = v.s_act.shape[1]
    arrivals = {}

    place.greet()
    prepare_shards(v, core, heads)
    place.meet()
    plane = Plane(place, moves, rows.visual)
    loads, swaps = [], []
    for s, source in enumerate((v.text, v.visual)):
        loads.append(moves.local(source.at[0], v.x.at[slice(*rows.own[s])]))
        swaps.append(moves.across(source.at[0], v.x.at[slice(*rows.other[s])]))
    loads.append(moves.local(v.text_dy.at[0], v.s_dy.at[slice(*rows.own[0])]))
    loads.append(moves.local(v.visual_dy.at[0], plane.part(v.s_dy_v, 0)))
    swaps.append(moves.across(v.text_dy.at[0], v.s_dy.at[slice(*rows.other[0])]))

    def prepare():
        prepare_hidden(v, core, block)

    def norm():
        prepare_bias(v, core)
        moves.save(v.s_bias, v.bias)
        for s in range(2):
            loads[s].wait()
            swaps[s].wait_recv()

        def body(s, piece):
            v.wide[piece, :] = normalize(v.x[piece, :].astype(full))[0]

        rows.over(body)

    def lower():
        moves.save(v.s_w_qkv, v.full_qkv)
        for s in range(2):
            small = v.s_w_qkv[s, :, 3 * width :].astype(full).T
            v.s_gains[s, :, :] = small[heads : heads + 2]

        def body(s, piece):
            v.s_h[piece, :] = (v.wide[piece, :] * v.s_gains[s, 0:1, :]).astype(low)

        rows.over(body)
        moves.save(v.s_gains, v.gains)
        moves.save(v.s_h, v.h)

    def project(s):
        first, last = rows.spans[s]
        even = 3 * width // 256 * 256

        def columns(piece):
            v.s_qkv[first:last, piece] = dot(v.s_h[first:last, :], v.s_w_qkv[s, :, piece]).astype(low)

        over_columns(0, even, 256, columns)
        rest = dot(v.s_h[first:last, :], v.s_w_qkv[s, :, even:])
        v.s_qkv[first:last, even:] = rest[:, : 3 * width - even].astype(low)
        v.gate_rows[first:last, :] = rest[:, 3 * width - even :]

    def project_visual():
        project(1)
        v.s_gates_t[...] = jax.nn.sigmoid(v.gate_rows[...].T[:8, :])
        v.q_t[...] = (v.s_qkv[:, :width] * jnp.asarray(scale, low)).T
        v.v_t[...] = v.s_qkv[:, 2 * width :].T
        moves.save(v.s_qkv, v.qkv)
        moves.save(v.s_gates_t, v.gates_t)

    def mix():
        moves.save(v.s_text_t, v.text_t)
        moves.save(v.s_visual_t, v.visual_t)
        moves.save(v.s_logs, v.logs)
        is_text = lax.broadcasted_iota(jnp.int32, (1, rows.count), 1) < rows.split
        for head in range(heads):
            span = slice(head * head_width, (head + 1) * head_width)
            gate = v.s_gates_t[head : head + 1, :]
            to_text = jnp.where(is_text, gate, 1.0 - gate)
            v.s_mix_t[span, :] = (
                to_text * v.s_text_t[span, :] + (1.0 - to_text) * v.s_visual_t[span, :]
            ).astype(low)
        v.mix[...] = v.s_mix_t[...].T
        moves.save(v.s_mix_t, v.mix_t)

    def branch():
        moves.save(v.s_w_out, v.full_out)
        for s, (first, last) in enumerate(rows.spans):

            def columns(piece):
                v.wide[first:last, piece] = dot(v.mix[first:last, :], v.s_w_out[s, :, piece])

            over_columns(0, v.wide.shape[1], 256, columns)
        arrivals[0] = rows.swap_parts(moves, v.wide, v.received)

    def spread_dy():
        arrivals[2] = plane.spread(v.visual_dy.at[0], v.s_dy_v)

    def pass_dy():
        arrivals[3] = plane.pass_on(v.s_dy_v, arrivals[2][1])

    def middle_rows(s, ref, start):
        arrivals[0][s].wait_recv()

        def body(piece, packed):
            value = v.x[piece, :].astype(full) + v.wide[piece, :] + v.received[packed, :]
            v.s_middle[packed, :] = value
            to = pl.ds(pl.multiple_of(packed.start - start, row_tile), packed.size)
            ref[to, :] = (normalize(value)[0] * v.s_gains[s, 1:2, :]).astype(low)

        rows.over_own(s, body)

    def middle_visual():
        middle_rows(1, v.s_hm_v, rows.packed[1][0])
        arrivals[4] = plane.spread(plane.part(v.s_hm_v, 0), v.s_hm_v)

    def middle_text():
        middle_rows(0, v.s_hm, 0)
        arrivals[1] = rows.swap_own(moves, v.s_hm, 0)
        moves.save(v.s_middle, v.middle)

    def pass_hm():
        arrivals[5] = plane.pass_on(v.s_hm_v, arrivals[4][1])

    def up_part(hm, w_up, act_ref, slope_ref, start, stop):
        size = 256 if (stop - start) % 256 == 0 else lane

        def columns(piece):
            act, slope = gelu_both(dot(hm[...], w_up[0, :, piece]))
            act_ref[:, piece] = act.astype(low)
            slope_ref[:, piece] = slope.astype(low)

        over_columns(start, stop, size, columns)

    def up_first():
        moves.save(v.s_w_up, v.full_up)
        arrivals[1].wait_recv()
        loads[2].wait()
        swaps[2].wait_recv()
        moves.save(v.s_hm, v.hm)
        moves.save(v.s_dy, v.dy)
        up_part(v.s_hm, v.s_w_up, v.s_act, v.s_slope, 0, hidden // 2)

    def up_second():
        up_part(v.s_hm, v.s_w_up, v.s_act, v.s_slope, hidden // 2, hidden)
        moves.save(v.s_act, v.act)
        moves.save(v.s_slope, v.slope)

    def up_visual():
        moves.save(v.s_w_up_v, v.full_up_v)
        arrivals[4][0].wait_recv()
        arrivals[5].wait_recv()
        moves.save(v.s_hm_v, v.hm_v)
        up_part(v.s_hm_v, v.s_w_up_v, v.s_act_v, v.s_slope_v, 0, v.s_act_v.shape[1])
        moves.save(v.s_act_v, v.act_v)
        moves.save(v.s_slope_v, v.slope_v)

    def down_part(act, dy, part):
        count = act.shape[1]

        def columns(piece):
            part[0, piece, :] = dot_rows(act[:, piece], dy[...]).astype(low)

        over_columns(0, count, 256 if count % 256 == 0 else lane, columns)

    def down_text():
        down_part(v.s_act, v.s_dy, v.s_part_down)
        moves.save(v.s_part_down, v.part_down)

    def down_visual():
        loads[3].wait()
        arrivals[2][0].wait_recv()
        arrivals[3].wait_recv()
        moves.save(v.s_dy_v, v.dy_v)
        down_part(v.s_act_v, v.s_dy_v, v.s_part_down_v)
        moves.save(v.s_part_down_v, v.part_down_v)

    stages = [prepare, norm, lower, functools.partial(project, 0), project_visual]
    stages += [functools.partial(attend_head, rows, head_width, v, head) for head in range(heads)]
    stages += [mix, branch, middle_visual, middle_text, pass_hm, up_first, up_second, up_visual]
    stages += [down_text, down_visual, spread_dy, pass_dy]
    gather.run(plan, stages)
    moves.finish()
    gather.finish()


def front(n_docs, heads, scale, pieces, plan, inputs):
    line_size = n_docs // 4
    count = 2 * (inputs.text.shape[1] + inputs.visual.shape[1])
    dim = inputs.w_out.shape[2]
    width, hidden = inputs.w_qkv.shape[2] // 6, inputs.w_up.shape[2] // 2
    text, plane = 2 * inputs.text.shape[1], 8 * inputs.visual.shape[1]
    wide = 3 * width + lane
    shard = inputs.w_qkv.shape[1]
    kept = FrontKept(
        s_h=((count, dim), low),
        s_qkv=((count, 3 * width), low),
        s_gates_t=((8, count), full),
        s_text_t=((width, count), full),
        s_visual_t=((width, count), full),
        s_logs=((16, count), full),
        s_mix_t=((width, count), low),
        s_middle=((count // 2, dim), full),
        s_hm=((text, dim), low),
        s_hm_v=((plane, dim), low),
        s_act=((text, hidden), low),
        s_act_v=((plane, hidden // 4), low),
        s_slope=((text, hidden), low),
        s_slope_v=((plane, hidden // 4), low),
        s_part_down=((1, hidden, dim), low),
        s_part_down_v=((1, hidden // 4, dim), low),
        s_dy=((text, dim), low),
        s_dy_v=((plane, dim), low),
        s_gains=((2, 2, dim), full),
        s_bias=((count, lane), full),
    )
    weights = (
        ((2, dim, wide), low),
        ((1, dim, hidden), low),
        ((2, width, dim), low),
        ((1, hidden, dim), low),
        ((1, dim, hidden // 4), low),
        ((1, hidden // 4, dim), low),
    )
    scratch = FrontScratch(
        own_qkv=((2, shard, wide), low),
        own_up=((1, shard, hidden), low),
        own_up_v=((4, shard, hidden // 4), low),
        s_w_qkv=weights[0],
        s_w_up=weights[1],
        s_w_up_v=weights[4],
        s_w_out=weights[2],
        x=((count, dim), low),
        wide=((count, dim), full),
        received=((count // 2, dim), full),
        gate_rows=((count, lane), full),
        q_t=((width, count), low),
        v_t=((width, count), low),
        mix=((count, width), low),
    )
    results = FrontOut(*weights, *kept)
    values = pl.pallas_call(
        functools.partial(front_kernel, line_size, heads, scale, pieces, plan),
        out_shape=shapes_of(results),
        in_specs=specs_of(len(inputs), 7),
        out_specs=specs_of(len(results), 0),
        scratch_shapes=scratch_of(kept)
        + scratch_of(scratch)
        + sems((len(pieces), n_docs, 5), (len(pieces), n_docs), len(pieces), 40, 24, 24),
        compiler_params=pltpu.CompilerParams(
            collective_id=0, has_side_effects=True, vmem_limit_bytes=vmem_limit
        ),
        name="gather_and_front",
    )(*inputs)
    return FrontOut(*values)


def scatter_buffers(pieces, arrays, splits, n_docs):
    line_size = n_docs // 4
    group = []
    for piece in pieces:
        ends = line_size // 2 if splits[piece.array] else line_size
        block = (piece.rows, arrays[piece.array][0][2])
        if piece.route == lines_first:
            group += [((ends, *block), low)] * 5
        elif piece.route == line_only:
            group += [((1, row_tile, lane), low)] * 3 + [((ends, 1, *block), low)] * 2
        else:
            group += [((1, *block), low)] * 3 + [((ends, 4, *block), low)] * 2
    return scratch_of(group)


def grouped(refs, size):
    return [refs[first : first + size] for first in range(0, len(refs), size)]


def norm_back(grad, normed, inverse, gain):
    scaled = grad * gain
    return inverse * (
        scaled
        - jnp.mean(scaled, -1, keepdims=True)
        - normed * jnp.mean(scaled * normed, -1, keepdims=True)
    )


class FfnIn(NamedTuple):
    full_down: object
    dy: object
    slope: object
    full_up: object
    part_down: object
    hm: object
    middle: object
    gains: object
    act: object
    full_out: object
    mix_t: object
    text_t: object
    visual_t: object
    gates_t: object
    full_down_v: object
    dy_v: object
    slope_v: object
    full_up_v: object
    part_down_v: object
    hm_v: object
    act_v: object


class FfnLoaded(NamedTuple):
    s_full_down: object
    s_dy: object
    s_slope: object
    s_full_up: object
    s_part_down: object
    s_hm: object
    s_middle: object
    s_gains: object
    s_act: object
    s_full_out: object
    s_mix_t: object
    s_text_t: object
    s_visual_t: object
    s_gates_t: object
    s_full_down_v: object
    s_dy_v: object
    s_slope_v: object
    s_full_up_v: object
    s_part_down_v: object
    s_hm_v: object
    s_act_v: object


class FfnOut(NamedTuple):
    text_out: object
    visual_out: object
    stage_down: object
    part_up: object
    part_up_v: object
    part_out: object
    grad_middle: object
    gain_part: object
    gate_grad_t: object
    text_grad_t: object
    visual_grad_t: object


class FfnScratch(NamedTuple):
    s_part_up: object
    s_part_up_v: object
    s_part_out: object
    s_grad_middle: object
    s_gain_part: object
    s_gate_grad_t: object
    s_text_grad_t: object
    s_visual_grad_t: object
    stage: object
    wide: object
    wide_out: object
    received: object
    received_out: object
    branch: object
    result: object
    mix_grad: object
    mix_grad_t: object
    wide_v: object
    received_v: object
    outgoing_v: object
    landing_v: object
    wide_out_v: object
    received_out_v: object
    outgoing_out_v: object
    landing_out_v: object


def ffn_kernel(line_size, heads, pieces, plan, *refs):
    groups = []
    for group in (FfnIn, FfnOut, FfnLoaded, FfnScratch):
        count = len(group._fields)
        groups.append(group(*refs[:count]))
        refs = refs[count:]
    v = merged(*groups)
    buffers = grouped(refs[: 5 * len(pieces)], 5)
    send_sems, recv_sems, *move_sems = refs[5 * len(pieces) :]
    place = Place(line_size)
    moves = Moves(place, *move_sems)
    rows = Rows(v.text_out.shape[1], v.visual_out.shape[1])
    width = v.mix_t.shape[0]
    head_width = width // heads
    dim = v.hm.shape[1]
    arrivals = {}

    plane = Plane(place, moves, rows.visual)

    def finish_rows(piece, total):
        add_rows(v.stage.at[piece.array], total, piece.first)

    scatter = Scatter(
        place,
        pieces,
        (False, False),
        (v.part_down, v.part_down_v),
        (v.s_part_down, v.s_part_down_v),
        buffers,
        send_sems,
        recv_sems,
        finish_rows,
    )
    place.greet()
    loads = FfnIn(*(moves.local(source, target) for source, target in zip(groups[0], groups[2])))
    place.meet()

    def hidden(dy, w_down, slope):
        count = slope.shape[1]

        def columns(piece):
            grad = dot_back(dy[...], w_down[0, piece, :])
            slope[:, piece] = (grad * slope[:, piece].astype(full)).astype(low)

        over_columns(0, count, 256 if count % 256 == 0 else lane, columns)

    def hidden_visual():
        loads.full_down_v.wait()
        loads.dy_v.wait()
        loads.slope_v.wait()
        hidden(v.s_dy_v, v.s_full_down_v, v.s_slope_v)

    def hidden_text():
        loads.full_down.wait()
        loads.dy.wait()
        loads.slope.wait()
        hidden(v.s_dy, v.s_full_down, v.s_slope)
        loads.part_down.wait()
        loads.part_down_v.wait()

    def back_visual():
        loads.full_up_v.wait()
        v.wide_v[...] = dot_back(v.s_slope_v[...], v.s_full_up_v[0, :, :])
        arrivals[0] = plane.halve(v.wide_v, v.received_v)

    def share_visual():
        arrivals[0].wait_recv()
        arrivals[1] = plane.share(v.wide_v, v.received_v, v.outgoing_v, v.landing_v)

    def back_text():
        loads.full_up.wait()

        def columns(piece):
            v.wide[:, piece] = dot_back(v.s_slope[...], v.s_full_up[0, piece, :])

        over_columns(0, dim, 256, columns)
        arrivals[2] = rows.swap_parts(moves, v.wide, v.received, (0,))[0]

    def up_part(hm, slope, part):
        def columns(piece):
            part[0, piece, :] = dot_rows(hm[:, piece], slope[...]).astype(low)

        over_columns(0, dim, 256, columns)

    def up_text():
        loads.hm.wait()
        up_part(v.s_hm, v.s_slope, v.s_part_up)
        moves.save(v.s_part_up, v.part_up)

    def up_visual():
        loads.hm_v.wait()
        up_part(v.s_hm_v, v.s_slope_v, v.s_part_up_v)
        moves.save(v.s_part_up_v, v.part_up_v)

    def middle_rows(s, piece, packed, grad, dy):
        normed, inverse = normalize(v.s_middle[packed, :])
        v.s_gain_part[s, 0:1, :] += jnp.sum(grad * normed, 0, keepdims=True)
        grad = dy.astype(full) + norm_back(grad, normed, inverse, v.s_gains[s, 1:2, :])
        v.s_grad_middle[packed, :] = grad
        v.branch[piece, :] = grad.astype(low)

    def middle_visual():
        loads.middle.wait()
        loads.gains.wait()
        v.s_gain_part[...] = jnp.zeros_like(v.s_gain_part)
        for arrival in arrivals[1]:
            arrival.wait_recv()
        grad = plane.total(v.wide_v, v.received_v, v.landing_v)
        middle_rows(1, slice(*rows.own[1]), slice(*rows.packed[1]), grad, v.s_dy_v[: rows.visual, :])
        arrivals[3] = rows.swap_own(moves, v.branch, 1)

    def middle_text():
        arrivals[2].wait_recv()

        def body(piece, packed):
            grad = v.wide[piece, :] + v.received[packed, :]
            middle_rows(0, piece, packed, grad, v.s_dy[piece, :])

        rows.over_own(0, body)
        arrivals[4] = rows.swap_own(moves, v.branch, 0)
        moves.save(v.s_gain_part, v.gain_part)
        moves.save(v.s_grad_middle, v.grad_middle)

    def result_text():
        loads.act.wait()

        def columns(piece):
            v.wide_out[:, piece] = dot(v.s_act[...], v.s_full_down[0, :, piece])

        over_columns(0, dim, 256, columns)
        arrivals[5] = rows.swap_parts(moves, v.wide_out, v.received_out, (0,))[0]

    def result_visual():
        loads.act_v.wait()
        v.wide_out_v[...] = dot(v.s_act_v[...], v.s_full_down_v[0, :, :])
        arrivals[6] = plane.halve(v.wide_out_v, v.received_out_v)

    def share_result():
        arrivals[6].wait_recv()
        arrivals[7] = plane.share(v.wide_out_v, v.received_out_v, v.outgoing_out_v, v.landing_out_v)

    def out_part():
        loads.full_out.wait()
        loads.mix_t.wait()
        for s, (first, last) in enumerate(rows.spans):
            arrivals[4 - s].wait_recv()
            v.s_part_out[s, :, :] = dot(v.s_mix_t[:, first:last], v.branch[first:last, :]).astype(low)
            v.mix_grad[first:last, :] = dot_back(v.branch[first:last, :], v.s_full_out[s, :, :])
        moves.save(v.s_part_out, v.part_out)

    def gates():
        loads.text_t.wait()
        loads.visual_t.wait()
        loads.gates_t.wait()
        v.mix_grad_t[...] = v.mix_grad[...].T
        is_text = lax.broadcasted_iota(jnp.int32, (1, rows.count), 1) < rows.split
        for head in range(heads):
            span = slice(head * head_width, (head + 1) * head_width)
            gate = v.s_gates_t[head : head + 1, :]
            to_text = jnp.where(is_text, gate, 1.0 - gate)
            grad = v.mix_grad_t[span, :]
            toward = jnp.sum(grad * (v.s_text_t[span, :] - v.s_visual_t[span, :]), 0, keepdims=True)
            v.s_gate_grad_t[head : head + 1, :] = (
                jnp.where(is_text, toward, -toward) * gate * (1.0 - gate)
            )
            v.s_text_grad_t[span, :] = (to_text * grad).astype(low)
            v.s_visual_grad_t[span, :] = ((1.0 - to_text) * grad).astype(low)
        v.s_gate_grad_t[heads:, :] = jnp.zeros((8 - heads, rows.count), full)
        moves.save(v.s_gate_grad_t, v.gate_grad_t)
        moves.save(v.s_text_grad_t, v.text_grad_t)
        moves.save(v.s_visual_grad_t, v.visual_grad_t)

    def finish_text():
        arrivals[5].wait_recv()

        def body(piece, packed):
            v.result[packed, :] = (
                v.s_middle[packed, :] + v.wide_out[piece, :] + v.received_out[packed, :]
            ).astype(low)

        rows.over_own(0, body)
        moves.save(v.result.at[slice(*rows.packed[0])], v.text_out.at[0])

    def finish_visual():
        for arrival in arrivals[7]:
            arrival.wait_recv()
        packed = slice(*rows.packed[1])
        total = plane.total(v.wide_out_v, v.received_out_v, v.landing_out_v)
        v.result[packed, :] = (v.s_middle[packed, :] + total).astype(low)
        moves.save(v.result.at[packed], v.visual_out.at[0])

    stages = [hidden_visual, back_visual, hidden_text, share_visual, back_text, up_text, up_visual]
    stages += [middle_visual, middle_text, result_text, result_visual, out_part, gates, share_result]
    scatter.run(plan, stages + [finish_text, finish_visual])
    moves.save(v.stage, v.stage_down)
    moves.finish()
    scatter.finish()


def ffn_back(n_docs, heads, pieces, plan, text, visual, inputs):
    line_size = n_docs // 4
    hidden = inputs.act.shape[1]
    width, count = inputs.mix_t.shape
    dim = inputs.hm.shape[1]
    rows = inputs.part_down.shape[1] // n_docs
    plane = 8 * visual.shape[1]
    scratch = FfnScratch(
        s_part_up=((1, dim, hidden), low),
        s_part_up_v=((1, dim, hidden // 4), low),
        s_part_out=((2, width, dim), low),
        s_grad_middle=((count // 2, dim), full),
        s_gain_part=((2, 8, dim), full),
        s_gate_grad_t=((8, count), full),
        s_text_grad_t=((width, count), low),
        s_visual_grad_t=((width, count), low),
        stage=((2, rows, dim), full),
        wide=((2 * text.shape[1], dim), full),
        wide_out=((2 * text.shape[1], dim), full),
        received=((text.shape[1], dim), full),
        received_out=((text.shape[1], dim), full),
        branch=((count, dim), low),
        result=((count // 2, dim), low),
        mix_grad=((count, width), full),
        mix_grad_t=((width, count), full),
        wide_v=((plane, dim), full),
        received_v=((plane // 2, dim), full),
        outgoing_v=((3 * plane // 8, dim), low),
        landing_v=((3 * plane // 8, dim), low),
        wide_out_v=((plane, dim), full),
        received_out_v=((plane // 2, dim), full),
        outgoing_out_v=((3 * plane // 8, dim), low),
        landing_out_v=((3 * plane // 8, dim), low),
    )
    results = FfnOut(
        (text.shape, low), (visual.shape, low), scratch.stage, *scratch[:8]
    )
    loaded = same_as(inputs)
    values = pl.pallas_call(
        functools.partial(ffn_kernel, line_size, heads, pieces, plan),
        out_shape=shapes_of(results),
        in_specs=specs_of(len(inputs), 0),
        out_specs=specs_of(len(results), 0),
        scratch_shapes=scratch_of(loaded)
        + scratch_of(scratch)
        + scatter_buffers(pieces, same_as([inputs.part_down, inputs.part_down_v]), (False, False), n_docs)
        + sems((len(pieces), line_size, 11), (len(pieces), line_size, 11), 40, 24, 24),
        compiler_params=pltpu.CompilerParams(
            collective_id=1, has_side_effects=True, vmem_limit_bytes=vmem_limit
        ),
        name="ffn_back_and_scatter",
    )(*inputs)
    return FfnOut(*values)


class AttentionIn(NamedTuple):
    qkv: object
    logs: object
    text_t: object
    visual_t: object
    text_grad_t: object
    visual_grad_t: object
    bias: object
    part_up: object
    part_up_v: object
    part_out: object
    gate_grad_t: object
    full_qkv: object
    h: object
    grad_middle: object
    gains: object
    gain_part: object
    stage_down: object
    text: object
    visual: object


class AttentionLoaded(NamedTuple):
    s_qkv: object
    s_logs: object
    s_text_t: object
    s_visual_t: object
    s_text_grad_t: object
    s_visual_grad_t: object
    s_bias: object
    s_part_up: object
    s_part_up_v: object
    s_part_out: object
    s_gate_grad_t: object
    s_full_qkv: object
    s_h: object
    s_grad_middle: object
    s_gains: object
    s_gain_part: object
    s_stage_down: object


class AttentionOut(NamedTuple):
    text_grad: object
    visual_grad: object
    grad_down: object
    grad_qkv: object
    grad_gate: object
    grad_up: object
    grad_out: object
    grad_gain_attn: object
    grad_gain_ffn: object


class AttentionScratch(NamedTuple):
    part_qkv: object
    x: object
    q_t: object
    k_t: object
    query_grad_t: object
    text_grad_n: object
    visual_grad_n: object
    key_sum: object
    value_sum: object
    grad_wide: object
    wide: object
    received: object
    gain_sum: object
    stage_up: object
    stage_out: object
    stage_qkv: object
    stage_up_v: object
    peer_up: object
    peer_up_v: object
    peer_small: object
    s_grad_up: object
    s_grad_gate: object
    s_grad_gain_attn: object
    s_grad_gain_ffn: object


def attend_head_back(rows, head_width, scale, v, number):
    width = v.s_qkv.shape[1] // 3
    pair = 2 * head_width
    at, odd = number // 2, number % 2
    columns = [slice(third * width + at * pair, third * width + (at + 1) * pair) for third in range(3)]
    keys, values = v.s_qkv[:, columns[1]], v.s_qkv[:, columns[2]]
    if not odd:
        v.key_sum[...] = jnp.zeros_like(v.key_sum)
        v.value_sum[...] = jnp.zeros_like(v.value_sum)
    mine = lax.broadcasted_iota(jnp.int32, (1, pair), 1) // head_width == odd
    bias = v.s_bias[:, 0:1]
    sets = (
        (v.s_text_t, v.s_text_grad_t, v.text_grad_n),
        (v.s_visual_t, v.s_visual_grad_t, v.visual_grad_n),
    )
    head = slice(number * head_width, (number + 1) * head_width)
    for first, last in query_spans(rows.count):
        scores = dot(keys, head_wide(v.q_t[head, first:last], odd)) + bias
        queries = jnp.where(mine, v.s_qkv[first:last, columns[0]] * jnp.asarray(scale, low), 0)
        pieces = []
        for t, (output_t, grad_t, grad) in enumerate(sets):
            start, stop = rows.spans[t]
            out_grad = grad_t[head, first:last]
            delta = jnp.sum(out_grad.astype(full) * output_t[head, first:last], 0, keepdims=True)
            row = 8 * t + number
            probs = jnp.exp(scores[start:stop] - v.s_logs[row : row + 1, first:last])
            grad_probs = dot(values[start:stop], head_wide(out_grad, odd))
            grad_scores = (probs * (grad_probs - delta)).astype(low)
            natural = jnp.where(mine, grad[first:last, columns[0]], 0)
            v.value_sum[start:stop, :] += dot(probs.astype(low), natural)
            v.key_sum[start:stop, :] += dot(grad_scores, queries)
            pieces.append(grad_scores)
        v.query_grad_t[head, first:last] = (
            dot(v.k_t[head, :], jnp.concatenate(pieces, 0)) * scale
        ).astype(low)
    if odd:
        v.grad_wide[:, columns[1]] = v.key_sum[...].astype(low)
        v.grad_wide[:, columns[2]] = v.value_sum[...].astype(low)


def attention_kernel(line_size, heads, scale, block, pieces, plan, *refs):
    groups = []
    for group in (AttentionIn, AttentionOut, AttentionLoaded, AttentionScratch):
        count = len(group._fields)
        groups.append(group(*refs[:count]))
        refs = refs[count:]
    v = merged(*groups)
    buffers = grouped(refs[: 5 * len(pieces)], 5)
    send_sems, recv_sems, *move_sems = refs[5 * len(pieces) :]
    place = Place(line_size)
    core = place.core
    moves = Moves(place, *move_sems)
    rows = Rows(v.text.shape[1], v.visual.shape[1])
    width = v.qkv.shape[1] // 3
    head_width = width // heads
    dim = v.h.shape[1]
    stages_of = (v.stage_up, v.stage_out, v.stage_qkv)
    arrivals = {}

    def finish_rows(piece, total, quad=quads[0]):
        if piece.route == plane_shared:
            add_rows(v.stage_up_v.at[place.index(0, *quad)], total, piece.first)
        else:
            add_rows(stages_of[piece.array].at[piece.part], total, piece.first)

    scatter = Scatter(
        place,
        pieces,
        (False, True, False, False),
        (v.part_up, v.part_out, v.part_qkv, v.part_up_v),
        (v.s_part_up, v.s_part_out, v.part_qkv, v.s_part_up_v),
        buffers,
        send_sems,
        recv_sems,
        finish_rows,
    )
    place.greet()
    loads = AttentionIn(
        *(moves.local(source, target) for source, target in zip(groups[0], groups[2])),
        *(moves.local(ref.at[0], v.x.at[slice(*rows.packed[s])]) for s, ref in enumerate((v.text, v.visual))),
    )
    place.meet()

    def prepare():
        for load in loads[:7]:
            load.wait()
        v.q_t[...] = (v.s_qkv[:, :width] * jnp.asarray(scale, low)).T
        v.k_t[...] = v.s_qkv[:, width : 2 * width].T
        v.text_grad_n[...] = v.s_text_grad_t[...].T
        v.visual_grad_n[...] = v.s_visual_grad_t[...].T
        loads.part_up.wait()
        loads.part_up_v.wait()
        loads.part_out.wait()

    def back_qkv():
        loads.gate_grad_t.wait()
        loads.full_qkv.wait()
        v.grad_wide[:, :width] = v.query_grad_t[...].T
        empty = jnp.zeros((lane - 8, rows.count), full)
        v.grad_wide[:, 3 * width :] = jnp.concatenate([v.s_gate_grad_t[...], empty], 0).T.astype(low)
        for s, (first, last) in enumerate(rows.spans):

            def columns(piece):
                v.wide[first:last, piece] = dot_back(v.grad_wide[first:last, :], v.s_full_qkv[s, piece, :])

            over_columns(0, dim, 256, columns)
        arrivals[0] = rows.swap_parts(moves, v.wide, v.received)

    def qkv_part():
        loads.h.wait()
        for s, (first, last) in enumerate(rows.spans):

            def columns(piece):
                v.part_qkv[s, piece, :] = dot_rows(v.s_h[first:last, piece], v.grad_wide[first:last, :]).astype(low)

            over_columns(0, dim, 256, columns)

    def tokens():
        loads.grad_middle.wait()
        loads.gains.wait()
        loads.gain_part.wait()
        for s in range(2):
            loads[17 + s].wait()
            arrivals[0][s].wait_recv()
            v.gain_sum[s, :, :] = jnp.zeros((lane, dim), full)
            v.gain_sum[s, heads + 1 : heads + 2, :] = v.s_gain_part[s, 0:1, :]

            def body(piece, packed):
                normed, inverse = normalize(v.x[packed, :].astype(full))
                grad = v.wide[piece, :] + v.received[packed, :]
                v.gain_sum[s, heads : heads + 1, :] += jnp.sum(grad * normed, 0, keepdims=True)
                v.s_grad_middle[packed, :] += norm_back(grad, normed, inverse, v.s_gains[s, 0:1, :])

            rows.over_own(s, body)
            small = v.part_qkv[s, :, 3 * width :].astype(full) + v.gain_sum[s, :, :].T
            v.part_qkv[s, :, 3 * width :] = small.astype(low)
            ref = (v.text_grad, v.visual_grad)[s]
            moves.save(v.s_grad_middle.at[slice(*rows.packed[s])], ref.at[0])

    def share_down():
        loads.stage_down.wait()
        block = v.s_stage_down.shape[1]
        mine = lambda of: v.grad_down.at[:, pl.ds(pl.multiple_of(of * block, row_tile), block), :]
        moves.save(v.s_stage_down, mine(core))
        arrivals[3] = moves.across(v.s_stage_down, mine(core), mine(1 - core))

    def share_up():
        arrivals[1] = moves.across(v.stage_up, v.peer_up)
        arrivals[2] = moves.across(v.stage_up_v, v.peer_up_v)

    def share_out():
        owner = place.z // (line_size // 2) == core
        moves_out = (
            pltpu.make_async_copy(v.stage_out, v.grad_out, moves.local_sems.at[moves.locals]),
            pltpu.make_async_remote_copy(
                src_ref=v.stage_out,
                dst_ref=v.grad_out,
                send_sem=moves.send_sems.at[moves.remotes],
                recv_sem=moves.recv_sems.at[moves.remotes],
                device_id=moves.other,
                device_id_type=MESH,
            ),
        )
        moves.locals += 1
        moves.remotes += 1

        def start():
            for move in moves_out:
                move.start()

        def wait():
            moves_out[0].wait()
            moves_out[1].wait_send()

        pl.when(owner)(start)
        moves.to_end.append(lambda: pl.when(owner)(wait))
        moves.to_end.append(lambda: pl.when(jnp.logical_not(owner))(lambda: moves_out[1].wait_recv()))

    def finish_up():
        arrivals[1].wait_recv()
        arrivals[2].wait_recv()
        first = core == 0
        count = v.stage_up.shape[2] // block
        for s in range(2):
            pieces = []
            for at in range(count):
                if s == 0:
                    span = slice(at * block, (at + 1) * block)
                    own, peer = (ref[0, :, span] for ref in (v.stage_up, v.peer_up))
                else:
                    span = slice(at // 4 * block, (at // 4 + 1) * block)
                    own, peer = (ref[at % 4, :, span] for ref in (v.stage_up_v, v.peer_up_v))
                pieces += [jnp.where(first, own, peer), jnp.where(first, peer, own)]
            v.s_grad_up[s, :, :] = jnp.concatenate(pieces, 1)
        moves.save(v.s_grad_up, v.grad_up)

    stages = [prepare]
    stages += [functools.partial(attend_head_back, rows, head_width, scale, v, head) for head in range(heads)]
    stages += [back_qkv, qkv_part, tokens, share_up, share_out, finish_up, share_down]
    scatter.run(plan, stages)

    def mine(third, of):
        first = third * 2 * width + of * width
        return v.grad_qkv.at[:, :, pl.ds(pl.multiple_of(first, lane), width)]

    small = v.stage_qkv.at[:, :, 3 * width :]
    last = [moves.across(small, v.peer_small)]
    for third in range(3):
        source = v.stage_qkv.at[:, :, third * width : (third + 1) * width]
        moves.save(source, mine(third, core))
        last.append(moves.across(source, mine(third, core), mine(third, 1 - core)))
    last[0].wait_recv()
    for s in range(2):
        own, peer = v.stage_qkv[s, :, 3 * width :], v.peer_small[s, :, :]
        columns = own.shape[0]
        empty = jnp.zeros((lane - columns, lane), full)
        own, peer = (jnp.concatenate([value, empty], 0).T[:, :columns] for value in (own, peer))
        v.s_grad_gate[:heads, s, :] = jnp.where(core == 0, own, peer)[:heads]
        v.s_grad_gate[heads:, s, :] = jnp.where(core == 0, peer, own)[:heads]
        both = own + peer
        v.s_grad_gain_attn[s : s + 1, :] = both[heads : heads + 1]
        v.s_grad_gain_ffn[s : s + 1, :] = both[heads + 1 : heads + 2]
    moves.save(v.s_grad_gate, v.grad_gate)
    moves.save(v.s_grad_gain_attn, v.grad_gain_attn)
    moves.save(v.s_grad_gain_ffn, v.grad_gain_ffn)
    for arrival in last[1:] + [arrivals[3]]:
        arrival.wait_recv()
    moves.finish()
    scatter.finish()


def attention_back(n_docs, heads, scale, pieces, plan, inputs):
    line_size = n_docs // 4
    count, dim = inputs.h.shape
    width, wide = inputs.qkv.shape[1] // 3, inputs.full_qkv.shape[2]
    hidden = inputs.part_up.shape[2]
    rows = dim // n_docs
    block = hidden // n_docs
    splits = (False, True, False, False)
    part_qkv = ((2, dim, wide), low)
    arrays = same_as([inputs.part_up, inputs.part_out]) + [part_qkv] + same_as([inputs.part_up_v])
    results = AttentionOut(
        text_grad=(inputs.text.shape, full),
        visual_grad=(inputs.visual.shape, full),
        grad_down=((2, 2 * inputs.stage_down.shape[1], dim), full),
        grad_qkv=((2, rows, 6 * width), full),
        grad_gate=((2 * heads, 2, rows), full),
        grad_up=((2, rows, 2 * hidden), full),
        grad_out=((2, rows, dim), full),
        grad_gain_attn=((2, rows), full),
        grad_gain_ffn=((2, rows), full),
    )
    scratch = AttentionScratch(
        part_qkv=part_qkv,
        x=((count // 2, dim), low),
        q_t=((width, count), low),
        k_t=((width, count), low),
        query_grad_t=((width, count), low),
        text_grad_n=((count, width), low),
        visual_grad_n=((count, width), low),
        key_sum=((count, lane), full),
        value_sum=((count, lane), full),
        grad_wide=((count, wide), low),
        wide=((count, dim), full),
        received=((count // 2, dim), full),
        gain_sum=((2, lane, dim), full),
        stage_up=((1, rows, hidden), full),
        stage_out=((2, rows, dim), full),
        stage_qkv=((2, rows, wide), full),
        stage_up_v=((4, rows, hidden // 4), full),
        peer_up=((1, rows, hidden), full),
        peer_up_v=((4, rows, hidden // 4), full),
        peer_small=((2, rows, lane), full),
        s_grad_up=results.grad_up,
        s_grad_gate=results.grad_gate,
        s_grad_gain_attn=results.grad_gain_attn,
        s_grad_gain_ffn=results.grad_gain_ffn,
    )
    loaded = same_as(inputs[:-2])
    values = pl.pallas_call(
        functools.partial(attention_kernel, line_size, heads, scale, block, pieces, plan),
        out_shape=shapes_of(results),
        in_specs=specs_of(len(inputs), 0),
        out_specs=specs_of(len(results), 0),
        scratch_shapes=scratch_of(loaded)
        + scratch_of(scratch)
        + scatter_buffers(pieces, arrays, splits, n_docs)
        + sems((len(pieces), line_size, 11), (len(pieces), line_size, 11), 40, 16, 16),
        compiler_params=pltpu.CompilerParams(
            collective_id=2, has_side_effects=True, vmem_limit_bytes=vmem_limit
        ),
        name="attention_back_and_scatter",
    )(*inputs)
    return AttentionOut(*values)


def publish_kernel(count, *refs):
    sources, results, held = refs[:count], refs[count : 2 * count], refs[2 * count : 3 * count]
    arriving, leaving = refs[3 * count :]
    copies_in = [pltpu.make_async_copy(sources[at], held[at], arriving.at[at]) for at in range(count)]
    copies_out = [pltpu.make_async_copy(held[at], results[at], leaving.at[at]) for at in range(count)]
    for copy in copies_in:
        copy.start()
    for copy_in, copy_out in zip(copies_in, copies_out):
        copy_in.wait()
        copy_out.start()
    for copy in copies_out:
        copy.wait()


def publish(arrays):
    count = len(arrays)
    return pl.pallas_call(
        functools.partial(publish_kernel, count),
        out_shape=shapes_of(same_as(arrays)),
        in_specs=specs_of(count, 0),
        out_specs=specs_of(count, 0),
        scratch_shapes=scratch_of(same_as(arrays)) + sems(count, count),
        compiler_params=pltpu.CompilerParams(vmem_limit_bytes=vmem_limit),
        name="publish",
    )(*arrays)


def kernel_path(n_docs, heads, scale, inputs):
    made = [tuple(Piece(*each) for each in pieces) for pieces in (front_pieces, ffn_pieces, attention_pieces)]
    first = front(n_docs, heads, scale, made[0], front_plan, inputs)
    ffn_inputs = FfnIn(*(getattr(first, name) for name in FfnIn._fields))
    second = ffn_back(n_docs, heads, made[1], ffn_plan, inputs.text, inputs.visual, ffn_inputs)
    known = merged(inputs, first, second)
    attention_inputs = AttentionIn(*(getattr(known, name) for name in AttentionIn._fields))
    third = attention_back(n_docs, heads, scale, made[2], attention_plan, attention_inputs)
    results = (
        second.text_out,
        second.visual_out,
        third.text_grad,
        third.visual_grad,
        third.grad_qkv,
        third.grad_out,
        third.grad_gate,
        third.grad_up,
        third.grad_down,
        third.grad_gain_attn,
        third.grad_gain_ffn,
    )
    results = publish(results)
    return (*results[:6], jnp.transpose(results[6], (1, 2, 0)), *results[7:])


def swap(value):
    return lax.ppermute(value, core_axis, [(0, 1), (1, 0)])


def both(own):
    return jnp.concatenate([own, swap(own)], 0)


def own_sum(partial):
    rows = partial.shape[0] // 2
    return partial[:rows] + swap(partial[rows:])


def normalize_back(gradient, normed, inverse, gain):
    scaled = gradient * gain
    grad_gain = jnp.sum(gradient * normed, 0)
    grad_input = inverse * (
        scaled
        - jnp.mean(scaled, -1, keepdims=True)
        - normed * jnp.mean(scaled * normed, -1, keepdims=True)
    )
    return grad_input, grad_gain


def heads_of(values, heads):
    return values.reshape(values.shape[0], heads, -1)


def attend(queries, keys, values, valid, scale):
    scores = jnp.einsum("qhe,khe->hqk", queries, keys, preferred_element_type=full) * scale
    scores = jnp.where(valid, scores, big_negative)
    top = jnp.max(scores, -1)
    probs = jnp.where(valid, jnp.exp(scores - top[..., None]), 0.0)
    total = jnp.sum(probs, -1)
    weighted = jnp.einsum(
        "hqk,khe->qhe", probs.astype(low), values, preferred_element_type=full
    )
    return weighted / total.T[..., None], top + jnp.log(total)


def attend_back(queries, keys, values, valid, scale, log_total, grad_output, output):
    delta = jnp.sum(grad_output.astype(full) * output, -1).T
    scores = jnp.einsum("qhe,khe->hqk", queries, keys, preferred_element_type=full) * scale
    probs = jnp.where(valid, jnp.exp(scores - log_total[..., None]), 0.0)
    grad_values = jnp.einsum(
        "hqk,qhe->khe", probs.astype(low), grad_output, preferred_element_type=full
    )
    grad_probs = jnp.einsum("qhe,khe->hqk", grad_output, values, preferred_element_type=full)
    grad_scores = (probs * (grad_probs - delta[..., None])).astype(low)
    grad_queries = (
        jnp.einsum("hqk,khe->qhe", grad_scores, keys, preferred_element_type=full) * scale
    )
    grad_keys = (
        jnp.einsum("hqk,qhe->khe", grad_scores, queries, preferred_element_type=full) * scale
    )
    return grad_queries, grad_keys, grad_values


def on_device(
    n_docs,
    text_tokens,
    visual_tokens,
    text_mask,
    visual_mask,
    w_qkv,
    w_out,
    w_gate,
    w_up,
    w_down,
    gain_attn,
    gain_ffn,
    text_cotangent,
    visual_cotangent,
):
    core = lax.axis_index(core_axis)
    width = w_out.shape[2]
    all_heads = w_gate.shape[2]
    heads = all_heads // 2
    half = width // 2
    scale = (width // all_heads) ** (-0.5)
    if n_docs == 16 and w_qkv.shape[1] % row_tile == 0:
        inputs = FrontIn(
            w_qkv=w_qkv,
            w_gate=jnp.transpose(w_gate, (2, 0, 1)),
            w_up=w_up,
            gain_attn=gain_attn,
            gain_ffn=gain_ffn,
            text_mask=text_mask,
            visual_mask=visual_mask,
            text=text_tokens,
            visual=visual_tokens,
            text_dy=text_cotangent,
            visual_dy=visual_cotangent,
            w_out=w_out,
            w_down=w_down,
        )
        return kernel_path(n_docs, heads, scale, inputs)

    def own_columns(array, size, start=0):
        return lax.dynamic_slice_in_dim(array, start + core * size, size, 2)

    own_tokens = (text_tokens[0], visual_tokens[0])
    own_grads = (text_cotangent[0], visual_cotangent[0])

    def reorder(mask):
        rows = mask.shape[1] // 2
        return (
            jnp.concatenate(
                [
                    lax.dynamic_slice_in_dim(mask[0], core * rows, rows),
                    lax.dynamic_slice_in_dim(mask[0], (1 - core) * rows, rows),
                ]
            )
            > 0
        )

    valids = (reorder(text_mask), reorder(visual_mask))

    pad = lane - heads - 2
    shard = jnp.concatenate(
        [own_columns(w_qkv, half, column * width) for column in range(3)]
        + [
            own_columns(w_gate, heads),
            gain_attn[..., None],
            gain_ffn[..., None],
            jnp.zeros(w_gate.shape[:2] + (pad,), low),
        ],
        2,
    )
    tokens = tuple(both(value) for value in own_tokens)
    grads_out = tuple(both(value) for value in own_grads)
    gather = lambda array: lax.all_gather(array, docs_axis, axis=1, tiled=True)
    rows_half = lambda array: lax.dynamic_slice_in_dim(
        array, core * (array.shape[1] // 2), array.shape[1] // 2, 1
    )
    full_qkv = gather(shard)
    full_up = gather(own_columns(w_up, w_up.shape[2] // 2))
    full_out, full_down = rows_half(gather(w_out)), rows_half(gather(w_down))
    gains_attn = full_qkv[:, :, 3 * half + heads].astype(full)
    gains_ffn = full_qkv[:, :, 3 * half + heads + 1].astype(full)

    fronts = []
    for s in range(2):
        normed, inverse = normalize(tokens[s].astype(full))
        lowered = (normed * gains_attn[s]).astype(low)
        wide = dot(lowered, full_qkv[s])
        narrow = wide[:, : 3 * half].astype(low)
        gates = jax.nn.sigmoid(wide[:, 3 * half : 3 * half + heads])
        queries, keys, values = (
            heads_of(narrow[:, column * half : (column + 1) * half], heads) for column in range(3)
        )
        fronts.append((normed, inverse, lowered, gates, queries, keys, values))

    outputs, totals = {}, {}
    for s in range(2):
        for t in range(2):
            outputs[s, t], totals[s, t] = attend(
                fronts[s][4], fronts[t][5], fronts[t][6], valids[t], scale
            )

    results, tails = [], []
    for s in range(2):
        gates = fronts[s][3][..., None]
        own, cross = outputs[s, s], outputs[s, 1 - s]
        mixed = gates * own + (1.0 - gates) * cross
        mix = mixed.reshape(mixed.shape[0], -1).astype(low)
        middle = own_tokens[s].astype(full) + own_sum(dot(mix, full_out[s]))
        normed, inverse = normalize(middle)
        lowered = both((normed * gains_ffn[s]).astype(low))
        upward = dot(lowered, full_up[s])
        activated, gelu_back = jax.vjp(jax.nn.gelu, upward)
        act = activated.astype(low)
        results.append((middle + own_sum(dot(act, full_down[s]))).astype(low))
        part_down = dot_rows(act, grads_out[s]).astype(low)
        grad_up = gelu_back(dot_back(grads_out[s], full_down[s]))[0].astype(low)
        part_up = dot_rows(lowered, grad_up).astype(low)
        grad_in, part_gain = normalize_back(
            own_sum(dot_back(grad_up, full_up[s])), normed, inverse, gains_ffn[s]
        )
        grad_middle = own_grads[s].astype(full) + grad_in
        grad_branch = both(grad_middle.astype(low))
        part_out = dot_rows(mix, grad_branch).astype(low)
        grad_mix = heads_of(dot_back(grad_branch, full_out[s]), heads)
        grad_gate = (
            jnp.sum(grad_mix * (own - cross), -1) * fronts[s][3] * (1.0 - fronts[s][3])
        ).astype(low)
        grad_own = (gates * grad_mix).astype(low)
        grad_cross = ((1.0 - gates) * grad_mix).astype(low)
        tails.append(
            (grad_middle, grad_gate, grad_own, grad_cross, part_out, part_up, part_down, part_gain)
        )

    backs = {}
    for s in range(2):
        for t in range(2):
            backs[s, t] = attend_back(
                fronts[s][4],
                fronts[t][5],
                fronts[t][6],
                valids[t],
                scale,
                totals[s, t],
                tails[s][2 if s == t else 3],
                outputs[s, t],
            )

    token_grads, parts_qkv = [], []
    for s in range(2):
        normed, inverse, lowered = fronts[s][:3]
        rows = lowered.shape[0]
        grad_q = backs[s, s][0] + backs[s, 1 - s][0]
        grad_k = backs[s, s][1] + backs[1 - s, s][1]
        grad_v = backs[s, s][2] + backs[1 - s, s][2]
        grad_wide = jnp.concatenate(
            [grad.reshape(rows, -1).astype(low) for grad in (grad_q, grad_k, grad_v)]
            + [tails[s][1], jnp.zeros((rows, lane - heads), low)],
            1,
        )
        part = dot_rows(lowered, grad_wide)
        own_rows = rows // 2
        grad_in, part_gain = normalize_back(
            own_sum(dot_back(grad_wide, full_qkv[s])),
            normed[:own_rows],
            inverse[:own_rows],
            gains_attn[s],
        )
        token_grads.append((tails[s][0] + grad_in)[None])
        parts_qkv.append(
            jnp.concatenate(
                [
                    part[:, : 3 * half + heads],
                    part_gain[:, None],
                    tails[s][7][:, None],
                    part[:, 3 * half + heads + 2 :],
                ],
                1,
            ).astype(low)
        )
    part_qkv = jnp.stack(parts_qkv)
    part_out, part_up, part_down = (
        jnp.stack([tails[0][at], tails[1][at]]) for at in (4, 5, 6)
    )
    scatter = lambda array: lax.psum_scatter(
        array.astype(full), docs_axis, scatter_dimension=1, tiled=True
    )

    def columns(own):
        other = swap(own)
        first = jnp.where(core == 0, own, other)
        second = jnp.where(core == 0, other, own)
        return first, second

    def rows_both(part):
        empty = jnp.zeros_like(part)
        first = jnp.where(core == 0, part, empty)
        second = jnp.where(core == 0, empty, part)
        return lax.psum(scatter(jnp.concatenate([first, second], 1)), core_axis)

    qkv_first, qkv_second = columns(scatter(part_qkv))
    grad_qkv = jnp.concatenate(
        [
            piece[:, :, column * half : (column + 1) * half]
            for column in range(3)
            for piece in (qkv_first, qkv_second)
        ],
        2,
    )
    small = jnp.stack([qkv_first[:, :, 3 * half :], qkv_second[:, :, 3 * half :]])
    grad_up = jnp.concatenate(columns(scatter(part_up)), 2)
    grad_out, grad_down = rows_both(part_out), rows_both(part_down)
    grad_gate = jnp.concatenate([small[0, :, :, :heads], small[1, :, :, :heads]], 2)
    gains = small[0] + small[1]
    return (
        results[0][None],
        results[1][None],
        token_grads[0],
        token_grads[1],
        grad_qkv,
        grad_out,
        grad_gate,
        grad_up,
        grad_down,
        gains[:, :, heads],
        gains[:, :, heads + 1],
    )


def solution(mesh):
    rows = P(docs_axis, core_axis, None)
    weights = P(None, docs_axis, None)
    gains = P(None, docs_axis)
    in_specs = (
        (rows, rows, P(docs_axis, None), P(docs_axis, None)) + (weights,) * 5 + (gains,) * 2 + (rows,) * 2
    )
    out_specs = (rows,) * 4 + (weights,) * 5 + (gains,) * 2
    return jax.shard_map(
        functools.partial(on_device, mesh.shape[docs_axis]),
        mesh=mesh,
        in_specs=in_specs,
        out_specs=out_specs,
        check_vma=False,
    )
```

profile of v0, /device:TPU:9, one launch (start us, length us, event | category | flops | bytes accessed | tf_op | source)
XLA Modules:
  0.0 227.5 jit_solution(6442329833272687515)
XLA Ops:
  0.6 101.8 %gather_and_front.1 = (bf16[2,768,1280]{2,1,0:T(8,128)(2,1)}, bf16[1,768,1536]{2,1,0:T(8,128)(2,1)}, bf16[2,384,768]{2,1,0:T(8,128)(2,1)}, bf16[1,1536,768]{2,1,...) custom-call(bf16[2,48,2304]{2,1,0:T(8,128)(2,1)} %refs_0_.1, ...), custom_call_target="tpu_custom_call" | custom-call | tf_op jit(solution)/shard_map/gather_and_front/pallas_call | solution.py:1141
  102.5 39.3 %ffn_back_and_scatter.1 = (bf16[1,368,768]{2,1,0:T(8,128)(2,1)}, bf16[1,48,768]{2,1,0:T(8,128)(2,1)}, f32[2,96,768]{2,1,0:T(8,128)}, bf16[1,768,1536]{2,1,0:T(8,...) custom-call(bf16[1,1536,768]{2,1,0:T(8,128)(2,1)} %get-tuple-element, ...), custom_call_target="tpu_custom_call" | custom-call | tf_op jit(solution)/shard_map/ffn_back_and_scatter/pallas_call | solution.py:1512
  141.8 80.2 %attention_back_and_scatter.1 = (f32[1,368,768]{2,1,0:T(8,128)}, f32[1,48,768]{2,1,0:T(8,128)}, f32[2,192,768]{2,1,0:T(8,128)}, f32[2,48,2304]{2,1,0:T(8,128)}, ...) custom-call(bf16[832,1152]{1,0:T(8,128)(2,1)} %get-tuple-element.91., ...), custom_call_target="tpu_custom_call" | custom-call | tf_op jit(solution)/shard_map/attention_back_and_scatter/pallas_call | solution.py:1889
  222.0 5.1 %publish.1 = (bf16[1,368,768]{2,1,0:T(8,128)(2,1)}, bf16[1,48,768]{2,1,0:T(8,128)(2,1)}, f32[1,368,768]{2,1,0:T(8,128)}, f32[1,48,768]{2,1,0:T(8,128)}, f32[2,48...) custom-call(bf16[1,368,768]{2,1,0:T(8,128)(2,1)} %get-tuple-element., ...), custom_call_target="tpu_custom_call" | custom-call | tf_op jit(solution)/shard_map/publish/pallas_call | solution.py:1922
where the time goes:
time: 231 us; the launch traced here: 228 us
  Pallas kernels  226 us (98%)
    pallas_call x1, Pallas kernels, front(): pl.pallas_call(functools.partial(front_kernel, line_size, heads, scale, p...  102 us
    pallas_call x1, Pallas kernels, attention_back(): pl.pallas_call(functools.partial(attention_kernel, line_size, heads, scal...  80.2 us
    pallas_call x1, Pallas kernels, ffn_back(): pl.pallas_call(functools.partial(ffn_kernel, line_size, heads, pieces, pl...  39.3 us
    pallas_call x1, Pallas kernels, publish(): pl.pallas_call(functools.partial(publish_kernel, count), out_shape=shapes...  5.05 us

commit v1 on v0

--- a/solution.py
+++ b/solution.py
@@ -152,7 +152,6 @@
         self.place, self.pieces, self.sizes, self.splits = place, pieces, sizes, splits
         self.owns, self.outs = owns, outs
         self.send_sems, self.recv_sems, self.local_sems = send_sems, recv_sems, local_sems
-        self.sends = []
 
     def has(self, at, source_z):
         half = self.place.line_size // 2
@@ -181,7 +180,7 @@
         return pltpu.make_async_remote_copy(
             src_ref=self.mine(at, step) if own else self.block(at, source),
             dst_ref=self.block(at, source),
-            send_sem=self.send_sems.at[at, source, step],
+            send_sem=self.send_sems.at[at, step],
             recv_sem=self.recv_sems.at[at, source],
             device_id=self.place.device(step),
             device_id_type=MESH,
@@ -193,7 +192,6 @@
 
     def send(self, conditions, *which):
         when(conditions, lambda: self.copy(*which).start())
-        self.sends.append((conditions, which))
 
     def wait(self, conditions, at, source):
         when(conditions, lambda: self.copy(at, source, by_x).wait_recv())
@@ -291,9 +289,43 @@
             else:
                 stages[at]()
 
+    def sent(self, at, step, blocks):
+        piece = self.pieces[at]
+        total = self.outs[piece.array].at[piece.part, pl.ds(0, blocks * piece.rows), :]
+        pltpu.make_async_remote_copy(
+            src_ref=total,
+            dst_ref=total,
+            send_sem=self.send_sems.at[at, step],
+            recv_sem=self.recv_sems.at[at, 0],
+            device_id=self.place.device(step),
+            device_id_type=MESH,
+        ).wait_send()
+
     def finish(self):
-        for conditions, which in self.sends:
-            when(conditions, lambda: self.copy(*which).wait_send())
+        size, place = self.place.line_size, self.place
+        for at, piece in enumerate(self.pieces):
+            split = self.splits[piece.array]
+            planes = size // 2 if split else size
+            if piece.route == lines_first:
+                self.sent(at, by_x, planes * (1 + piece.flip))
+                self.sent(at, by_y, planes * (2 - piece.flip))
+            elif piece.route == planes_first:
+                self.sent(at, by_x, 1 + piece.flip)
+                self.sent(at, by_y, 2 - piece.flip)
+            elif piece.route == plane_shared:
+                for step in (by_x, by_y, crosswise):
+                    self.sent(at, step, 1)
+            chips = 4 if piece.route in (planes_first, plane_shared) else 1
+            for z in range(size):
+                for core in range(2 if split else 1):
+                    held = [source for source in range(size) if not split or source // (size // 2) == core]
+                    here = [place.z == z] + ([place.core == core] if split else [])
+                    up = chips * sum(source <= z for source in held) if z < size - 1 else 0
+                    down = chips * sum(source >= z for source in held) if z > 0 else 0
+                    if up:
+                        when(here, lambda: self.sent(at, upward, up))
+                    if down:
+                        when(here, lambda: self.sent(at, downward, down))
 
 
 class Scatter:
@@ -301,7 +333,7 @@
         self.place, self.pieces, self.splits = place, pieces, splits
         self.raws, self.parts, self.buffers = raws, parts, buffers
         self.send_sems, self.recv_sems, self.finish_rows = send_sems, recv_sems, finish
-        self.sends = []
+        self.first = arrival_offsets(pieces, place.line_size)
 
     shares = ((quads[1], 1, by_x), (quads[2], 2, by_y), (quads[3], 0, crosswise))
 
@@ -339,24 +371,31 @@
             return ref.at[self.slot(at, z_to)]
         return ref.at[self.slot(at, z_to), quad] if kind >= 3 else ref.at[0]
 
-    def copy(self, source, at, kind, z_to, step, number, quad=0):
-        arrival = kind if kind < 3 else 3 + (kind - 3) * 4 + quad
+    def arrival(self, at, kind, z_to, quad):
+        route = self.pieces[at].route
+        if route == lines_first:
+            return self.first[at] + z_to * 5 + kind
+        if kind < 3:
+            return self.first[at] + kind
+        chips = len(self.quads(at))
+        return self.first[at] + 3 + (z_to * 2 + kind - 3) * chips + quad
+
+    def copy(self, source, at, kind, z_to, step, quad=0):
         return pltpu.make_async_remote_copy(
             src_ref=source,
             dst_ref=self.landed(at, kind, z_to, quad),
-            send_sem=self.send_sems.at[at, z_to, number],
-            recv_sem=self.recv_sems.at[at, z_to, arrival],
+            send_sem=self.send_sems.at[at],
+            recv_sem=self.recv_sems.at[self.arrival(at, kind, z_to, quad)],
             device_id=self.place.device(step),
             device_id_type=MESH,
         )
 
     def arrived(self, at, kind, z_to, quad=0):
         held = self.landed(at, kind, z_to, quad)
-        self.copy(held, at, kind, z_to, by_x, 0, quad).wait_recv()
+        self.copy(held, at, kind, z_to, by_x, quad).wait_recv()
 
     def send(self, conditions, *which):
         when(conditions, lambda: self.copy(*which).start())
-        self.sends.append((conditions, which))
 
     def destination(self, step):
         size = self.place.line_size
@@ -377,17 +416,17 @@
         for number, quad in enumerate(self.quads(at)):
             source = self.raw_of(at, z_to, quad)
             up = conditions + [first, z_to > place.z]
-            self.send(up, source, at, 3, z_to, upward, number, number)
+            self.send(up, source, at, 3, z_to, upward, number)
             down = conditions + [last, z_to < place.z]
-            self.send(down, source, at, 4, z_to, downward, 4 + number, number)
+            self.send(down, source, at, 4, z_to, downward, number)
 
     def plane_raw(self, conditions, source, at, z_to):
         if self.pieces[at].flip == 0:
-            self.send(conditions, source(at, z_to, (True, True)), at, 0, z_to, by_y, 8)
-            self.send(conditions, source(at, z_to, (True, False)), at, 2, z_to, by_y, 9)
+            self.send(conditions, source(at, z_to, (True, True)), at, 0, z_to, by_y)
+            self.send(conditions, source(at, z_to, (True, False)), at, 2, z_to, by_y)
         else:
-            self.send(conditions, source(at, z_to, (True, True)), at, 0, z_to, by_x, 8)
-            self.send(conditions, source(at, z_to, (False, True)), at, 1, z_to, by_x, 9)
+            self.send(conditions, source(at, z_to, (True, True)), at, 0, z_to, by_x)
+            self.send(conditions, source(at, z_to, (False, True)), at, 1, z_to, by_x)
 
     def plane_pair(self, conditions, at, z_to):
         flip = self.pieces[at].flip
@@ -399,9 +438,9 @@
 
         when(conditions, body)
         if flip == 0:
-            self.send(conditions, held, at, 1, z_to, by_x, 10)
+            self.send(conditions, held, at, 1, z_to, by_x)
         else:
-            self.send(conditions, held, at, 2, z_to, by_y, 10)
+            self.send(conditions, held, at, 2, z_to, by_y)
 
     def pair(self, at, step):
         z_to = self.destination(step)
@@ -415,8 +454,8 @@
         first, last = z == 0, z == place.line_size - 1
         inner = jnp.logical_and(z > 0, z < place.line_size - 1)
         ways = (
-            (3, [z_to > z], [first], [z > 0], upward, 0),
-            (4, [z_to < z], [last], [z < place.line_size - 1], downward, 4),
+            (3, [z_to > z], [first], [z > 0], upward),
+            (4, [z_to < z], [last], [z < place.line_size - 1], downward),
         )
         ends = (([first], (4,)), ([last], (3,)), ([inner], (3, 4)))
         if piece.route == lines_first:
@@ -428,7 +467,7 @@
                 self.arrived(at, 2, z_to)
 
             when(conditions, wait)
-            for kind, onward, starts, passes, step_to, number in ways:
+            for kind, onward, starts, passes, step_to in ways:
                 when(conditions + onward + starts, lambda: add_rows(held, base))
 
                 def passing():
@@ -436,7 +475,7 @@
                     add_rows(held, base + [self.landed(at, kind, z_to)])
 
                 when(conditions + onward + passes, passing)
-                self.send(conditions + onward, held, at, kind, z_to, step_to, number)
+                self.send(conditions + onward, held, at, kind, z_to, step_to)
             for which, kinds in ends:
 
                 def end():
@@ -446,7 +485,7 @@
 
                 when(conditions + [z_to == z] + which, end)
             return
-        for kind, onward, _, passes, step_to, number in ways:
+        for kind, onward, _, passes, step_to in ways:
             for at_quad, quad in enumerate(self.quads(at)):
                 held = self.landed(at, kind, z_to, at_quad)
 
@@ -456,7 +495,7 @@
 
                 which = conditions + onward + passes
                 when(which, passing)
-                self.send(which, held, at, kind, z_to, step_to, number + at_quad, at_quad)
+                self.send(which, held, at, kind, z_to, step_to, at_quad)
         here = conditions + [z_to == z]
         for which, kinds in ends:
 
@@ -475,8 +514,8 @@
         if step == place.line_size - 1 and piece.route == planes_first:
             self.plane_raw(here, self.part_of, at, z_to)
         if step == place.line_size - 1 and piece.route == plane_shared:
-            for number, (quad, kind, step_to) in enumerate(self.shares):
-                self.send(here, self.part_of(at, z_to, quad), at, kind, z_to, step_to, 8 + number)
+            for quad, kind, step_to in self.shares:
+                self.send(here, self.part_of(at, z_to, quad), at, kind, z_to, step_to)
 
     def tail(self, at):
         z, piece = self.place.z, self.pieces[at]
@@ -509,9 +548,40 @@
             else:
                 stages[at]()
 
+    def sent(self, at, blocks):
+        piece = self.pieces[at]
+        total = self.raws[piece.array].at[piece.part, pl.ds(0, blocks * piece.rows), :]
+        pltpu.make_async_remote_copy(
+            src_ref=total,
+            dst_ref=total,
+            send_sem=self.send_sems.at[at],
+            recv_sem=self.recv_sems.at[0],
+            device_id=self.place.device(by_x),
+            device_id_type=MESH,
+        ).wait_send()
+
     def finish(self):
-        for conditions, which in self.sends:
-            when(conditions, lambda: self.copy(*which).wait_send())
+        size, place = self.place.line_size, self.place
+        for at, piece in enumerate(self.pieces):
+            if self.splits[piece.array]:
+                half = place.z // (size // 2) == place.core
+                when([half], lambda: self.sent(at, 3 * (size // 2) + size // 2 - 1))
+                when([jnp.logical_not(half)], lambda: self.sent(at, 4 * (size // 2)))
+            elif piece.route == lines_first:
+                self.sent(at, 4 * size - 1)
+            elif piece.route == line_only:
+                self.sent(at, size - 1)
+            else:
+                self.sent(at, 4 * (size - 1) + 3)
+
+
+def arrival_offsets(pieces, line_size):
+    offsets = [0]
+    for piece in pieces:
+        chips = 1 if piece.route == line_only else 4
+        count = 5 * line_size if piece.route == lines_first else 3 + 2 * line_size * chips
+        offsets.append(offsets[-1] + count)
+    return offsets
 
 
 class Moves:
@@ -545,21 +615,22 @@
         arrives = target if arrives is None else arrives
         return pltpu.make_async_remote_copy(src_ref=arrives, dst_ref=arrives, **sems)
 
-    def peer(self, source, target, step):
-        made = pltpu.make_async_remote_copy(
-            src_ref=source,
-            dst_ref=target,
+    def peer(self, source, target, step, arrives=None):
+        sems = dict(
             send_sem=self.send_sems.at[self.remotes],
             recv_sem=self.recv_sems.at[self.remotes],
             device_id=self.place.device(step),
             device_id_type=MESH,
         )
         self.remotes += 1
+        made = pltpu.make_async_remote_copy(src_ref=source, dst_ref=target, **sems)
         made.start()
         self.to_end.append(made.wait_send)
-        return made
+        arrives = target if arrives is None else arrives
+        return pltpu.make_async_remote_copy(src_ref=arrives, dst_ref=arrives, **sems)
 
     def finish(self):
+        assert self.locals == self.local_sems.shape[0] and self.remotes == self.send_sems.shape[0]
         for wait in self.to_end:
             wait()
 
@@ -575,10 +646,6 @@
         self.packed = ((0, text), (text, text + visual))
         self.sizes = (chunk_of(text), chunk_of(visual))
 
-    def over(self, body):
-        for s, (first, last) in enumerate(self.spans):
-            over_rows(first, last, self.sizes[s], functools.partial(body, s))
-
     def over_own(self, s, body):
         shift = self.own[s][0] - self.packed[s][0]
 
@@ -603,6 +670,12 @@
     def __init__(self, place, moves, size):
         self.place, self.moves, self.size = place, moves, size
         self.half = 4 * size
+
+    def chip(self, step=None):
+        return self.place.index(0, step in (by_y, crosswise), step in (by_x, crosswise))
+
+    def document(self, at):
+        return [slice(first, first + self.size) for first in (at * self.size, self.half + at * self.size)]
 
     def part(self, ref, at, count=1):
         return ref.at[at * self.size : (at + count) * self.size]
@@ -677,52 +750,59 @@
 
 
 front_pieces = (
-    (0, 0, 0, 48, 0, 0), (0, 1, 0, 48, 1, 0), (1, 0, 0, 16, 0, 0), (1, 0, 16, 32, 1, 0),
-    (2, 0, 0, 48, 0, 0), (2, 1, 0, 48, 1, 0), (3, 0, 0, 16, 0, 0), (3, 0, 16, 16, 1, 0),
-    (3, 0, 32, 64, 0, 1), (4, 0, 0, 48, 0, 3), (5, 0, 0, 96, 0, 2),
+    (0, 0, 0, 32, 0, 0), (0, 0, 32, 16, 1, 0), (1, 0, 0, 32, 0, 0), (1, 0, 32, 16, 1, 0),
+    (2, 0, 0, 48, 0, 0), (2, 1, 0, 48, 1, 0), (3, 0, 0, 32, 0, 0), (3, 0, 32, 16, 1, 0),
+    (3, 0, 48, 48, 1, 1), (4, 0, 0, 48, 0, 3), (5, 0, 0, 96, 0, 2), (6, 0, 0, 48, 0, 3),
+    (7, 0, 0, 48, 1, 0),
 )
 front_plan = (
-    (0, 1, 0), (5, 0, 0), (0, 9, 0), (0, 5, 0), (0, 0, 0), (2, 1, 1), (2, 0, 1), (2, 1, 2), (1, 1, 0),
-    (2, 5, 1), (3, 9, 1), (0, 2, 0), (1, 0, 1), (2, 0, 2), (1, 1, 1), (0, 10, 0), (2, 1, 3), (0, 7, 0),
-    (1, 5, 1), (3, 9, 2), (1, 1, 3), (2, 2, 1), (0, 6, 0), (2, 7, 1), (1, 0, 2), (5, 1, 0), (1, 0, 0),
-    (2, 0, 3), (1, 1, 2), (2, 7, 2), (2, 5, 2), (2, 5, 3), (0, 4, 0), (1, 0, 3), (0, 3, 0), (2, 4, 1),
-    (1, 5, 3), (2, 2, 2), (2, 6, 1), (2, 4, 2), (1, 7, 1), (0, 8, 0), (4, 0, 0), (1, 2, 0), (2, 7, 3),
-    (2, 10, 1), (5, 2, 0), (5, 3, 0), (1, 5, 0), (3, 9, 3), (2, 2, 3), (2, 3, 1), (2, 10, 2), (2, 4, 3),
-    (5, 4, 0), (5, 5, 0), (5, 6, 0), (3, 9, 4), (2, 3, 2), (1, 2, 3), (1, 4, 2), (5, 7, 0), (3, 8, 1),
-    (2, 6, 2), (5, 8, 0), (1, 4, 3), (1, 5, 2), (1, 4, 1), (1, 3, 1), (1, 4, 0), (1, 3, 0), (2, 10, 3),
-    (1, 7, 0), (4, 4, 0), (1, 2, 1), (1, 2, 2), (5, 9, 0), (5, 10, 0), (1, 3, 2), (1, 6, 0), (1, 6, 1),
-    (5, 11, 0), (3, 8, 2), (1, 7, 2), (1, 7, 3), (4, 2, 0), (5, 12, 0), (2, 3, 3), (1, 3, 3), (5, 13, 0),
-    (2, 6, 3), (5, 14, 0), (4, 5, 0), (5, 21, 0), (3, 8, 3), (4, 1, 0), (5, 16, 0), (1, 6, 3), (1, 6, 2),
-    (5, 17, 0), (5, 22, 0), (5, 15, 0), (3, 8, 4), (5, 19, 0), (4, 3, 0), (5, 18, 0), (5, 20, 0),
+    (0, 4, 0), (0, 11, 0), (5, 23, 0), (0, 1, 0), (0, 8, 0), (3, 11, 1), (2, 4, 1), (5, 25, 0), (0, 12, 0),
+    (3, 11, 2), (2, 12, 1), (0, 7, 0), (5, 0, 0), (0, 0, 0), (0, 6, 0), (2, 12, 2), (3, 11, 3), (2, 1, 1),
+    (2, 0, 1), (3, 11, 4), (5, 26, 0), (0, 5, 0), (2, 4, 2), (2, 12, 3), (0, 9, 0), (2, 0, 2), (0, 3, 0),
+    (1, 1, 0), (0, 10, 0), (2, 1, 2), (1, 12, 3), (1, 4, 2), (1, 0, 2), (1, 12, 0), (0, 2, 0), (2, 0, 3),
+    (2, 5, 1), (2, 10, 1), (1, 0, 0), (1, 12, 1), (1, 0, 1), (2, 1, 3), (1, 12, 2), (3, 9, 1), (2, 4, 3),
+    (1, 1, 2), (3, 8, 1), (4, 6, 0), (2, 5, 2), (5, 1, 0), (1, 0, 3), (1, 1, 3), (1, 1, 1), (2, 2, 1),
+    (2, 10, 2), (4, 7, 0), (5, 4, 0), (5, 5, 0), (2, 7, 1), (5, 24, 0), (1, 5, 1), (4, 0, 0), (3, 9, 2),
+    (2, 3, 1), (5, 2, 0), (5, 3, 0), (1, 5, 2), (2, 6, 1), (1, 4, 3), (2, 5, 3), (1, 2, 1), (1, 5, 0),
+    (2, 2, 2), (5, 6, 0), (5, 7, 0), (5, 8, 0), (1, 4, 0), (5, 9, 0), (1, 4, 1), (2, 7, 2), (2, 3, 2),
+    (3, 8, 2), (1, 5, 3), (1, 2, 0), (5, 10, 0), (5, 11, 0), (2, 2, 3), (1, 3, 1), (2, 3, 3), (5, 12, 0),
+    (5, 13, 0), (2, 6, 2), (2, 10, 3), (1, 2, 2), (4, 2, 0), (5, 14, 0), (1, 3, 0), (2, 7, 3), (1, 3, 2),
+    (3, 9, 3), (2, 6, 3), (1, 7, 1), (1, 2, 3), (1, 3, 3), (1, 7, 0), (1, 7, 3), (3, 8, 3), (5, 16, 0),
+    (5, 15, 0), (3, 9, 4), (1, 7, 2), (1, 6, 1), (1, 6, 2), (4, 5, 0), (1, 6, 0), (4, 1, 0), (5, 18, 0),
+    (5, 19, 0), (3, 8, 4), (5, 17, 0), (1, 6, 3), (5, 21, 0), (4, 4, 0), (5, 20, 0), (4, 3, 0), (5, 22, 0),
 )
 ffn_pieces = (
     (0, 0, 0, 48, 0, 0), (0, 0, 48, 48, 1, 0), (1, 0, 0, 96, 0, 2),
 )
 ffn_plan = (
-    (0, 1, 0), (0, 0, 0), (0, 2, 0), (0, 1, 1), (4, 2, 0), (0, 2, 1), (0, 0, 1), (0, 2, 2), (1, 0, 0),
-    (0, 0, 2), (2, 2, 0), (1, 1, 0), (4, 0, 0), (4, 1, 0), (1, 0, 1), (0, 1, 2), (2, 2, 1), (4, 10, 0),
-    (1, 1, 1), (2, 2, 2), (4, 4, 0), (4, 3, 0), (2, 0, 0), (0, 1, 3), (4, 9, 0), (2, 1, 0), (1, 0, 2),
-    (1, 1, 2), (0, 2, 3), (0, 0, 3), (4, 5, 0), (4, 13, 0), (4, 7, 0), (2, 1, 1), (4, 8, 0), (1, 1, 3),
-    (2, 0, 1), (2, 1, 2), (2, 0, 2), (4, 14, 0), (4, 6, 0), (1, 0, 3), (2, 2, 3), (4, 11, 0), (4, 12, 0),
-    (2, 1, 3), (2, 0, 3), (4, 15, 0),
+    (0, 0, 0), (0, 2, 0), (0, 1, 0), (0, 1, 1), (0, 1, 2), (0, 0, 1), (4, 2, 0), (2, 2, 0), (0, 0, 2),
+    (0, 2, 1), (4, 0, 0), (4, 1, 0), (1, 1, 0), (4, 9, 0), (2, 2, 1), (1, 0, 0), (1, 0, 1), (0, 2, 2),
+    (4, 3, 0), (0, 2, 3), (2, 2, 2), (4, 4, 0), (0, 0, 3), (1, 0, 2), (1, 1, 1), (4, 10, 0), (2, 0, 0),
+    (1, 1, 2), (0, 1, 3), (4, 5, 0), (2, 1, 0), (4, 13, 0), (4, 7, 0), (2, 0, 1), (4, 8, 0), (4, 6, 0),
+    (2, 2, 3), (2, 1, 1), (2, 1, 2), (1, 0, 3), (1, 1, 3), (4, 14, 0), (2, 0, 2), (4, 11, 0), (4, 12, 0),
+    (4, 15, 0), (2, 0, 3), (2, 1, 3),
 )
 attention_pieces = (
-    (0, 0, 0, 16, 0, 0), (0, 0, 16, 16, 1, 0), (0, 0, 32, 16, 1, 1), (1, 0, 0, 48, 0, 0),
-    (1, 1, 0, 48, 1, 0), (2, 0, 0, 48, 0, 0), (2, 1, 0, 48, 1, 0), (3, 0, 0, 48, 0, 3),
+    (0, 0, 0, 16, 0, 0), (0, 0, 16, 32, 1, 0), (1, 0, 0, 48, 0, 0), (1, 1, 0, 48, 1, 0),
+    (2, 0, 0, 32, 1, 0), (2, 0, 32, 16, 0, 0), (3, 0, 0, 48, 0, 3), (4, 0, 0, 48, 0, 3),
+    (5, 0, 0, 48, 0, 0), (5, 1, 0, 48, 1, 0),
 )
 attention_plan = (
-    (0, 1, 0), (0, 7, 0), (0, 4, 0), (0, 3, 0), (0, 0, 0), (0, 1, 1), (0, 7, 1), (0, 2, 0), (4, 0, 0),
-    (0, 0, 1), (0, 1, 2), (0, 0, 2), (4, 1, 0), (2, 7, 0), (1, 1, 0), (0, 2, 1), (1, 4, 0), (0, 3, 1),
-    (0, 4, 1), (1, 0, 0), (1, 0, 1), (4, 2, 0), (4, 3, 0), (1, 4, 1), (0, 3, 2), (0, 3, 3), (2, 2, 0),
-    (0, 2, 2), (0, 4, 2), (4, 4, 0), (0, 0, 3), (1, 1, 1), (1, 1, 2), (4, 5, 0), (1, 3, 0), (1, 4, 2),
-    (1, 3, 1), (0, 7, 2), (2, 7, 1), (1, 3, 2), (0, 1, 3), (2, 7, 2), (0, 7, 3), (4, 6, 0), (4, 7, 0),
-    (1, 3, 3), (1, 0, 2), (0, 4, 3), (2, 7, 3), (4, 8, 0), (2, 4, 0), (4, 9, 0), (0, 5, 0), (0, 6, 0),
-    (2, 0, 0), (2, 4, 1), (0, 2, 3), (1, 0, 3), (2, 1, 0), (2, 3, 0), (2, 0, 1), (1, 5, 0), (0, 6, 1),
-    (1, 6, 0), (2, 1, 1), (0, 5, 1), (2, 2, 1), (2, 3, 1), (1, 4, 3), (2, 0, 2), (2, 2, 2), (3, 7, 0),
-    (2, 1, 2), (1, 1, 3), (2, 6, 0), (2, 4, 2), (1, 5, 1), (2, 0, 3), (0, 6, 2), (2, 3, 2), (2, 2, 3),
-    (1, 6, 1), (0, 5, 2), (2, 5, 0), (2, 4, 3), (2, 5, 1), (1, 6, 2), (1, 5, 2), (0, 6, 3), (2, 3, 3),
-    (2, 6, 1), (3, 2, 0), (0, 5, 3), (4, 13, 0), (2, 1, 3), (4, 10, 0), (2, 5, 2), (2, 6, 2), (1, 5, 3),
-    (1, 6, 3), (4, 11, 0), (4, 12, 0), (2, 5, 3), (2, 6, 3),
+    (0, 1, 0), (0, 0, 0), (0, 3, 0), (0, 3, 1), (0, 1, 1), (4, 0, 0), (0, 0, 1), (4, 1, 0), (0, 2, 0),
+    (4, 2, 0), (1, 3, 0), (0, 6, 0), (0, 2, 1), (0, 2, 2), (4, 3, 0), (0, 1, 2), (2, 6, 0), (0, 3, 2),
+    (1, 1, 0), (1, 0, 0), (4, 4, 0), (4, 5, 0), (0, 2, 3), (1, 3, 1), (4, 6, 0), (4, 7, 0), (1, 2, 0),
+    (2, 1, 0), (0, 3, 3), (4, 9, 0), (2, 0, 0), (1, 2, 1), (0, 6, 1), (0, 5, 0), (0, 4, 0), (0, 0, 2),
+    (0, 0, 3), (4, 10, 0), (0, 6, 2), (4, 8, 0), (4, 12, 0), (1, 1, 1), (2, 2, 0), (1, 4, 0), (1, 0, 1),
+    (2, 3, 0), (0, 4, 1), (2, 6, 1), (4, 11, 0), (0, 7, 0), (0, 7, 1), (4, 13, 0), (4, 14, 0), (0, 9, 0),
+    (1, 5, 0), (0, 9, 1), (1, 0, 2), (1, 2, 2), (0, 6, 3), (0, 8, 0), (2, 6, 2), (1, 1, 2), (2, 3, 1),
+    (2, 7, 0), (1, 9, 0), (0, 8, 1), (2, 0, 1), (0, 4, 2), (1, 8, 0), (0, 5, 1), (2, 4, 0), (0, 9, 2),
+    (2, 0, 2), (0, 7, 2), (0, 8, 2), (1, 4, 1), (1, 0, 3), (0, 5, 2), (2, 7, 1), (1, 9, 1), (0, 1, 3),
+    (1, 8, 1), (1, 4, 2), (1, 5, 1), (2, 7, 2), (0, 8, 3), (2, 9, 0), (2, 6, 3), (2, 1, 1), (2, 2, 1),
+    (1, 3, 2), (1, 3, 3), (1, 8, 2), (2, 1, 2), (1, 1, 3), (2, 9, 1), (2, 8, 0), (0, 4, 3), (0, 7, 3),
+    (2, 5, 0), (1, 9, 2), (1, 2, 3), (0, 5, 3), (1, 5, 2), (2, 8, 1), (1, 8, 3), (2, 5, 1), (2, 4, 1),
+    (2, 8, 2), (2, 3, 2), (3, 6, 0), (2, 0, 3), (4, 18, 0), (2, 2, 2), (0, 9, 3), (1, 4, 3), (2, 1, 3),
+    (4, 15, 0), (2, 9, 2), (2, 4, 2), (2, 7, 3), (1, 5, 3), (2, 2, 3), (2, 5, 2), (1, 9, 3), (2, 3, 3),
+    (4, 17, 0), (2, 4, 3), (2, 8, 3), (3, 7, 0), (4, 16, 0), (2, 9, 3), (2, 5, 3),
 )
 
 
@@ -749,7 +829,10 @@
     full_down: object
     full_up_v: object
     full_down_v: object
+    full_qkv_v: object
+    full_small_v: object
     h: object
+    h_v: object
     qkv: object
     gates_t: object
     text_t: object
@@ -773,6 +856,7 @@
 
 class FrontKept(NamedTuple):
     s_h: object
+    s_h_v: object
     s_qkv: object
     s_gates_t: object
     s_text_t: object
@@ -795,15 +879,29 @@
 
 
 class FrontScratch(NamedTuple):
+    shard_qkv: object
+    shard_gate: object
+    shard_up: object
+    shard_attn: object
+    shard_ffn: object
+    shard_text_mask: object
+    shard_visual_mask: object
     own_qkv: object
+    own_qkv_v: object
+    own_small_v: object
     own_up: object
     own_up_v: object
     s_w_qkv: object
+    s_w_qkv_v: object
+    s_w_small_v: object
     s_w_up: object
     s_w_up_v: object
     s_w_out: object
     x: object
+    x_v: object
     wide: object
+    qkv_v: object
+    landing_qkv: object
     received: object
     gate_rows: object
     q_t: object
@@ -813,27 +911,39 @@
 
 def prepare_shards(v, core, heads):
     first = core == 0
-    rows = v.w_qkv.shape[1]
-    third = v.w_qkv.shape[2] // 3
+    rows = v.shard_qkv.shape[1]
+    third = v.shard_qkv.shape[2] // 3
     half = third // 2
     for s in range(2):
-        for at in range(3):
-            columns = [v.w_qkv[s, :, at * third + way * half : at * third + (way + 1) * half] for way in (0, 1)]
-            v.own_qkv[s, :, at * half : (at + 1) * half] = jnp.where(first, *columns)
-        gate = v.w_gate[:, s, :].astype(full)
+        for pair in range(half // lane):
+            for at in range(3):
+                start = at * third + pair * lane
+                columns = [v.shard_qkv[s, :, start + way * half : start + way * half + lane] for way in (0, 1)]
+                chosen = jnp.where(first, *columns)
+                if s == 0:
+                    to = (3 * pair + at) * lane
+                    v.own_qkv[0, :, to : to + lane] = chosen
+                else:
+                    v.own_qkv_v[pair, :, at * lane : (at + 1) * lane] = chosen
+        gate = v.shard_gate[:, s, :].astype(full)
         gate = jnp.where(first, gate[:heads], gate[heads:])
-        gains = [ref[s : s + 1, :].astype(full) for ref in (v.gain_attn, v.gain_ffn)]
+        gains = [ref[s : s + 1, :].astype(full) for ref in (v.shard_attn, v.shard_ffn)]
         small = jnp.concatenate([gate, *gains, jnp.zeros((lane - heads - 2, rows), full)], 0)
         small = jnp.concatenate([small, jnp.zeros((lane, lane - rows), full)], 1).T[:rows]
-        v.own_qkv[s, :, 3 * half :] = small.astype(low)
+        if s == 0:
+            v.own_qkv[0, :, 3 * half :] = small.astype(low)
+        else:
+            v.own_small_v[0, :, :] = small.astype(low)
+    for pair in range(half // lane, 4):
+        v.own_qkv_v[pair, :, :] = jnp.zeros(v.own_qkv_v.shape[1:], low)
 
 
 def prepare_hidden(v, core, block):
     first = core == 0
     pieces = []
     for s in range(2):
-        for start in range(0, v.w_up.shape[2], 2 * block):
-            ways = [v.w_up[s, :, start + way * block : start + (way + 1) * block].astype(full) for way in (0, 1)]
+        for start in range(0, v.shard_up.shape[2], 2 * block):
+            ways = [v.shard_up[s, :, start + way * block : start + (way + 1) * block].astype(full) for way in (0, 1)]
             pieces.append(jnp.where(first, *ways))
     count = len(pieces) // 2
     v.own_up[0, :, :] = jnp.concatenate(pieces[:count], 1).astype(low)
@@ -843,7 +953,7 @@
 
 def prepare_bias(v, core):
     pieces = []
-    for ref in (v.text_mask, v.visual_mask):
+    for ref in (v.shard_text_mask, v.shard_visual_mask):
         mask = ref[...].astype(full)
         half = mask.shape[1] // 2
         swapped = jnp.concatenate([mask[:, half:], mask[:, :half]], 1)
@@ -853,10 +963,9 @@
 
 
 def attend_head(rows, head_width, v, number):
-    width = v.s_qkv.shape[1] // 3
     pair = 2 * head_width
     at, odd = number // 2, number % 2
-    keys = v.s_qkv[:, width + at * pair : width + (at + 1) * pair]
+    keys = v.s_qkv[:, (3 * at + 1) * pair : (3 * at + 2) * pair]
     bias = v.s_bias[:, 0:1]
     head = slice(number * head_width, (number + 1) * head_width)
     for first, last in query_spans(rows.count):
@@ -883,7 +992,7 @@
     place = Place(line_size)
     core = place.core
     rows = Rows(v.text.shape[1], v.visual.shape[1])
-    shard, block = v.w_qkv.shape[1], v.w_down.shape[1] // 2
+    shard, block = v.shard_qkv.shape[1], v.w_down.shape[1] // 2
     owns = (
         (v.own_qkv, 0),
         (v.own_up, 0),
@@ -891,14 +1000,19 @@
         (v.w_down, core * block),
         (v.own_up_v, 0),
         (v.w_down.at[pl.ds(1, 1)], core * block),
+        (v.own_qkv_v, 0),
+        (v.own_small_v, 0),
     )
     gather = Gather(
         place,
         pieces,
-        (shard, shard, shard, block, shard, block),
-        (False, False, True, False, False, False),
+        (shard, shard, shard, block, shard, block, shard, shard),
+        (False, False, True, False, False, False, False, False),
         owns,
-        (v.s_w_qkv, v.s_w_up, v.s_w_out, v.full_down, v.s_w_up_v, v.full_down_v),
+        (
+            v.s_w_qkv, v.s_w_up, v.s_w_out, v.full_down, v.s_w_up_v, v.full_down_v, v.s_w_qkv_v,
+            v.s_w_small_v,
+        ),
         *refs[:3],
     )
     moves = Moves(place, *refs[3:])
@@ -908,62 +1022,110 @@
     arrivals = {}
 
     place.greet()
+    shards = [moves.local(source, target) for source, target in zip(groups[0][:7], groups[3][:7])]
+    shards[0].wait()
+    shards[1].wait()
+    shards[3].wait()
+    shards[4].wait()
     prepare_shards(v, core, heads)
     place.meet()
     plane = Plane(place, moves, rows.visual)
-    loads, swaps = [], []
-    for s, source in enumerate((v.text, v.visual)):
-        loads.append(moves.local(source.at[0], v.x.at[slice(*rows.own[s])]))
-        swaps.append(moves.across(source.at[0], v.x.at[slice(*rows.other[s])]))
-    loads.append(moves.local(v.text_dy.at[0], v.s_dy.at[slice(*rows.own[0])]))
-    loads.append(moves.local(v.visual_dy.at[0], plane.part(v.s_dy_v, 0)))
-    swaps.append(moves.across(v.text_dy.at[0], v.s_dy.at[slice(*rows.other[0])]))
+    loads = [
+        moves.local(v.text.at[0], v.x.at[slice(*rows.own[0])]),
+        moves.local(v.visual.at[0], plane.part(v.x_v, 0)),
+        moves.local(v.text_dy.at[0], v.s_dy.at[slice(*rows.own[0])]),
+        moves.local(v.visual_dy.at[0], plane.part(v.s_dy_v, 0)),
+    ]
+    swaps = [
+        moves.across(v.text.at[0], v.x.at[slice(*rows.other[0])]),
+        moves.across(v.text_dy.at[0], v.s_dy.at[slice(*rows.other[0])]),
+    ]
 
     def prepare():
+        shards[2].wait()
         prepare_hidden(v, core, block)
 
     def norm():
+        shards[5].wait()
+        shards[6].wait()
         prepare_bias(v, core)
         moves.save(v.s_bias, v.bias)
-        for s in range(2):
-            loads[s].wait()
-            swaps[s].wait_recv()
-
-        def body(s, piece):
+        loads[0].wait()
+        swaps[0].wait_recv()
+
+        def body(piece):
             v.wide[piece, :] = normalize(v.x[piece, :].astype(full))[0]
 
-        rows.over(body)
-
-    def lower():
+        over_rows(0, rows.split, rows.sizes[0], body)
+
+    def gains_of(s, small):
+        v.s_gains[s, :, :] = small.astype(full).T[heads : heads + 2]
+
+    def lower_text():
         moves.save(v.s_w_qkv, v.full_qkv)
-        for s in range(2):
-            small = v.s_w_qkv[s, :, 3 * width :].astype(full).T
-            v.s_gains[s, :, :] = small[heads : heads + 2]
-
-        def body(s, piece):
-            v.s_h[piece, :] = (v.wide[piece, :] * v.s_gains[s, 0:1, :]).astype(low)
-
-        rows.over(body)
+        gains_of(0, v.s_w_qkv[0, :, 3 * width :])
+
+        def body(piece):
+            v.s_h[piece, :] = (v.wide[piece, :] * v.s_gains[0, 0:1, :]).astype(low)
+
+        over_rows(0, rows.split, rows.sizes[0], body)
+        moves.save(v.s_h, v.h)
+
+    def project_text():
+        even = 3 * width // 256 * 256
+
+        def columns(piece):
+            v.s_qkv[: rows.split, piece] = dot(v.s_h[...], v.s_w_qkv[0, :, piece]).astype(low)
+
+        over_columns(0, even, 256, columns)
+        rest = dot(v.s_h[...], v.s_w_qkv[0, :, even:])
+        v.s_qkv[: rows.split, even:] = rest[:, : 3 * width - even].astype(low)
+        v.gate_rows[: rows.split, :] = rest[:, 3 * width - even :]
+
+    def spread_x():
+        arrivals[6] = plane.spread(v.visual.at[0], v.x_v)
+
+    def pass_x():
+        arrivals[7] = plane.pass_on(v.x_v, arrivals[6][1])
+
+    def lower_visual():
+        moves.save(v.s_w_small_v, v.full_small_v)
+        loads[1].wait()
+        arrivals[6][0].wait_recv()
+        arrivals[7].wait_recv()
+        gains_of(1, v.s_w_small_v[0, :, :])
+        v.s_h_v[...] = (normalize(v.x_v[...].astype(full))[0] * v.s_gains[1, 0:1, :]).astype(low)
+        moves.save(v.s_h_v, v.h_v)
+        for at, piece in enumerate(plane.document(0)):
+            first = rows.split + at * rows.visual
+            v.gate_rows[first : first + rows.visual, :] = dot(v.s_h_v[piece, :], v.s_w_small_v[0, :, :])
+
+    def project_visual():
+        moves.save(v.s_w_qkv_v, v.full_qkv_v)
+        v.qkv_v[...] = dot(v.s_h_v[...], v.s_w_qkv_v[0, :, :]).astype(low)
+        landing = lambda chip, half: v.landing_qkv.at[chip, half * rows.visual : (half + 1) * rows.visual]
+        arrivals[8] = []
+        for half, piece in enumerate(plane.document(0)):
+            v.landing_qkv[plane.chip(), half * rows.visual : (half + 1) * rows.visual, :] = v.qkv_v[piece, :]
+        for at, step in enumerate(plane.steps):
+            for half, piece in enumerate(plane.document(1 + at)):
+                source = v.qkv_v.at[piece]
+                arrivals[8].append(
+                    moves.peer(source, landing(plane.chip(), half), step, landing(plane.chip(step), half))
+                )
+
+    def receive_visual():
+        for arrival in arrivals[8]:
+            arrival.wait_recv()
+        pair = 3 * lane
+        for at in range(heads // 2):
+            v.s_qkv[rows.split :, at * pair : (at + 1) * pair] = v.landing_qkv[at, :, :]
+            span = slice(at * lane, (at + 1) * lane)
+            queries = v.s_qkv[:, at * pair : at * pair + lane] * jnp.asarray(scale, low)
+            v.q_t[span, :] = queries.T
+            v.v_t[span, :] = v.s_qkv[:, at * pair + 2 * lane : (at + 1) * pair].T
+        v.s_gates_t[...] = jax.nn.sigmoid(v.gate_rows[...].T[:8, :])
         moves.save(v.s_gains, v.gains)
-        moves.save(v.s_h, v.h)
-
-    def project(s):
-        first, last = rows.spans[s]
-        even = 3 * width // 256 * 256
-
-        def columns(piece):
-            v.s_qkv[first:last, piece] = dot(v.s_h[first:last, :], v.s_w_qkv[s, :, piece]).astype(low)
-
-        over_columns(0, even, 256, columns)
-        rest = dot(v.s_h[first:last, :], v.s_w_qkv[s, :, even:])
-        v.s_qkv[first:last, even:] = rest[:, : 3 * width - even].astype(low)
-        v.gate_rows[first:last, :] = rest[:, 3 * width - even :]
-
-    def project_visual():
-        project(1)
-        v.s_gates_t[...] = jax.nn.sigmoid(v.gate_rows[...].T[:8, :])
-        v.q_t[...] = (v.s_qkv[:, :width] * jnp.asarray(scale, low)).T
-        v.v_t[...] = v.s_qkv[:, 2 * width :].T
         moves.save(v.s_qkv, v.qkv)
         moves.save(v.s_gates_t, v.gates_t)
 
@@ -998,25 +1160,26 @@
     def pass_dy():
         arrivals[3] = plane.pass_on(v.s_dy_v, arrivals[2][1])
 
-    def middle_rows(s, ref, start):
+    def middle_rows(s, x, ref, start):
         arrivals[0][s].wait_recv()
 
         def body(piece, packed):
-            value = v.x[piece, :].astype(full) + v.wide[piece, :] + v.received[packed, :]
+            to = pl.ds(pl.multiple_of(packed.start - start, row_tile), packed.size)
+            value = x[to, :].astype(full) + v.wide[piece, :] + v.received[packed, :]
             v.s_middle[packed, :] = value
-            to = pl.ds(pl.multiple_of(packed.start - start, row_tile), packed.size)
             ref[to, :] = (normalize(value)[0] * v.s_gains[s, 1:2, :]).astype(low)
 
         rows.over_own(s, body)
+        packed = slice(*rows.packed[s])
+        moves.save(v.s_middle.at[packed], v.middle.at[packed])
 
     def middle_visual():
-        middle_rows(1, v.s_hm_v, rows.packed[1][0])
+        middle_rows(1, v.x_v, v.s_hm_v, rows.packed[1][0])
         arrivals[4] = plane.spread(plane.part(v.s_hm_v, 0), v.s_hm_v)
 
     def middle_text():
-        middle_rows(0, v.s_hm, 0)
+        middle_rows(0, v.x, v.s_hm, 0)
         arrivals[1] = rows.swap_own(moves, v.s_hm, 0)
-        moves.save(v.s_middle, v.middle)
 
     def pass_hm():
         arrivals[5] = plane.pass_on(v.s_hm_v, arrivals[4][1])
@@ -1035,7 +1198,7 @@
         moves.save(v.s_w_up, v.full_up)
         arrivals[1].wait_recv()
         loads[2].wait()
-        swaps[2].wait_recv()
+        swaps[1].wait_recv()
         moves.save(v.s_hm, v.hm)
         moves.save(v.s_dy, v.dy)
         up_part(v.s_hm, v.s_w_up, v.s_act, v.s_slope, 0, hidden // 2)
@@ -1074,10 +1237,10 @@
         down_part(v.s_act_v, v.s_dy_v, v.s_part_down_v)
         moves.save(v.s_part_down_v, v.part_down_v)
 
-    stages = [prepare, norm, lower, functools.partial(project, 0), project_visual]
+    stages = [prepare, norm, lower_text, project_text, lower_visual, project_visual, receive_visual]
     stages += [functools.partial(attend_head, rows, head_width, v, head) for head in range(heads)]
     stages += [mix, branch, middle_visual, middle_text, pass_hm, up_first, up_second, up_visual]
-    stages += [down_text, down_visual, spread_dy, pass_dy]
+    stages += [down_text, down_visual, spread_dy, pass_dy, spread_x, pass_x]
     gather.run(plan, stages)
     moves.finish()
     gather.finish()
@@ -1092,7 +1255,8 @@
     wide = 3 * width + lane
     shard = inputs.w_qkv.shape[1]
     kept = FrontKept(
-        s_h=((count, dim), low),
+        s_h=((text, dim), low),
+        s_h_v=((plane, dim), low),
         s_qkv=((count, 3 * width), low),
         s_gates_t=((8, count), full),
         s_text_t=((width, count), full),
@@ -1114,23 +1278,40 @@
         s_bias=((count, lane), full),
     )
     weights = (
-        ((2, dim, wide), low),
+        ((1, dim, wide), low),
         ((1, dim, hidden), low),
         ((2, width, dim), low),
         ((1, hidden, dim), low),
         ((1, dim, hidden // 4), low),
         ((1, hidden // 4, dim), low),
-    )
+        ((1, dim, 3 * lane), low),
+        ((1, dim, lane), low),
+    )
+    shards = same_as(inputs[:7])
     scratch = FrontScratch(
-        own_qkv=((2, shard, wide), low),
+        shard_qkv=shards[0],
+        shard_gate=shards[1],
+        shard_up=shards[2],
+        shard_attn=shards[3],
+        shard_ffn=shards[4],
+        shard_text_mask=shards[5],
+        shard_visual_mask=shards[6],
+        own_qkv=((1, shard, wide), low),
+        own_qkv_v=((4, shard, 3 * lane), low),
+        own_small_v=((1, shard, lane), low),
         own_up=((1, shard, hidden), low),
         own_up_v=((4, shard, hidden // 4), low),
         s_w_qkv=weights[0],
+        s_w_qkv_v=weights[6],
+        s_w_small_v=weights[7],
         s_w_up=weights[1],
         s_w_up_v=weights[4],
         s_w_out=weights[2],
-        x=((count, dim), low),
+        x=((text, dim), low),
+        x_v=((plane, dim), low),
         wide=((count, dim), full),
+        qkv_v=((plane, 3 * lane), low),
+        landing_qkv=((4, 2 * inputs.visual.shape[1], 3 * lane), low),
         received=((count // 2, dim), full),
         gate_rows=((count, lane), full),
         q_t=((width, count), low),
@@ -1141,11 +1322,11 @@
     values = pl.pallas_call(
         functools.partial(front_kernel, line_size, heads, scale, pieces, plan),
         out_shape=shapes_of(results),
-        in_specs=specs_of(len(inputs), 7),
+        in_specs=specs_of(len(inputs), 0),
         out_specs=specs_of(len(results), 0),
         scratch_shapes=scratch_of(kept)
         + scratch_of(scratch)
-        + sems((len(pieces), n_docs, 5), (len(pieces), n_docs), len(pieces), 40, 24, 24),
+        + sems((len(pieces), 5), (len(pieces), n_docs), len(pieces), 39, 26, 26),
         compiler_params=pltpu.CompilerParams(
             collective_id=0, has_side_effects=True, vmem_limit_bytes=vmem_limit
         ),
@@ -1517,7 +1698,7 @@
         scratch_shapes=scratch_of(loaded)
         + scratch_of(scratch)
         + scatter_buffers(pieces, same_as([inputs.part_down, inputs.part_down_v]), (False, False), n_docs)
-        + sems((len(pieces), line_size, 11), (len(pieces), line_size, 11), 40, 24, 24),
+        + sems(len(pieces), arrival_offsets(pieces, line_size)[-1], 32, 12, 12),
         compiler_params=pltpu.CompilerParams(
             collective_id=1, has_side_effects=True, vmem_limit_bytes=vmem_limit
         ),
@@ -1539,7 +1720,10 @@
     part_out: object
     gate_grad_t: object
     full_qkv: object
+    full_qkv_v: object
+    full_small_v: object
     h: object
+    h_v: object
     grad_middle: object
     gains: object
     gain_part: object
@@ -1561,7 +1745,10 @@
     s_part_out: object
     s_gate_grad_t: object
     s_full_qkv: object
+    s_full_qkv_v: object
+    s_full_small_v: object
     s_h: object
+    s_h_v: object
     s_grad_middle: object
     s_gains: object
     s_gain_part: object
@@ -1582,6 +1769,8 @@
 
 class AttentionScratch(NamedTuple):
     part_qkv: object
+    part_qkv_v: object
+    part_small: object
     x: object
     q_t: object
     k_t: object
@@ -1593,11 +1782,20 @@
     grad_wide: object
     wide: object
     received: object
+    grad_v: object
+    wide_v: object
+    received_v: object
+    outgoing_v: object
+    landing_v: object
     gain_sum: object
+    gains_row: object
     stage_up: object
     stage_out: object
     stage_qkv: object
     stage_up_v: object
+    stage_qkv_v: object
+    stage_small: object
+    own_qkv: object
     peer_up: object
     peer_up_v: object
     peer_small: object
@@ -1608,10 +1806,10 @@
 
 
 def attend_head_back(rows, head_width, scale, v, number):
-    width = v.s_qkv.shape[1] // 3
     pair = 2 * head_width
     at, odd = number // 2, number % 2
-    columns = [slice(third * width + at * pair, third * width + (at + 1) * pair) for third in range(3)]
+    columns = [slice((3 * at + third) * pair, (3 * at + third + 1) * pair) for third in range(3)]
+    wide = slice(at * pair, (at + 1) * pair)
     keys, values = v.s_qkv[:, columns[1]], v.s_qkv[:, columns[2]]
     if not odd:
         v.key_sum[...] = jnp.zeros_like(v.key_sum)
@@ -1635,7 +1833,7 @@
             probs = jnp.exp(scores[start:stop] - v.s_logs[row : row + 1, first:last])
             grad_probs = dot(values[start:stop], head_wide(out_grad, odd))
             grad_scores = (probs * (grad_probs - delta)).astype(low)
-            natural = jnp.where(mine, grad[first:last, columns[0]], 0)
+            natural = jnp.where(mine, grad[first:last, wide], 0)
             v.value_sum[start:stop, :] += dot(probs.astype(low), natural)
             v.key_sum[start:stop, :] += dot(grad_scores, queries)
             pieces.append(grad_scores)
@@ -1643,6 +1841,7 @@
             dot(v.k_t[head, :], jnp.concatenate(pieces, 0)) * scale
         ).astype(low)
     if odd:
+        v.grad_wide[:, columns[0]] = v.query_grad_t[wide, :].T
         v.grad_wide[:, columns[1]] = v.key_sum[...].astype(low)
         v.grad_wide[:, columns[2]] = v.value_sum[...].astype(low)
 
@@ -1663,21 +1862,20 @@
     width = v.qkv.shape[1] // 3
     head_width = width // heads
     dim = v.h.shape[1]
-    stages_of = (v.stage_up, v.stage_out, v.stage_qkv)
+    stages_of = (v.stage_up, v.stage_out, v.stage_qkv, v.stage_up_v, v.stage_qkv_v, v.stage_small)
     arrivals = {}
+    plane = Plane(place, moves, rows.visual)
 
     def finish_rows(piece, total, quad=quads[0]):
-        if piece.route == plane_shared:
-            add_rows(v.stage_up_v.at[place.index(0, *quad)], total, piece.first)
-        else:
-            add_rows(stages_of[piece.array].at[piece.part], total, piece.first)
+        part = place.index(0, *quad) if piece.route == plane_shared else piece.part
+        add_rows(stages_of[piece.array].at[part], total, piece.first)
 
     scatter = Scatter(
         place,
         pieces,
-        (False, True, False, False),
-        (v.part_up, v.part_out, v.part_qkv, v.part_up_v),
-        (v.s_part_up, v.s_part_out, v.part_qkv, v.s_part_up_v),
+        (False, True, False, False, False, False),
+        (v.part_up, v.part_out, v.part_qkv, v.part_up_v, v.part_qkv_v, v.part_small),
+        (v.s_part_up, v.s_part_out, v.part_qkv, v.s_part_up_v, v.part_qkv_v, v.part_small),
         buffers,
         send_sems,
         recv_sems,
@@ -1693,58 +1891,117 @@
     def prepare():
         for load in loads[:7]:
             load.wait()
-        v.q_t[...] = (v.s_qkv[:, :width] * jnp.asarray(scale, low)).T
-        v.k_t[...] = v.s_qkv[:, width : 2 * width].T
+        for at in range(heads // 2):
+            span, first = slice(at * lane, (at + 1) * lane), 3 * at * lane
+            v.q_t[span, :] = (v.s_qkv[:, first : first + lane] * jnp.asarray(scale, low)).T
+            v.k_t[span, :] = v.s_qkv[:, first + lane : first + 2 * lane].T
         v.text_grad_n[...] = v.s_text_grad_t[...].T
         v.visual_grad_n[...] = v.s_visual_grad_t[...].T
         loads.part_up.wait()
         loads.part_up_v.wait()
         loads.part_out.wait()
 
-    def back_qkv():
+    def send_visual():
         loads.gate_grad_t.wait()
+        empty = jnp.zeros((lane - 8, rows.count), full)
+        v.grad_wide[:, 3 * width : 3 * width + lane] = (
+            jnp.concatenate([v.s_gate_grad_t[...], empty], 0).T.astype(low)
+        )
+        v.grad_wide[:, 3 * width + lane :] = jnp.zeros((rows.count, 2 * lane), low)
+        arrivals[4] = []
+        pair = 3 * lane
+        for half, piece in enumerate(plane.document(0)):
+            first = rows.split + half * rows.visual
+            span = slice(first, first + rows.visual)
+            of = lambda step: v.grad_wide.at[span, pl.ds(pl.multiple_of(plane.chip(step) * pair, lane), pair)]
+            arrivals[4].append(moves.local(of(None), v.grad_v.at[piece]).wait)
+            for at, step in enumerate(plane.steps):
+                target = v.grad_v.at[plane.document(1 + at)[half]]
+                arrivals[4].append(moves.peer(of(step), target, step).wait_recv)
+
+    def back_text():
         loads.full_qkv.wait()
-        v.grad_wide[:, :width] = v.query_grad_t[...].T
-        empty = jnp.zeros((lane - 8, rows.count), full)
-        v.grad_wide[:, 3 * width :] = jnp.concatenate([v.s_gate_grad_t[...], empty], 0).T.astype(low)
-        for s, (first, last) in enumerate(rows.spans):
-
-            def columns(piece):
-                v.wide[first:last, piece] = dot_back(v.grad_wide[first:last, :], v.s_full_qkv[s, piece, :])
-
-            over_columns(0, dim, 256, columns)
-        arrivals[0] = rows.swap_parts(moves, v.wide, v.received)
-
-    def qkv_part():
+
+        def columns(piece):
+            grad = v.grad_wide[: rows.split, : 3 * width + lane]
+            v.wide[:, piece] = dot_back(grad, v.s_full_qkv[0, piece, :])
+
+        over_columns(0, dim, 256, columns)
+        arrivals[0] = rows.swap_parts(moves, v.wide, v.received, (0,))[0]
+
+    def text_part():
         loads.h.wait()
-        for s, (first, last) in enumerate(rows.spans):
-
-            def columns(piece):
-                v.part_qkv[s, piece, :] = dot_rows(v.s_h[first:last, piece], v.grad_wide[first:last, :]).astype(low)
-
-            over_columns(0, dim, 256, columns)
-
-    def tokens():
+
+        def columns(piece):
+            grad = dot_rows(v.s_h[:, piece], v.grad_wide[: rows.split, : 3 * width + lane])
+            v.part_qkv[0, piece, :] = grad[:, : 3 * width].astype(low)
+            v.gain_sum[0, piece, :] = grad[:, 3 * width :]
+
+        over_columns(0, dim, 256, columns)
+
+    def back_visual():
+        loads.full_qkv_v.wait()
+        loads.full_small_v.wait()
+        for wait in arrivals[4]:
+            wait()
+        v.wide_v[...] = dot_back(v.grad_v[...], v.s_full_qkv_v[0, :, :])
+        for half, piece in enumerate(plane.document(0)):
+            first = rows.split + half * rows.visual
+            small = v.grad_wide[first : first + rows.visual, 3 * width : 3 * width + lane]
+            v.wide_v[piece, :] += dot_back(small, v.s_full_small_v[0, :, :])
+        arrivals[5] = plane.halve(v.wide_v, v.received_v)
+
+    def visual_part():
+        loads.h_v.wait()
+
+        def columns(piece):
+            v.part_qkv_v[0, piece, :] = dot_rows(v.s_h_v[:, piece], v.grad_v[...]).astype(low)
+
+        over_columns(0, dim, 256, columns)
+        total = 0.0
+        for half, piece in enumerate(plane.document(0)):
+            first = rows.split + half * rows.visual
+            small = v.grad_wide[first : first + rows.visual, 3 * width : 3 * width + lane]
+            total = total + dot_rows(v.s_h_v[piece, :], small)
+        v.gain_sum[1, :, :] = total
+
+    def share_visual():
+        arrivals[5].wait_recv()
+        arrivals[6] = plane.share(v.wide_v, v.received_v, v.outgoing_v, v.landing_v)
+
+    def token_rows(s, packed, grad):
+        normed, inverse = normalize(v.x[packed, :].astype(full))
+        v.gains_row[s, heads : heads + 1, :] += jnp.sum(grad * normed, 0, keepdims=True)
+        v.s_grad_middle[packed, :] += norm_back(grad, normed, inverse, v.s_gains[s, 0:1, :])
+
+    def small_part(s):
+        small = v.gain_sum[s, :, :] + v.gains_row[s, :, :].T
+        v.part_small[s, :, :] = small.astype(low)
+        ref = (v.text_grad, v.visual_grad)[s]
+        moves.save(v.s_grad_middle.at[slice(*rows.packed[s])], ref.at[0])
+
+    def tokens_text():
         loads.grad_middle.wait()
         loads.gains.wait()
         loads.gain_part.wait()
+        v.gains_row[...] = jnp.zeros_like(v.gains_row)
         for s in range(2):
-            loads[17 + s].wait()
-            arrivals[0][s].wait_recv()
-            v.gain_sum[s, :, :] = jnp.zeros((lane, dim), full)
-            v.gain_sum[s, heads + 1 : heads + 2, :] = v.s_gain_part[s, 0:1, :]
-
-            def body(piece, packed):
-                normed, inverse = normalize(v.x[packed, :].astype(full))
-                grad = v.wide[piece, :] + v.received[packed, :]
-                v.gain_sum[s, heads : heads + 1, :] += jnp.sum(grad * normed, 0, keepdims=True)
-                v.s_grad_middle[packed, :] += norm_back(grad, normed, inverse, v.s_gains[s, 0:1, :])
-
-            rows.over_own(s, body)
-            small = v.part_qkv[s, :, 3 * width :].astype(full) + v.gain_sum[s, :, :].T
-            v.part_qkv[s, :, 3 * width :] = small.astype(low)
-            ref = (v.text_grad, v.visual_grad)[s]
-            moves.save(v.s_grad_middle.at[slice(*rows.packed[s])], ref.at[0])
+            loads[-2 + s].wait()
+            v.gains_row[s, heads + 1 : heads + 2, :] = v.s_gain_part[s, 0:1, :]
+        arrivals[0].wait_recv()
+
+        def body(piece, packed):
+            token_rows(0, packed, v.wide[piece, :] + v.received[packed, :])
+
+        rows.over_own(0, body)
+        small_part(0)
+
+    def tokens_visual():
+        for arrival in arrivals[6]:
+            arrival.wait_recv()
+        grad = plane.total(v.wide_v, v.received_v, v.landing_v)
+        token_rows(1, slice(*rows.packed[1]), grad)
+        small_part(1)
 
     def share_down():
         loads.stage_down.wait()
@@ -1805,22 +2062,26 @@
 
     stages = [prepare]
     stages += [functools.partial(attend_head_back, rows, head_width, scale, v, head) for head in range(heads)]
-    stages += [back_qkv, qkv_part, tokens, share_up, share_out, finish_up, share_down]
+    stages += [send_visual, back_text, text_part, back_visual, visual_part, share_visual]
+    stages += [tokens_text, tokens_visual, share_up, share_out, finish_up, share_down]
     scatter.run(plan, stages)
 
     def mine(third, of):
         first = third * 2 * width + of * width
         return v.grad_qkv.at[:, :, pl.ds(pl.multiple_of(first, lane), width)]
 
-    small = v.stage_qkv.at[:, :, 3 * width :]
-    last = [moves.across(small, v.peer_small)]
+    last = [moves.across(v.stage_small, v.peer_small)]
     for third in range(3):
-        source = v.stage_qkv.at[:, :, third * width : (third + 1) * width]
+        for at in range(heads // 2):
+            to = slice(at * lane, (at + 1) * lane)
+            v.own_qkv[third, 0, :, to] = v.stage_qkv[0, :, (3 * at + third) * lane : (3 * at + third + 1) * lane]
+            v.own_qkv[third, 1, :, to] = v.stage_qkv_v[at, :, third * lane : (third + 1) * lane]
+        source = v.own_qkv.at[third]
         moves.save(source, mine(third, core))
         last.append(moves.across(source, mine(third, core), mine(third, 1 - core)))
     last[0].wait_recv()
     for s in range(2):
-        own, peer = v.stage_qkv[s, :, 3 * width :], v.peer_small[s, :, :]
+        own, peer = v.stage_small[s, :, :], v.peer_small[s, :, :]
         columns = own.shape[0]
         empty = jnp.zeros((lane - columns, lane), full)
         own, peer = (jnp.concatenate([value, empty], 0).T[:, :columns] for value in (own, peer))
@@ -1840,14 +2101,16 @@
 
 def attention_back(n_docs, heads, scale, pieces, plan, inputs):
     line_size = n_docs // 4
-    count, dim = inputs.h.shape
-    width, wide = inputs.qkv.shape[1] // 3, inputs.full_qkv.shape[2]
+    count, dim = inputs.qkv.shape[0], inputs.h.shape[1]
+    width = inputs.qkv.shape[1] // 3
+    text, visual = inputs.text.shape[1], inputs.visual.shape[1]
     hidden = inputs.part_up.shape[2]
     rows = dim // n_docs
     block = hidden // n_docs
-    splits = (False, True, False, False)
-    part_qkv = ((2, dim, wide), low)
-    arrays = same_as([inputs.part_up, inputs.part_out]) + [part_qkv] + same_as([inputs.part_up_v])
+    splits = (False, True, False, False, False, False)
+    parts = (((1, dim, 3 * width), low), ((1, dim, 3 * lane), low), ((2, dim, lane), low))
+    arrays = same_as([inputs.part_up, inputs.part_out]) + [parts[0]] + same_as([inputs.part_up_v])
+    arrays += parts[1:]
     results = AttentionOut(
         text_grad=(inputs.text.shape, full),
         visual_grad=(inputs.visual.shape, full),
@@ -1860,7 +2123,9 @@
         grad_gain_ffn=((2, rows), full),
     )
     scratch = AttentionScratch(
-        part_qkv=part_qkv,
+        part_qkv=parts[0],
+        part_qkv_v=parts[1],
+        part_small=parts[2],
         x=((count // 2, dim), low),
         q_t=((width, count), low),
         k_t=((width, count), low),
@@ -1869,14 +2134,23 @@
         visual_grad_n=((count, width), low),
         key_sum=((count, lane), full),
         value_sum=((count, lane), full),
-        grad_wide=((count, wide), low),
-        wide=((count, dim), full),
-        received=((count // 2, dim), full),
-        gain_sum=((2, lane, dim), full),
+        grad_wide=((count, 3 * width + 3 * lane), low),
+        wide=((2 * text, dim), full),
+        received=((text, dim), full),
+        grad_v=((8 * visual, 3 * lane), low),
+        wide_v=((8 * visual, dim), full),
+        received_v=((4 * visual, dim), full),
+        outgoing_v=((3 * visual, dim), low),
+        landing_v=((3 * visual, dim), low),
+        gain_sum=((2, dim, lane), full),
+        gains_row=((2, lane, dim), full),
         stage_up=((1, rows, hidden), full),
         stage_out=((2, rows, dim), full),
-        stage_qkv=((2, rows, wide), full),
+        stage_qkv=((1, rows, 3 * width), full),
         stage_up_v=((4, rows, hidden // 4), full),
+        stage_qkv_v=((4, rows, 3 * lane), full),
+        stage_small=((2, rows, lane), full),
+        own_qkv=((3, 2, rows, width), full),
         peer_up=((1, rows, hidden), full),
         peer_up_v=((4, rows, hidden // 4), full),
         peer_small=((2, rows, lane), full),
@@ -1894,7 +2168,7 @@
         scratch_shapes=scratch_of(loaded)
         + scratch_of(scratch)
         + scatter_buffers(pieces, arrays, splits, n_docs)
-        + sems((len(pieces), line_size, 11), (len(pieces), line_size, 11), 40, 16, 16),
+        + sems(len(pieces), arrival_offsets(pieces, line_size)[-1], 35, 19, 19),
         compiler_params=pltpu.CompilerParams(
             collective_id=2, has_side_effects=True, vmem_limit_bytes=vmem_limit
         ),

time: 231 us -> 204 us (0.88)
  Pallas kernels: 226 us -> 199 us
    pallas_call x1, Pallas kernels: 102 us -> 89.2 us  [front(): pl.pallas_call(functools.partial(front_kernel, line_size, heads, scale, p...]
    pallas_call x1, Pallas kernels: 80.2 us -> 71.8 us  [attention_back(): pl.pallas_call(functools.partial(attention_kernel, line_size, heads, scal...]
    pallas_call x1, Pallas kernels: 39.3 us -> 33.4 us  [ffn_back(): pl.pallas_call(functools.partial(ffn_kernel, line_size, heads, pieces, pl...]
where the time goes in v1:
time: 204 us; the launch traced here: 200 us
  Pallas kernels  199 us (98%)
    pallas_call x1, Pallas kernels, front(): pl.pallas_call(functools.partial(front_kernel, line_size, heads, scale, p...  89.2 us
    pallas_call x1, Pallas kernels, attention_back(): pl.pallas_call(functools.partial(attention_kernel, line_size, heads, scal...  71.8 us
    pallas_call x1, Pallas kernels, ffn_back(): pl.pallas_call(functools.partial(ffn_kernel, line_size, heads, pieces, pl...  33.4 us
    pallas_call x1, Pallas kernels, publish(): pl.pallas_call(functools.partial(publish_kernel, count), out_shape=shapes...  5.05 us

profile of v1, /device:TPU:9, one launch (start us, length us, event | category | flops | bytes accessed | tf_op | source)
XLA Modules:
  0.0 200.4 jit_solution(10729724373867411526)
XLA Ops:
  0.6 89.2 %gather_and_front.1 = (bf16[1,768,1280]{2,1,0:T(8,128)(2,1)}, bf16[1,768,1536]{2,1,0:T(8,128)(2,1)}, bf16[2,384,768]{2,1,0:T(8,128)(2,1)}, bf16[1,1536,768]{2,1,...) custom-call(bf16[2,48,2304]{2,1,0:T(8,128)(2,1)} %refs_0_.1, ...), custom_call_target="tpu_custom_call" | custom-call | tf_op jit(solution)/shard_map/gather_and_front/pallas_call | solution.py:1322
  89.8 33.4 %ffn_back_and_scatter.1 = (bf16[1,368,768]{2,1,0:T(8,128)(2,1)}, bf16[1,48,768]{2,1,0:T(8,128)(2,1)}, f32[2,96,768]{2,1,0:T(8,128)}, bf16[1,768,1536]{2,1,0:T(8,...) custom-call(bf16[1,1536,768]{2,1,0:T(8,128)(2,1)} %get-tuple-element, ...), custom_call_target="tpu_custom_call" | custom-call | tf_op jit(solution)/shard_map/ffn_back_and_scatter/pallas_call | solution.py:1693
  123.2 71.8 %attention_back_and_scatter.1 = (f32[1,368,768]{2,1,0:T(8,128)}, f32[1,48,768]{2,1,0:T(8,128)}, f32[2,192,768]{2,1,0:T(8,128)}, f32[2,48,2304]{2,1,0:T(8,128)}, ...) custom-call(bf16[832,1152]{1,0:T(8,128)(2,1)} %get-tuple-element.94., ...), custom_call_target="tpu_custom_call" | custom-call | tf_op jit(solution)/shard_map/attention_back_and_scatter/pallas_call | solution.py:2163
  195.1 5.1 %publish.1 = (bf16[1,368,768]{2,1,0:T(8,128)(2,1)}, bf16[1,48,768]{2,1,0:T(8,128)(2,1)}, f32[1,368,768]{2,1,0:T(8,128)}, f32[1,48,768]{2,1,0:T(8,128)}, f32[2,48...) custom-call(bf16[1,368,768]{2,1,0:T(8,128)(2,1)} %get-tuple-element., ...), custom_call_target="tpu_custom_call" | custom-call | tf_op jit(solution)/shard_map/publish/pallas_call | solution.py:2196

commit v2 on v1

--- a/solution.py
+++ b/solution.py
@@ -683,12 +683,37 @@
     def spread(self, own, target):
         other = self.moves.across(own, self.part(target, 4))
         return other, [
-            self.moves.peer(own, self.part(target, 1 + at), step) for at, step in enumerate(self.steps)
+            self.moves.peer(own, self.part(target, 1 + at), step) for at, step in enumerate(self.steps[:2])
         ]
 
-    def pass_on(self, target, arrivals):
-        for arrival in arrivals:
-            arrival.wait_recv()
+    def relay(self, target, arrivals):
+        moves, core = self.moves, self.place.core
+        made = [
+            pltpu.make_async_remote_copy(
+                src_ref=self.part(target, 1 + at),
+                dst_ref=self.part(target, 3),
+                send_sem=moves.send_sems.at[moves.remotes],
+                recv_sem=moves.recv_sems.at[moves.remotes],
+                device_id=self.place.device(step),
+                device_id_type=MESH,
+            )
+            for at, step in enumerate((by_y, by_x))
+        ]
+        moves.remotes += 1
+        for at in range(2):
+
+            def pass_along():
+                arrivals[at].wait_recv()
+                made[at].start()
+
+            pl.when(core == at)(pass_along)
+            moves.to_end.append(functools.partial(pl.when(core == at), made[at].wait_send))
+        return made[0]
+
+    def pass_on(self, target, arrivals, fourth):
+        for at in range(2):
+            pl.when(self.place.core != at)(arrivals[at].wait_recv)
+        fourth.wait_recv()
         return self.moves.across(self.part(target, 1, 3), self.part(target, 5, 3))
 
     def halve(self, wide, received):
@@ -750,59 +775,60 @@
 
 
 front_pieces = (
-    (0, 0, 0, 32, 0, 0), (0, 0, 32, 16, 1, 0), (1, 0, 0, 32, 0, 0), (1, 0, 32, 16, 1, 0),
-    (2, 0, 0, 48, 0, 0), (2, 1, 0, 48, 1, 0), (3, 0, 0, 32, 0, 0), (3, 0, 32, 16, 1, 0),
-    (3, 0, 48, 48, 1, 1), (4, 0, 0, 48, 0, 3), (5, 0, 0, 96, 0, 2), (6, 0, 0, 48, 0, 3),
+    (0, 0, 0, 32, 0, 0), (0, 0, 32, 16, 1, 0), (1, 0, 0, 16, 0, 0), (1, 0, 16, 32, 1, 0),
+    (3, 0, 0, 32, 0, 0), (3, 0, 32, 16, 1, 0), (3, 0, 48, 48, 0, 1), (2, 0, 0, 48, 0, 0),
+    (2, 1, 0, 48, 1, 0), (4, 0, 0, 48, 0, 3), (5, 0, 0, 96, 0, 2), (6, 0, 0, 48, 0, 3),
     (7, 0, 0, 48, 1, 0),
 )
 front_plan = (
-    (0, 4, 0), (0, 11, 0), (5, 23, 0), (0, 1, 0), (0, 8, 0), (3, 11, 1), (2, 4, 1), (5, 25, 0), (0, 12, 0),
-    (3, 11, 2), (2, 12, 1), (0, 7, 0), (5, 0, 0), (0, 0, 0), (0, 6, 0), (2, 12, 2), (3, 11, 3), (2, 1, 1),
-    (2, 0, 1), (3, 11, 4), (5, 26, 0), (0, 5, 0), (2, 4, 2), (2, 12, 3), (0, 9, 0), (2, 0, 2), (0, 3, 0),
-    (1, 1, 0), (0, 10, 0), (2, 1, 2), (1, 12, 3), (1, 4, 2), (1, 0, 2), (1, 12, 0), (0, 2, 0), (2, 0, 3),
-    (2, 5, 1), (2, 10, 1), (1, 0, 0), (1, 12, 1), (1, 0, 1), (2, 1, 3), (1, 12, 2), (3, 9, 1), (2, 4, 3),
-    (1, 1, 2), (3, 8, 1), (4, 6, 0), (2, 5, 2), (5, 1, 0), (1, 0, 3), (1, 1, 3), (1, 1, 1), (2, 2, 1),
-    (2, 10, 2), (4, 7, 0), (5, 4, 0), (5, 5, 0), (2, 7, 1), (5, 24, 0), (1, 5, 1), (4, 0, 0), (3, 9, 2),
-    (2, 3, 1), (5, 2, 0), (5, 3, 0), (1, 5, 2), (2, 6, 1), (1, 4, 3), (2, 5, 3), (1, 2, 1), (1, 5, 0),
-    (2, 2, 2), (5, 6, 0), (5, 7, 0), (5, 8, 0), (1, 4, 0), (5, 9, 0), (1, 4, 1), (2, 7, 2), (2, 3, 2),
-    (3, 8, 2), (1, 5, 3), (1, 2, 0), (5, 10, 0), (5, 11, 0), (2, 2, 3), (1, 3, 1), (2, 3, 3), (5, 12, 0),
-    (5, 13, 0), (2, 6, 2), (2, 10, 3), (1, 2, 2), (4, 2, 0), (5, 14, 0), (1, 3, 0), (2, 7, 3), (1, 3, 2),
-    (3, 9, 3), (2, 6, 3), (1, 7, 1), (1, 2, 3), (1, 3, 3), (1, 7, 0), (1, 7, 3), (3, 8, 3), (5, 16, 0),
-    (5, 15, 0), (3, 9, 4), (1, 7, 2), (1, 6, 1), (1, 6, 2), (4, 5, 0), (1, 6, 0), (4, 1, 0), (5, 18, 0),
-    (5, 19, 0), (3, 8, 4), (5, 17, 0), (1, 6, 3), (5, 21, 0), (4, 4, 0), (5, 20, 0), (4, 3, 0), (5, 22, 0),
+    (5, 25, 0), (0, 6, 0), (5, 27, 0), (0, 12, 0), (0, 0, 0), (0, 7, 0), (0, 5, 0), (2, 12, 1), (0, 1, 0),
+    (0, 11, 0), (2, 0, 1), (2, 12, 2), (0, 4, 0), (2, 7, 1), (2, 5, 1), (5, 0, 0), (5, 23, 0), (0, 2, 0),
+    (2, 7, 2), (2, 12, 3), (1, 12, 1), (2, 0, 2), (2, 1, 1), (3, 11, 1), (1, 12, 3), (0, 9, 0), (2, 1, 2),
+    (2, 0, 3), (2, 7, 3), (2, 5, 2), (2, 2, 1), (3, 11, 2), (5, 28, 0), (0, 8, 0), (1, 12, 2), (1, 12, 0),
+    (2, 1, 3), (1, 0, 3), (2, 5, 3), (1, 7, 3), (1, 1, 0), (3, 11, 3), (5, 1, 0), (1, 0, 2), (3, 9, 1),
+    (2, 8, 1), (1, 0, 0), (3, 9, 2), (5, 26, 0), (4, 7, 0), (3, 11, 4), (2, 8, 2), (1, 1, 2), (1, 1, 1),
+    (5, 4, 0), (1, 0, 1), (0, 3, 0), (1, 1, 3), (4, 6, 0), (5, 5, 0), (2, 8, 3), (2, 2, 2), (3, 6, 1),
+    (2, 4, 1), (2, 3, 1), (1, 5, 0), (1, 7, 0), (4, 0, 0), (0, 10, 0), (5, 2, 0), (5, 3, 0), (3, 9, 3),
+    (5, 6, 0), (1, 8, 1), (2, 2, 3), (5, 7, 0), (1, 8, 3), (1, 7, 1), (1, 3, 0), (1, 7, 2), (1, 8, 0),
+    (1, 8, 2), (2, 3, 2), (5, 8, 0), (5, 9, 0), (3, 6, 2), (1, 4, 0), (1, 2, 3), (2, 4, 2), (5, 10, 0),
+    (5, 11, 0), (1, 5, 2), (5, 12, 0), (2, 3, 3), (1, 2, 2), (5, 13, 0), (4, 2, 0), (1, 2, 0), (1, 3, 2),
+    (3, 9, 4), (5, 14, 0), (1, 3, 1), (2, 10, 1), (1, 2, 1), (1, 3, 3), (5, 15, 0), (5, 16, 0), (1, 4, 1),
+    (3, 6, 3), (1, 5, 1), (5, 29, 0), (2, 10, 2), (1, 4, 2), (4, 4, 0), (4, 1, 0), (1, 5, 3), (2, 4, 3),
+    (5, 18, 0), (5, 30, 0), (5, 19, 0), (5, 24, 0), (3, 6, 4), (1, 4, 3), (5, 17, 0), (5, 21, 0),
+    (5, 20, 0), (5, 22, 0), (2, 10, 3), (4, 3, 0), (4, 5, 0),
 )
 ffn_pieces = (
     (0, 0, 0, 48, 0, 0), (0, 0, 48, 48, 1, 0), (1, 0, 0, 96, 0, 2),
 )
 ffn_plan = (
-    (0, 0, 0), (0, 2, 0), (0, 1, 0), (0, 1, 1), (0, 1, 2), (0, 0, 1), (4, 2, 0), (2, 2, 0), (0, 0, 2),
-    (0, 2, 1), (4, 0, 0), (4, 1, 0), (1, 1, 0), (4, 9, 0), (2, 2, 1), (1, 0, 0), (1, 0, 1), (0, 2, 2),
-    (4, 3, 0), (0, 2, 3), (2, 2, 2), (4, 4, 0), (0, 0, 3), (1, 0, 2), (1, 1, 1), (4, 10, 0), (2, 0, 0),
-    (1, 1, 2), (0, 1, 3), (4, 5, 0), (2, 1, 0), (4, 13, 0), (4, 7, 0), (2, 0, 1), (4, 8, 0), (4, 6, 0),
-    (2, 2, 3), (2, 1, 1), (2, 1, 2), (1, 0, 3), (1, 1, 3), (4, 14, 0), (2, 0, 2), (4, 11, 0), (4, 12, 0),
-    (4, 15, 0), (2, 0, 3), (2, 1, 3),
+    (0, 1, 0), (0, 2, 0), (0, 0, 0), (0, 2, 1), (0, 1, 1), (0, 1, 2), (0, 0, 1), (4, 2, 0), (2, 2, 0),
+    (0, 2, 2), (1, 1, 0), (4, 0, 0), (1, 0, 0), (4, 1, 0), (2, 2, 1), (1, 1, 1), (0, 0, 2), (4, 4, 0),
+    (4, 3, 0), (4, 6, 0), (1, 0, 1), (4, 10, 0), (2, 2, 2), (1, 1, 2), (0, 1, 3), (2, 1, 0), (4, 9, 0),
+    (0, 0, 3), (2, 0, 0), (1, 0, 2), (4, 13, 0), (2, 1, 1), (0, 2, 3), (4, 7, 0), (4, 8, 0), (1, 1, 3),
+    (2, 0, 1), (2, 1, 2), (4, 5, 0), (2, 0, 2), (2, 2, 3), (1, 0, 3), (4, 11, 0), (4, 12, 0), (4, 15, 0),
+    (2, 1, 3), (4, 14, 0), (2, 0, 3),
 )
 attention_pieces = (
-    (0, 0, 0, 16, 0, 0), (0, 0, 16, 32, 1, 0), (1, 0, 0, 48, 0, 0), (1, 1, 0, 48, 1, 0),
+    (0, 0, 0, 32, 0, 0), (0, 0, 32, 16, 1, 0), (1, 0, 0, 48, 0, 0), (1, 1, 0, 48, 1, 0),
     (2, 0, 0, 32, 1, 0), (2, 0, 32, 16, 0, 0), (3, 0, 0, 48, 0, 3), (4, 0, 0, 48, 0, 3),
     (5, 0, 0, 48, 0, 0), (5, 1, 0, 48, 1, 0),
 )
 attention_plan = (
-    (0, 1, 0), (0, 0, 0), (0, 3, 0), (0, 3, 1), (0, 1, 1), (4, 0, 0), (0, 0, 1), (4, 1, 0), (0, 2, 0),
-    (4, 2, 0), (1, 3, 0), (0, 6, 0), (0, 2, 1), (0, 2, 2), (4, 3, 0), (0, 1, 2), (2, 6, 0), (0, 3, 2),
-    (1, 1, 0), (1, 0, 0), (4, 4, 0), (4, 5, 0), (0, 2, 3), (1, 3, 1), (4, 6, 0), (4, 7, 0), (1, 2, 0),
-    (2, 1, 0), (0, 3, 3), (4, 9, 0), (2, 0, 0), (1, 2, 1), (0, 6, 1), (0, 5, 0), (0, 4, 0), (0, 0, 2),
-    (0, 0, 3), (4, 10, 0), (0, 6, 2), (4, 8, 0), (4, 12, 0), (1, 1, 1), (2, 2, 0), (1, 4, 0), (1, 0, 1),
-    (2, 3, 0), (0, 4, 1), (2, 6, 1), (4, 11, 0), (0, 7, 0), (0, 7, 1), (4, 13, 0), (4, 14, 0), (0, 9, 0),
-    (1, 5, 0), (0, 9, 1), (1, 0, 2), (1, 2, 2), (0, 6, 3), (0, 8, 0), (2, 6, 2), (1, 1, 2), (2, 3, 1),
-    (2, 7, 0), (1, 9, 0), (0, 8, 1), (2, 0, 1), (0, 4, 2), (1, 8, 0), (0, 5, 1), (2, 4, 0), (0, 9, 2),
-    (2, 0, 2), (0, 7, 2), (0, 8, 2), (1, 4, 1), (1, 0, 3), (0, 5, 2), (2, 7, 1), (1, 9, 1), (0, 1, 3),
-    (1, 8, 1), (1, 4, 2), (1, 5, 1), (2, 7, 2), (0, 8, 3), (2, 9, 0), (2, 6, 3), (2, 1, 1), (2, 2, 1),
-    (1, 3, 2), (1, 3, 3), (1, 8, 2), (2, 1, 2), (1, 1, 3), (2, 9, 1), (2, 8, 0), (0, 4, 3), (0, 7, 3),
-    (2, 5, 0), (1, 9, 2), (1, 2, 3), (0, 5, 3), (1, 5, 2), (2, 8, 1), (1, 8, 3), (2, 5, 1), (2, 4, 1),
-    (2, 8, 2), (2, 3, 2), (3, 6, 0), (2, 0, 3), (4, 18, 0), (2, 2, 2), (0, 9, 3), (1, 4, 3), (2, 1, 3),
-    (4, 15, 0), (2, 9, 2), (2, 4, 2), (2, 7, 3), (1, 5, 3), (2, 2, 3), (2, 5, 2), (1, 9, 3), (2, 3, 3),
-    (4, 17, 0), (2, 4, 3), (2, 8, 3), (3, 7, 0), (4, 16, 0), (2, 9, 3), (2, 5, 3),
+    (0, 1, 0), (0, 0, 0), (0, 2, 0), (0, 1, 1), (0, 1, 2), (4, 0, 0), (4, 1, 0), (1, 1, 0), (0, 6, 0),
+    (0, 1, 3), (0, 3, 0), (1, 0, 0), (0, 0, 1), (4, 2, 0), (4, 3, 0), (4, 4, 0), (1, 2, 0), (1, 0, 1),
+    (1, 1, 1), (0, 0, 2), (4, 5, 0), (0, 3, 1), (4, 6, 0), (4, 7, 0), (0, 6, 1), (4, 9, 0), (0, 5, 0),
+    (2, 6, 0), (1, 3, 0), (0, 4, 0), (0, 5, 1), (2, 1, 0), (0, 6, 2), (0, 2, 1), (4, 10, 0), (1, 0, 2),
+    (4, 11, 0), (0, 4, 1), (0, 7, 0), (2, 6, 1), (1, 1, 2), (0, 7, 1), (1, 4, 0), (4, 8, 0), (4, 12, 0),
+    (0, 5, 2), (0, 4, 2), (2, 7, 0), (1, 4, 1), (2, 6, 2), (2, 0, 0), (1, 2, 1), (0, 2, 2), (1, 5, 0),
+    (2, 3, 0), (0, 6, 3), (4, 13, 0), (2, 1, 1), (2, 2, 0), (1, 5, 1), (2, 1, 2), (4, 14, 0), (0, 8, 0),
+    (0, 0, 3), (0, 9, 0), (0, 9, 1), (0, 3, 2), (0, 4, 3), (2, 0, 1), (0, 8, 1), (0, 8, 2), (0, 7, 2),
+    (2, 7, 1), (2, 7, 2), (0, 9, 2), (1, 1, 3), (1, 9, 0), (1, 5, 2), (1, 8, 0), (1, 3, 1), (0, 8, 3),
+    (1, 9, 1), (0, 2, 3), (2, 5, 0), (2, 6, 3), (0, 3, 3), (1, 3, 2), (2, 4, 0), (2, 0, 2), (0, 5, 3),
+    (0, 7, 3), (1, 8, 1), (1, 0, 3), (2, 2, 1), (1, 9, 2), (2, 9, 0), (1, 4, 2), (2, 8, 0), (1, 2, 2),
+    (2, 4, 1), (2, 1, 3), (2, 3, 1), (1, 2, 3), (4, 18, 0), (1, 4, 3), (1, 8, 2), (2, 5, 1), (3, 6, 0),
+    (2, 5, 2), (1, 8, 3), (1, 3, 3), (0, 9, 3), (2, 9, 1), (2, 8, 1), (2, 3, 2), (1, 5, 3), (2, 0, 3),
+    (4, 15, 0), (2, 2, 2), (2, 7, 3), (2, 8, 2), (2, 4, 2), (2, 9, 2), (1, 9, 3), (4, 17, 0), (3, 7, 0),
+    (2, 5, 3), (2, 2, 3), (2, 8, 3), (2, 3, 3), (4, 16, 0), (2, 4, 3), (2, 9, 3),
 )
 
 
@@ -1023,11 +1049,6 @@
 
     place.greet()
     shards = [moves.local(source, target) for source, target in zip(groups[0][:7], groups[3][:7])]
-    shards[0].wait()
-    shards[1].wait()
-    shards[3].wait()
-    shards[4].wait()
-    prepare_shards(v, core, heads)
     place.meet()
     plane = Plane(place, moves, rows.visual)
     loads = [
@@ -1041,6 +1062,11 @@
         moves.across(v.text_dy.at[0], v.s_dy.at[slice(*rows.other[0])]),
     ]
 
+    def prepare_qkv():
+        for at in (0, 1, 3, 4):
+            shards[at].wait()
+        prepare_shards(v, core, heads)
+
     def prepare():
         shards[2].wait()
         prepare_hidden(v, core, block)
@@ -1085,8 +1111,11 @@
     def spread_x():
         arrivals[6] = plane.spread(v.visual.at[0], v.x_v)
 
+    def relay_x():
+        arrivals[9] = plane.relay(v.x_v, arrivals[6][1])
+
     def pass_x():
-        arrivals[7] = plane.pass_on(v.x_v, arrivals[6][1])
+        arrivals[7] = plane.pass_on(v.x_v, arrivals[6][1], arrivals[9])
 
     def lower_visual():
         moves.save(v.s_w_small_v, v.full_small_v)
@@ -1157,8 +1186,11 @@
     def spread_dy():
         arrivals[2] = plane.spread(v.visual_dy.at[0], v.s_dy_v)
 
+    def relay_dy():
+        arrivals[10] = plane.relay(v.s_dy_v, arrivals[2][1])
+
     def pass_dy():
-        arrivals[3] = plane.pass_on(v.s_dy_v, arrivals[2][1])
+        arrivals[3] = plane.pass_on(v.s_dy_v, arrivals[2][1], arrivals[10])
 
     def middle_rows(s, x, ref, start):
         arrivals[0][s].wait_recv()
@@ -1181,8 +1213,11 @@
         middle_rows(0, v.x, v.s_hm, 0)
         arrivals[1] = rows.swap_own(moves, v.s_hm, 0)
 
+    def relay_hm():
+        arrivals[11] = plane.relay(v.s_hm_v, arrivals[4][1])
+
     def pass_hm():
-        arrivals[5] = plane.pass_on(v.s_hm_v, arrivals[4][1])
+        arrivals[5] = plane.pass_on(v.s_hm_v, arrivals[4][1], arrivals[11])
 
     def up_part(hm, w_up, act_ref, slope_ref, start, stop):
         size = 256 if (stop - start) % 256 == 0 else lane
@@ -1241,6 +1276,7 @@
     stages += [functools.partial(attend_head, rows, head_width, v, head) for head in range(heads)]
     stages += [mix, branch, middle_visual, middle_text, pass_hm, up_first, up_second, up_visual]
     stages += [down_text, down_visual, spread_dy, pass_dy, spread_x, pass_x]
+    stages += [prepare_qkv, relay_x, relay_dy, relay_hm]
     gather.run(plan, stages)
     moves.finish()
     gather.finish()
@@ -2162,44 +2198,51 @@
     loaded = same_as(inputs[:-2])
     values = pl.pallas_call(
         functools.partial(attention_kernel, line_size, heads, scale, block, pieces, plan),
-        out_shape=shapes_of(results),
+        out_shape=scratch_of(results),
         in_specs=specs_of(len(inputs), 0),
-        out_specs=specs_of(len(results), 0),
+        out_specs=specs_of(len(results), len(results)),
         scratch_shapes=scratch_of(loaded)
         + scratch_of(scratch)
         + scatter_buffers(pieces, arrays, splits, n_docs)
         + sems(len(pieces), arrival_offsets(pieces, line_size)[-1], 35, 19, 19),
         compiler_params=pltpu.CompilerParams(
-            collective_id=2, has_side_effects=True, vmem_limit_bytes=vmem_limit
+            collective_id=2, has_side_effects=True, vmem_limit_bytes=50 * 1024 * 1024
         ),
         name="attention_back_and_scatter",
     )(*inputs)
     return AttentionOut(*values)
 
 
-def publish_kernel(count, *refs):
-    sources, results, held = refs[:count], refs[count : 2 * count], refs[2 * count : 3 * count]
-    arriving, leaving = refs[3 * count :]
-    copies_in = [pltpu.make_async_copy(sources[at], held[at], arriving.at[at]) for at in range(count)]
-    copies_out = [pltpu.make_async_copy(held[at], results[at], leaving.at[at]) for at in range(count)]
+def publish_kernel(held, count, *refs):
+    sources, results, passing = refs[:count], refs[count : 2 * count], refs[2 * count : 3 * count - held]
+    arriving, leaving = refs[3 * count - held :]
+    copies_in = [
+        pltpu.make_async_copy(source, target, arriving.at[at])
+        for at, (source, target) in enumerate(zip(sources[held:], passing))
+    ]
+    ready = [*sources[:held], *passing]
+    copies_out = [pltpu.make_async_copy(ready[at], results[at], leaving.at[at]) for at in range(count)]
     for copy in copies_in:
         copy.start()
-    for copy_in, copy_out in zip(copies_in, copies_out):
+    for copy in copies_out[:held]:
+        copy.start()
+    for copy_in, copy_out in zip(copies_in, copies_out[held:]):
         copy_in.wait()
         copy_out.start()
     for copy in copies_out:
         copy.wait()
 
 
-def publish(arrays):
+def publish(held, others):
+    arrays = (*held, *others)
     count = len(arrays)
     return pl.pallas_call(
-        functools.partial(publish_kernel, count),
+        functools.partial(publish_kernel, len(held), count),
         out_shape=shapes_of(same_as(arrays)),
-        in_specs=specs_of(count, 0),
+        in_specs=specs_of(count, len(held)),
         out_specs=specs_of(count, 0),
-        scratch_shapes=scratch_of(same_as(arrays)) + sems(count, count),
-        compiler_params=pltpu.CompilerParams(vmem_limit_bytes=vmem_limit),
+        scratch_shapes=scratch_of(same_as(others)) + sems(len(others), count),
+        compiler_params=pltpu.CompilerParams(vmem_limit_bytes=8 * 1024 * 1024),
         name="publish",
     )(*arrays)
 
@@ -2212,21 +2255,20 @@
     known = merged(inputs, first, second)
     attention_inputs = AttentionIn(*(getattr(known, name) for name in AttentionIn._fields))
     third = attention_back(n_docs, heads, scale, made[2], attention_plan, attention_inputs)
-    results = (
-        second.text_out,
-        second.visual_out,
-        third.text_grad,
-        third.visual_grad,
-        third.grad_qkv,
-        third.grad_out,
-        third.grad_gate,
-        third.grad_up,
-        third.grad_down,
-        third.grad_gain_attn,
-        third.grad_gain_ffn,
-    )
-    results = publish(results)
-    return (*results[:6], jnp.transpose(results[6], (1, 2, 0)), *results[7:])
+    held = publish(third, (second.text_out, second.visual_out))
+    done = AttentionOut(*held[: len(third)])
+    return (
+        *held[len(third) :],
+        done.text_grad,
+        done.visual_grad,
+        done.grad_qkv,
+        done.grad_out,
+        jnp.transpose(done.grad_gate, (1, 2, 0)),
+        done.grad_up,
+        done.grad_down,
+        done.grad_gain_attn,
+        done.grad_gain_ffn,
+    )
 
 
 def swap(value):

time: 204 us -> 192 us (0.941)
  Pallas kernels: 199 us -> 188 us
    pallas_call x1, Pallas kernels: 71.8 us -> 67.5 us  [attention_back(): pl.pallas_call(functools.partial(attention_kernel, line_size, heads, scal...]
    pallas_call x1, Pallas kernels: 89.2 us -> 85.6 us  [front(): pl.pallas_call(functools.partial(front_kernel, line_size, heads, scale, p...]
    pallas_call x1, Pallas kernels: 5.05 us -> 2.7 us  [publish(): pl.pallas_call(functools.partial(publish_kernel, len(held), count), out_s...]
where the time goes in v2:
time: 192 us; the launch traced here: 189 us
  Pallas kernels  188 us (98%)
    pallas_call x1, Pallas kernels, front(): pl.pallas_call(functools.partial(front_kernel, line_size, heads, scale, p...  85.6 us
    pallas_call x1, Pallas kernels, attention_back(): pl.pallas_call(functools.partial(attention_kernel, line_size, heads, scal...  67.5 us
    pallas_call x1, Pallas kernels, ffn_back(): pl.pallas_call(functools.partial(ffn_kernel, line_size, heads, pieces, pl...  32.5 us

profile of v2, /device:TPU:9, one launch (start us, length us, event | category | flops | bytes accessed | tf_op | source)
XLA Modules:
  0.0 189.3 jit_solution(9242436141621752108)
XLA Ops:
  0.6 85.6 %gather_and_front.1 = (bf16[1,768,1280]{2,1,0:T(8,128)(2,1)}, bf16[1,768,1536]{2,1,0:T(8,128)(2,1)}, bf16[2,384,768]{2,1,0:T(8,128)(2,1)}, bf16[1,1536,768]{2,1,...) custom-call(bf16[2,48,2304]{2,1,0:T(8,128)(2,1)} %refs_0_.1, ...), custom_call_target="tpu_custom_call" | custom-call | tf_op jit(solution)/shard_map/gather_and_front/pallas_call | solution.py:1358
  86.3 32.5 %ffn_back_and_scatter.1 = (bf16[1,368,768]{2,1,0:T(8,128)(2,1)}, bf16[1,48,768]{2,1,0:T(8,128)(2,1)}, f32[2,96,768]{2,1,0:T(8,128)}, bf16[1,768,1536]{2,1,0:T(8,...) custom-call(bf16[1,1536,768]{2,1,0:T(8,128)(2,1)} %get-tuple-element, ...), custom_call_target="tpu_custom_call" | custom-call | tf_op jit(solution)/shard_map/ffn_back_and_scatter/pallas_call | solution.py:1729
  118.8 0.0 copy-start
  118.8 0.0 copy-start.1
  118.8 67.5 %attention_back_and_scatter.1 = (f32[1,368,768]{2,1,0:T(8,128)S(1)}, f32[1,48,768]{2,1,0:T(8,128)S(1)}, f32[2,192,768]{2,1,0:T(8,128)S(1)}, f32[2,48,2304]{2,1,0...) custom-call(bf16[832,1152]{1,0:T(8,128)(2,1)} %get-tuple-element.71., ...), custom_call_target="tpu_custom_call" | custom-call | tf_op jit(solution)/shard_map/attention_back_and_scatter/pallas_call | solution.py:2199
  186.4 0.0 copy-done
  186.4 0.0 copy-done.1
  186.4 2.7 %publish.1 = (f32[1,368,768]{2,1,0:T(8,128)}, f32[1,48,768]{2,1,0:T(8,128)}, f32[2,192,768]{2,1,0:T(8,128)}, f32[2,48,2304]{2,1,0:T(8,128)}, f32[12,2,48]{2,1,0:...) custom-call(f32[1,368,768]{2,1,0:T(8,128)S(1)} %get-tuple-element.10, ...), custom_call_target="tpu_custom_call" | custom-call | tf_op jit(solution)/shard_map/publish/pallas_call | solution.py:2239
Async XLA Ops:
  118.8 67.6 %copy-start = (bf16[1,368,768]{2,1,0:T(8,128)(2,1)S(1)}, bf16[1,368,768]{2,1,0:T(8,128)(2,1)}, u32[]{:S(2)}) copy-start(bf16[1,368,768]{2,1,0:T(8,128)(2,1)} %get-tuple-element.118.refs_9_) | copy-start | bytes 1695748
  118.8 67.6 %copy-start.1 = (bf16[1,48,768]{2,1,0:T(8,128)(2,1)S(1)}, bf16[1,48,768]{2,1,0:T(8,128)(2,1)}, u32[]{:S(2)}) copy-start(bf16[1,48,768]{2,1,0:T(8,128)(2,1)} %get-tuple-element.119.refs_10_) | copy-start | bytes 221188

commit v3 on v2

--- a/solution.py
+++ b/solution.py
@@ -781,21 +781,21 @@
     (7, 0, 0, 48, 1, 0),
 )
 front_plan = (
-    (5, 25, 0), (0, 6, 0), (5, 27, 0), (0, 12, 0), (0, 0, 0), (0, 7, 0), (0, 5, 0), (2, 12, 1), (0, 1, 0),
-    (0, 11, 0), (2, 0, 1), (2, 12, 2), (0, 4, 0), (2, 7, 1), (2, 5, 1), (5, 0, 0), (5, 23, 0), (0, 2, 0),
-    (2, 7, 2), (2, 12, 3), (1, 12, 1), (2, 0, 2), (2, 1, 1), (3, 11, 1), (1, 12, 3), (0, 9, 0), (2, 1, 2),
-    (2, 0, 3), (2, 7, 3), (2, 5, 2), (2, 2, 1), (3, 11, 2), (5, 28, 0), (0, 8, 0), (1, 12, 2), (1, 12, 0),
-    (2, 1, 3), (1, 0, 3), (2, 5, 3), (1, 7, 3), (1, 1, 0), (3, 11, 3), (5, 1, 0), (1, 0, 2), (3, 9, 1),
-    (2, 8, 1), (1, 0, 0), (3, 9, 2), (5, 26, 0), (4, 7, 0), (3, 11, 4), (2, 8, 2), (1, 1, 2), (1, 1, 1),
-    (5, 4, 0), (1, 0, 1), (0, 3, 0), (1, 1, 3), (4, 6, 0), (5, 5, 0), (2, 8, 3), (2, 2, 2), (3, 6, 1),
-    (2, 4, 1), (2, 3, 1), (1, 5, 0), (1, 7, 0), (4, 0, 0), (0, 10, 0), (5, 2, 0), (5, 3, 0), (3, 9, 3),
-    (5, 6, 0), (1, 8, 1), (2, 2, 3), (5, 7, 0), (1, 8, 3), (1, 7, 1), (1, 3, 0), (1, 7, 2), (1, 8, 0),
-    (1, 8, 2), (2, 3, 2), (5, 8, 0), (5, 9, 0), (3, 6, 2), (1, 4, 0), (1, 2, 3), (2, 4, 2), (5, 10, 0),
-    (5, 11, 0), (1, 5, 2), (5, 12, 0), (2, 3, 3), (1, 2, 2), (5, 13, 0), (4, 2, 0), (1, 2, 0), (1, 3, 2),
-    (3, 9, 4), (5, 14, 0), (1, 3, 1), (2, 10, 1), (1, 2, 1), (1, 3, 3), (5, 15, 0), (5, 16, 0), (1, 4, 1),
-    (3, 6, 3), (1, 5, 1), (5, 29, 0), (2, 10, 2), (1, 4, 2), (4, 4, 0), (4, 1, 0), (1, 5, 3), (2, 4, 3),
-    (5, 18, 0), (5, 30, 0), (5, 19, 0), (5, 24, 0), (3, 6, 4), (1, 4, 3), (5, 17, 0), (5, 21, 0),
-    (5, 20, 0), (5, 22, 0), (2, 10, 3), (4, 3, 0), (4, 5, 0),
+    (0, 8, 0), (5, 27, 0), (0, 0, 0), (0, 11, 0), (5, 0, 0), (0, 12, 0), (0, 7, 0), (2, 8, 1), (0, 5, 0),
+    (0, 1, 0), (0, 6, 0), (2, 12, 1), (2, 7, 1), (2, 0, 1), (2, 1, 1), (2, 5, 1), (3, 11, 1), (5, 25, 0),
+    (2, 12, 2), (2, 7, 2), (2, 1, 2), (0, 9, 0), (2, 0, 2), (5, 1, 0), (3, 11, 2), (2, 8, 2), (5, 28, 0),
+    (2, 0, 3), (2, 5, 2), (1, 12, 0), (2, 1, 3), (3, 11, 3), (3, 9, 1), (2, 12, 3), (1, 12, 2), (1, 12, 1),
+    (1, 0, 0), (1, 0, 2), (0, 2, 0), (1, 0, 1), (1, 1, 1), (1, 5, 0), (0, 3, 0), (1, 12, 3), (1, 0, 3),
+    (1, 1, 0), (2, 8, 3), (2, 5, 3), (2, 7, 3), (1, 1, 3), (3, 11, 4), (5, 26, 0), (3, 9, 2), (1, 1, 2),
+    (1, 8, 1), (4, 7, 0), (4, 6, 0), (5, 4, 0), (5, 5, 0), (1, 7, 0), (2, 3, 1), (2, 2, 1), (0, 4, 0),
+    (3, 6, 1), (4, 0, 0), (1, 7, 2), (5, 2, 0), (1, 8, 0), (1, 7, 1), (1, 8, 2), (5, 3, 0), (1, 5, 3),
+    (2, 4, 1), (2, 3, 2), (1, 7, 3), (5, 6, 0), (5, 7, 0), (2, 2, 2), (0, 10, 0), (1, 8, 3), (5, 8, 0),
+    (5, 9, 0), (2, 4, 2), (2, 2, 3), (2, 3, 3), (1, 2, 0), (3, 9, 3), (1, 3, 0), (5, 10, 0), (5, 23, 0),
+    (5, 11, 0), (1, 3, 1), (3, 6, 2), (4, 2, 0), (5, 12, 0), (5, 13, 0), (5, 14, 0), (1, 2, 3), (1, 3, 2),
+    (1, 3, 3), (2, 10, 1), (1, 2, 2), (1, 2, 1), (1, 4, 2), (5, 15, 0), (5, 16, 0), (1, 5, 2), (1, 4, 0),
+    (3, 9, 4), (2, 4, 3), (5, 29, 0), (3, 6, 3), (2, 10, 2), (4, 1, 0), (5, 18, 0), (5, 30, 0), (4, 4, 0),
+    (5, 19, 0), (1, 4, 1), (1, 4, 3), (1, 5, 1), (3, 6, 4), (5, 24, 0), (5, 17, 0), (5, 21, 0), (5, 20, 0),
+    (2, 10, 3), (4, 5, 0), (5, 22, 0), (4, 3, 0),
 )
 ffn_pieces = (
     (0, 0, 0, 48, 0, 0), (0, 0, 48, 48, 1, 0), (1, 0, 0, 96, 0, 2),
@@ -814,21 +814,21 @@
     (5, 0, 0, 48, 0, 0), (5, 1, 0, 48, 1, 0),
 )
 attention_plan = (
-    (0, 1, 0), (0, 0, 0), (0, 2, 0), (0, 1, 1), (0, 1, 2), (4, 0, 0), (4, 1, 0), (1, 1, 0), (0, 6, 0),
-    (0, 1, 3), (0, 3, 0), (1, 0, 0), (0, 0, 1), (4, 2, 0), (4, 3, 0), (4, 4, 0), (1, 2, 0), (1, 0, 1),
-    (1, 1, 1), (0, 0, 2), (4, 5, 0), (0, 3, 1), (4, 6, 0), (4, 7, 0), (0, 6, 1), (4, 9, 0), (0, 5, 0),
-    (2, 6, 0), (1, 3, 0), (0, 4, 0), (0, 5, 1), (2, 1, 0), (0, 6, 2), (0, 2, 1), (4, 10, 0), (1, 0, 2),
-    (4, 11, 0), (0, 4, 1), (0, 7, 0), (2, 6, 1), (1, 1, 2), (0, 7, 1), (1, 4, 0), (4, 8, 0), (4, 12, 0),
-    (0, 5, 2), (0, 4, 2), (2, 7, 0), (1, 4, 1), (2, 6, 2), (2, 0, 0), (1, 2, 1), (0, 2, 2), (1, 5, 0),
-    (2, 3, 0), (0, 6, 3), (4, 13, 0), (2, 1, 1), (2, 2, 0), (1, 5, 1), (2, 1, 2), (4, 14, 0), (0, 8, 0),
-    (0, 0, 3), (0, 9, 0), (0, 9, 1), (0, 3, 2), (0, 4, 3), (2, 0, 1), (0, 8, 1), (0, 8, 2), (0, 7, 2),
-    (2, 7, 1), (2, 7, 2), (0, 9, 2), (1, 1, 3), (1, 9, 0), (1, 5, 2), (1, 8, 0), (1, 3, 1), (0, 8, 3),
-    (1, 9, 1), (0, 2, 3), (2, 5, 0), (2, 6, 3), (0, 3, 3), (1, 3, 2), (2, 4, 0), (2, 0, 2), (0, 5, 3),
-    (0, 7, 3), (1, 8, 1), (1, 0, 3), (2, 2, 1), (1, 9, 2), (2, 9, 0), (1, 4, 2), (2, 8, 0), (1, 2, 2),
-    (2, 4, 1), (2, 1, 3), (2, 3, 1), (1, 2, 3), (4, 18, 0), (1, 4, 3), (1, 8, 2), (2, 5, 1), (3, 6, 0),
-    (2, 5, 2), (1, 8, 3), (1, 3, 3), (0, 9, 3), (2, 9, 1), (2, 8, 1), (2, 3, 2), (1, 5, 3), (2, 0, 3),
-    (4, 15, 0), (2, 2, 2), (2, 7, 3), (2, 8, 2), (2, 4, 2), (2, 9, 2), (1, 9, 3), (4, 17, 0), (3, 7, 0),
-    (2, 5, 3), (2, 2, 3), (2, 8, 3), (2, 3, 3), (4, 16, 0), (2, 4, 3), (2, 9, 3),
+    (0, 3, 0), (0, 1, 0), (0, 0, 0), (0, 0, 1), (0, 3, 1), (4, 0, 0), (4, 1, 0), (0, 6, 0), (0, 2, 0),
+    (1, 0, 0), (0, 3, 2), (0, 3, 3), (0, 1, 1), (0, 1, 2), (4, 2, 0), (0, 2, 1), (1, 3, 0), (0, 6, 1),
+    (1, 0, 1), (4, 3, 0), (1, 1, 0), (2, 6, 0), (4, 4, 0), (2, 6, 1), (1, 2, 0), (1, 2, 1), (0, 0, 2),
+    (1, 3, 1), (0, 6, 2), (4, 5, 0), (1, 3, 2), (0, 2, 2), (4, 6, 0), (4, 7, 0), (2, 0, 0), (4, 9, 0),
+    (0, 4, 0), (1, 1, 1), (2, 3, 0), (0, 4, 1), (0, 0, 3), (1, 1, 2), (2, 0, 1), (1, 2, 2), (4, 10, 0),
+    (4, 11, 0), (0, 7, 0), (4, 8, 0), (4, 12, 0), (2, 1, 0), (2, 7, 0), (2, 6, 2), (1, 0, 2), (2, 3, 1),
+    (1, 4, 0), (0, 4, 2), (1, 4, 1), (2, 1, 1), (0, 1, 3), (4, 13, 0), (0, 7, 1), (0, 5, 0), (0, 7, 2),
+    (4, 14, 0), (0, 8, 0), (0, 9, 0), (0, 9, 1), (4, 18, 0), (2, 1, 2), (0, 8, 1), (0, 8, 2), (2, 7, 1),
+    (0, 5, 1), (0, 6, 3), (2, 7, 2), (1, 5, 0), (0, 5, 2), (0, 8, 3), (2, 2, 0), (1, 8, 0), (1, 8, 1),
+    (2, 6, 3), (2, 4, 0), (0, 9, 2), (1, 5, 1), (1, 9, 0), (2, 2, 1), (0, 2, 3), (0, 7, 3), (2, 0, 2),
+    (1, 0, 3), (0, 9, 3), (1, 8, 2), (0, 4, 3), (1, 1, 3), (1, 9, 1), (2, 8, 0), (1, 5, 2), (3, 6, 0),
+    (1, 4, 2), (2, 5, 0), (0, 5, 3), (2, 9, 0), (2, 4, 1), (1, 9, 2), (1, 2, 3), (2, 8, 1), (1, 8, 3),
+    (2, 2, 2), (2, 5, 1), (2, 1, 3), (2, 9, 1), (1, 3, 3), (2, 3, 2), (2, 0, 3), (1, 9, 3), (4, 15, 0),
+    (2, 8, 2), (2, 4, 2), (1, 4, 3), (1, 5, 3), (2, 9, 2), (2, 7, 3), (2, 5, 2), (2, 2, 3), (4, 17, 0),
+    (2, 8, 3), (2, 4, 3), (2, 3, 3), (2, 9, 3), (4, 16, 0), (3, 7, 0), (2, 5, 3),
 )
 
 

time: 192 us -> 193 us (level)
  no operation moved by 1% of the time
where the time goes in v3:
time: 193 us; the launch traced here: 190 us
  Pallas kernels  189 us (98%)
    pallas_call x1, Pallas kernels, front(): pl.pallas_call(functools.partial(front_kernel, line_size, heads, scale, p...  84.6 us
    pallas_call x1, Pallas kernels, attention_back(): pl.pallas_call(functools.partial(attention_kernel, line_size, heads, scal...  69.3 us
    pallas_call x1, Pallas kernels, ffn_back(): pl.pallas_call(functools.partial(ffn_kernel, line_size, heads, pieces, pl...  32.2 us

profile of v3, /device:TPU:9, one launch (start us, length us, event | category | flops | bytes accessed | tf_op | source)
XLA Modules:
  0.0 189.7 jit_solution(3884404013111678259)
XLA Ops:
  0.6 84.6 %gather_and_front.1 = (bf16[1,768,1280]{2,1,0:T(8,128)(2,1)}, bf16[1,768,1536]{2,1,0:T(8,128)(2,1)}, bf16[2,384,768]{2,1,0:T(8,128)(2,1)}, bf16[1,1536,768]{2,1,...) custom-call(bf16[2,48,2304]{2,1,0:T(8,128)(2,1)} %refs_0_.1, ...), custom_call_target="tpu_custom_call" | custom-call | tf_op jit(solution)/shard_map/gather_and_front/pallas_call | solution.py:1358
  85.2 32.2 %ffn_back_and_scatter.1 = (bf16[1,368,768]{2,1,0:T(8,128)(2,1)}, bf16[1,48,768]{2,1,0:T(8,128)(2,1)}, f32[2,96,768]{2,1,0:T(8,128)}, bf16[1,768,1536]{2,1,0:T(8,...) custom-call(bf16[1,1536,768]{2,1,0:T(8,128)(2,1)} %get-tuple-element, ...), custom_call_target="tpu_custom_call" | custom-call | tf_op jit(solution)/shard_map/ffn_back_and_scatter/pallas_call | solution.py:1729
  117.4 0.0 copy-start
  117.4 0.0 copy-start.1
  117.4 69.3 %attention_back_and_scatter.1 = (f32[1,368,768]{2,1,0:T(8,128)S(1)}, f32[1,48,768]{2,1,0:T(8,128)S(1)}, f32[2,192,768]{2,1,0:T(8,128)S(1)}, f32[2,48,2304]{2,1,0...) custom-call(bf16[832,1152]{1,0:T(8,128)(2,1)} %get-tuple-element.71., ...), custom_call_target="tpu_custom_call" | custom-call | tf_op jit(solution)/shard_map/attention_back_and_scatter/pallas_call | solution.py:2199
  186.8 0.0 copy-done
  186.8 0.0 copy-done.1
  186.8 2.7 %publish.1 = (f32[1,368,768]{2,1,0:T(8,128)}, f32[1,48,768]{2,1,0:T(8,128)}, f32[2,192,768]{2,1,0:T(8,128)}, f32[2,48,2304]{2,1,0:T(8,128)}, f32[12,2,48]{2,1,0:...) custom-call(f32[1,368,768]{2,1,0:T(8,128)S(1)} %get-tuple-element.10, ...), custom_call_target="tpu_custom_call" | custom-call | tf_op jit(solution)/shard_map/publish/pallas_call | solution.py:2239
Async XLA Ops:
  117.4 69.3 %copy-start = (bf16[1,368,768]{2,1,0:T(8,128)(2,1)S(1)}, bf16[1,368,768]{2,1,0:T(8,128)(2,1)}, u32[]{:S(2)}) copy-start(bf16[1,368,768]{2,1,0:T(8,128)(2,1)} %get-tuple-element.118.refs_9_) | copy-start | bytes 1695748
  117.4 69.3 %copy-start.1 = (bf16[1,48,768]{2,1,0:T(8,128)(2,1)S(1)}, bf16[1,48,768]{2,1,0:T(8,128)(2,1)}, u32[]{:S(2)}) copy-start(bf16[1,48,768]{2,1,0:T(8,128)(2,1)} %get-tuple-element.119.refs_10_) | copy-start | bytes 221188
